TPU v7x, 32 devices: a whole 2x2x4 slice. The times are simulated.
32 devices in a mesh: req: 4 (over y, core), exp: 8 (over z, x).
Axes of the slice: x: 2, y: 2, z: 4, core: 2. Of those that a mesh axis runs over, the one named last changes fastest.
Arguments:
- stream_in: bfloat16 [4096, 2048], P(('req', 'exp')), may hold values from -3 to 3
- queries: bfloat16 [4096, 2048], P('req', 'exp'), may hold values from -9 to 9
- keys: bfloat16 [4096, 2048], P('req', 'exp'), may hold values from -7 to 7
- values: bfloat16 [4096, 2048], P('req', 'exp'), may hold values from -6 to 6
- out_weight: bfloat16 [2048, 2048], P('exp'), may hold values from -0.29882812 to 0.29882812
- norm_gain: float32 [2048], replicated, may hold values from 0.1 to 1.9
- w_gate: bfloat16 [128, 2048, 512], P(('req', 'exp')), may hold values from -0.125 to 0.125
- w_up: bfloat16 [128, 2048, 512], P(('req', 'exp')), may hold values from -0.125 to 0.125
- w_down: bfloat16 [128, 512, 2048], P(('req', 'exp')), may hold values from -0.1875 to 0.1875
- combine: float32 [4096, 8], P(('req', 'exp')), may hold values from 0.05 to 0.6
- segment_ids: int32 [4, 1024], P('req'), may hold values from 0 to 7, never falling along the last dimension, each value on 1 to 512 neighbouring positions
- routes: int32 [4096, 8], P(('req', 'exp')), may hold values from 0 to 63, all different within a row; in each aligned block of 128 rows (0 to 127, 128 to 255, ...) at most 20 rows name the same one
- page_table: int32 [256], replicated, may hold values from 0 to 255, as said below
Outputs:
- layer_out: bfloat16 [4096, 2048], P(('req', 'exp'))
- kv_cache: bfloat16 [256, 2, 16, 2048], P('req', None, None, 'exp')
Inputs may be any that keep to these rules, and one draw needn't show every extreme that they name: `segment_ids`: ids never fall along a row; every request has at most 512 tokens and one has exactly that many. `routes`: the 8 experts of a token differ; among the 128 tokens of one device each expert is named at most 20 times. `page_table`: a permutation of the pages; the 64 logical pages of each row of requests go in equal numbers to the physical pages of every row, row q holding pages q * 64 to (q + 1) * 64 - 1.
All inputs are finite; a program needn't handle non-finite values.
Results may differ from a plain program's by a relative error of at most 0.0062.
Values may be sent and summed in bfloat16 or wider, within the bound.
No kernel may reach another device: no remote copies, remote signals or barrier semaphores. Data moves between devices by JAX's collectives and lax.ppermute only.
A program may use at most 128 MiB of HBM per device.

v0:
```python
import math

import jax
import jax.numpy as jnp
from jax import lax
from jax.sharding import PartitionSpec as P

D = 2048
HD = 128
EXPERTS = 64
TOPK = 8
PAGE = 16
MOST = 20


def from_partner(block, axis, distance):
    count = lax.axis_size(axis)
    route = []
    for low in range(count):
        high = low | 1 << distance
        if high != low and high < count:
            route += [(low, high), (high, low)]
    return lax.ppermute(block, axis, route)


def attend_rows(queries, keys, values, segments):
    length = queries.shape[0]
    head_count = queries.shape[1] // HD
    query_heads = queries.reshape(length, head_count, HD)
    key_heads = keys.reshape(length, head_count, HD)
    value_heads = values.reshape(length, head_count, HD)
    scaling = 1.0 / math.sqrt(HD)
    rows_block = min(512, length)

    def attend_block(position):
        start = position * rows_block
        query_block = lax.dynamic_slice_in_dim(query_heads, start, rows_block, 0)
        segment_block = lax.dynamic_slice_in_dim(segments, start, rows_block, 0)
        scores = (
            jnp.einsum("qhd,khd->hqk", query_block, key_heads, preferred_element_type=jnp.float32)
            * scaling
        )
        allowed = (segment_block[:, None] == segments[None, :])[None, :, :]
        scores = jnp.where(allowed, scores, jnp.float32(-1e30))
        highest = jnp.max(scores, axis=2, keepdims=True)
        weights_exp = jnp.exp(scores - highest)
        totals = jnp.sum(weights_exp, axis=2)
        mixed = jnp.einsum(
            "hqk,khd->qhd",
            weights_exp.astype(jnp.bfloat16),
            value_heads,
            preferred_element_type=jnp.float32,
        )
        mixed = mixed / jnp.transpose(totals)[:, :, None]
        return mixed.astype(jnp.bfloat16)

    blocks = lax.map(attend_block, jnp.arange(length // rows_block))
    return blocks.reshape(length, head_count * HD)


def write_pages(keys, values, page_table):
    page_rows = keys.shape[0] // PAGE
    groups = lax.axis_size("req")
    per_group = page_rows // groups
    width = keys.shape[1]
    pages = jnp.stack(
        [keys.reshape(page_rows, PAGE, width), values.reshape(page_rows, PAGE, width)], axis=1
    )
    myself = lax.axis_index("req")
    whole_table = page_table.reshape(groups, page_rows)
    own_table = lax.dynamic_slice_in_dim(page_table, myself * page_rows, page_rows, 0)
    target = own_table // page_rows
    picked = (target[:, None] == jnp.arange(groups, dtype=jnp.int32)[None, :]).astype(jnp.int32)
    ranking = jnp.sum(jnp.cumsum(picked, axis=0) * picked, axis=1) - 1
    outgoing = jnp.zeros_like(pages).at[target * per_group + ranking].set(pages)
    incoming = lax.all_to_all(
        outgoing.reshape(groups, per_group, 2, PAGE, width),
        "req",
        split_axis=0,
        concat_axis=0,
        tiled=True,
    )
    arriving = whole_table // page_rows == myself
    arrival_rank = jnp.cumsum(arriving.astype(jnp.int32), axis=1) - 1
    placing = jnp.where(
        arriving, jnp.arange(groups, dtype=jnp.int32)[:, None] * per_group + arrival_rank, page_rows
    )
    slot_table = (
        jnp.zeros((page_rows + 1,), jnp.int32)
        .at[placing.reshape(-1)]
        .set((whole_table % page_rows).reshape(-1))
    )
    slot_table = slot_table[:page_rows]
    return jnp.zeros_like(pages).at[slot_table].set(incoming.reshape(page_rows, 2, PAGE, width))


def whole_experts(w_gate, w_up, w_down):
    local_halves = w_gate.shape[0]
    half_units = w_gate.shape[2]
    if local_halves == 1:
        packed = jnp.stack([w_gate[0], w_up[0], w_down[0].reshape(D, half_units)])
        partner = from_partner(packed, "exp", 0)
        leading = lax.axis_index("exp") % 2 == 0
        first = jnp.where(leading, packed, partner)
        second = jnp.where(leading, partner, packed)
        gate_full = jnp.stack([first[0], second[0]])[None]
        up_full = jnp.stack([first[1], second[1]])[None]
        down_full = jnp.stack([first[2].reshape(half_units, D), second[2].reshape(half_units, D)])[
            None
        ]
        return (gate_full, up_full, down_full, 1)
    gate_full = w_gate.reshape(local_halves // 2, 2, D, half_units)
    up_full = w_up.reshape(local_halves // 2, 2, D, half_units)
    down_full = w_down.reshape(local_halves // 2, 2, half_units, D)
    return (gate_full, up_full, down_full, 2)


def on_device(
    stream_in,
    queries,
    keys,
    values,
    out_weight,
    norm_gain,
    w_gate,
    w_up,
    w_down,
    combine,
    segment_ids,
    routes,
    page_table,
):
    attended = attend_rows(queries, keys, values, segment_ids[0])
    kv_cache = write_pages(keys, values, page_table)
    tok_rows = stream_in.shape[0]
    projected = lax.psum_scatter(
        jnp.dot(attended, out_weight, preferred_element_type=jnp.float32),
        "exp",
        scatter_dimension=0,
        tiled=True,
    )
    residual = stream_in.astype(jnp.float32) + projected
    scale_rows = lax.rsqrt(jnp.mean(residual * residual, axis=1, keepdims=True) + 1e-06)
    normed = (residual * scale_rows * norm_gain).astype(jnp.bfloat16)
    expert_ids = routes.reshape(-1)
    owners = (expert_ids[:, None] == jnp.arange(EXPERTS, dtype=jnp.int32)[None, :]).astype(
        jnp.int32
    )
    ranking = jnp.sum(jnp.cumsum(owners, axis=0) * owners, axis=1) - 1
    pair_rows = jnp.repeat(normed, TOPK, axis=0)
    devices = lax.axis_size(("req", "exp"))
    local_halves = w_gate.shape[0]
    slots = (MOST + 1) // 2
    holder = 2 * expert_ids + ranking % 2
    position = ranking // 2
    outgoing = jnp.zeros((devices * local_halves * slots, D), jnp.bfloat16)
    outgoing = outgoing.at[holder * slots + position].set(pair_rows)
    gate_full, up_full, down_full, copies = whole_experts(w_gate, w_up, w_down)
    local_experts = gate_full.shape[0]
    arrived = lax.all_to_all(
        outgoing.reshape(devices, local_halves, slots, D),
        ("req", "exp"),
        split_axis=0,
        concat_axis=0,
        tiled=True,
    )
    count = arrived.shape[2]
    grouped = arrived.reshape(devices, local_experts, copies, count, D)
    gate_val = jnp.einsum(
        "sercd,ejdf->serjcf", grouped, gate_full, preferred_element_type=jnp.float32
    )
    up_val = jnp.einsum("sercd,ejdf->serjcf", grouped, up_full, preferred_element_type=jnp.float32)
    activated = (jax.nn.silu(gate_val) * up_val).astype(jnp.bfloat16)
    halves_out = jnp.einsum(
        "serjcf,ejfd->serjcd", activated, down_full, preferred_element_type=jnp.float32
    ).astype(jnp.bfloat16)
    returned = lax.all_to_all(
        halves_out.reshape(devices, local_halves, 2, count, D),
        ("req", "exp"),
        split_axis=0,
        concat_axis=0,
        tiled=True,
    )
    flat_back = returned.reshape(devices * local_halves, 2, slots, D)
    combined = flat_back[holder, 0, position].astype(jnp.float32) + flat_back[
        holder, 1, position
    ].astype(jnp.float32)
    weighted = combined * combine.reshape(-1)[:, None]
    expert_sum = jnp.sum(weighted.reshape(tok_rows, TOPK, D), axis=1)
    layer_out = (residual + expert_sum).astype(jnp.bfloat16)
    return (layer_out, kv_cache)


def solution(mesh):
    return jax.shard_map(
        on_device,
        mesh=mesh,
        in_specs=(
            P(("req", "exp"), None),
            P("req", "exp"),
            P("req", "exp"),
            P("req", "exp"),
            P("exp", None),
            P(),
            P(("req", "exp"), None, None),
            P(("req", "exp"), None, None),
            P(("req", "exp"), None, None),
            P(("req", "exp"), None),
            P("req", None),
            P(("req", "exp"), None),
            P(),
        ),
        out_specs=(P(("req", "exp"), None), P("req", None, None, "exp")),
        check_vma=False,
    )
```

profile of v0, /device:TPU:0, one launch (start us, length us, event | category | flops | bytes accessed | tf_op | source)
XLA Modules:
  0.0 721.1 jit_solution(17136744825639388825)
XLA Ops:
  11.7 10.9 %while.10 = (s32[]{:T(128)}, bf16[2,512,2,128]{3,2,1,0:T(2,128)(2,1)S(1)}, s32[2]{0:T(128)S(1)}, s32[1024]{0:T(1024)S(1)}, s32[1,1024]{1,0:T(1,128)S(1)}, /*inde...) while((s32[]{:T(128)}, ...), condition=%wide.region_3.4_spmd, body=%wide.region_0.3_spmd.sunk | while | flops 549189632 | bytes 16808124 | solution.py:57
  22.6 4.5 fusion.33
  28.1 18.0 %reduce-window.6 = s32[64,8,128]{2,1,0:T(8,128)S(1)} reduce-window(s32[64,8,128]{2,1,0:T(8,128)S(1)} %fusion.38, s32[]{:T(128)} %constant.120.clone.1), window={size=1x1x128 pad=0_0x0_0x127_0}, to_apply=%region_5.6 | reduce-window | flops 8323072 | bytes 524292 | tf_op jit(solution)/shard_map/reduce-window
  47.0 132.0 %reduce-scatter.2.cloned.1.call-done = f32[128,2048]{1,0:T(8,128)} async-done(((f32[1024,2048]{1,0:T(8,128)}), f32[128,2048]{1,0:T(8,128)}) %reduce-scatter.2.cloned.1.call-update) | async-done | bytes 1048592 | tf_op jit(solution)/shard_map/reduce_scatter | solution.py:136
  182.0 9.8 %scatter_custom_fusion = bf16[1280,2048]{1,0:T(8,128)(2,1)} fusion(s32[1024]{0:T(1024)S(1)} %bitcast.140, bf16[]{:T(256)} %constant.121.clone.1, bf16[128,2048]{1,0:T(8,128)(2,1)S(1)} %multiply_convert_fusion), kind=kCustom, calls=%fused_computation.34 | custom fusion | bytes 5767170 | tf_op jit(solution)/shard_map/scatter | solution.py:157
  191.8 9.5 %reshape.272 = bf16[32,4,10,2048]{3,2,1,0:T(8,128)(2,1)} reshape(bf16[1280,2048]{1,0:T(8,128)(2,1)} %scatter_custom_fusion) | data formatting | bytes 10485760 | tf_op jit(solution)/shard_map/reshape | solution.py:161
  201.4 10.7 %copy.69 = bf16[32,4,10,2048]{3,1,2,0:T(4,128)(2,1)} copy(bf16[32,4,10,2048]{3,2,1,0:T(8,128)(2,1)} %reshape.272) | data formatting | bytes 10485760 | tf_op jit(solution)/shard_map/reshape | solution.py:161
  212.1 3.7 all-to-all-start
  217.6 8.1 %scatter_fusion = bf16[64,2,16,256]{3,2,1,0:T(8,128)(2,1)} fusion(bf16[64,2,16,256]{3,2,1,0:T(8,128)(2,1)} %broadcast.337.clone, s32[64]{0:T(128)S(1)} %compare_select_fusion.7, bf16[64,2,16,256]{3,2,1,0:T(8,128)(2,1)S(1)} %pad_maximum_fusion), kind=kCustom, calls=%fused_computation.4 | custom fusion | bytes 3145984 | tf_op jit(solution)/shard_map/scatter | solution.py:75
  225.7 107.7 %all-to-all-done = bf16[32,4,10,2048]{3,1,2,0:T(4,128)(2,1)} async-done(((bf16[32,4,10,2048]{3,1,2,0:T(4,128)(2,1)}), bf16[32,4,10,2048]{3,1,2,0:T(4,128)(2,1)}, u32[]{:S(2)}, u32[]{:S(2)}) %all-to-all-start) | async-done | bytes 5242912 | tf_op jit(solution)/shard_map/all_to_all | solution.py:160
  333.5 3.7 all-to-all-start.2
  337.2 5.5 copy.70
  342.8 9.6 %fusion.53 = f32[2,32,2,10,2,512]{5,1,4,3,2,0:T(8,128)} fusion(bf16[32,2,2,10,2048,1]{4,0,5,3,2,1:T(8,128)(2,1)S(1)} %bitcast.124, bf16[2,2,2048,512,1,1]{3,2,1,5,4,0:T(8,128)(2,1)} %bitcast.141), kind=kOutput, calls=%fused_computation.103 | convolution fusion | flops 5368709120 | bytes 18874368 | tf_op jit(solution)/shard_map/sercd,ejdf->serjcf/dot_general | solution.py:172
  352.4 9.3 %fusion.24 = bf16[32,2,2,2,10,512]{5,0,3,4,2,1:T(8,128)(2,1)} fusion(f32[2,32,2,10,2,512]{5,1,4,3,2,0:T(8,128)} %fusion.53, bf16[32,2,2,10,2048,1]{4,0,5,3,2,1:T(8,128)(2,1)S(1)} %bitcast.125, bf16[2,2,2048,512,1,1]{3,2,1,5,4,0:T(8,128)(2,1)S(1)} %bitcast.144), kind=kOutput, calls=%fused_computation.28 | convolution fusion | flops 5376573440 | bytes 21495808 | tf_op jit(solution)/shard_map/sercd,ejdf->serjcf/dot_general | solution.py:169
  361.8 10.0 %convert_bitcast_fusion = bf16[32,2,2,2,10,2048]{5,0,4,2,3,1:T(8,128)(2,1)} fusion(bf16[2,2,512,2048,1,1]{3,2,5,4,1,0:T(8,128)(2,1)S(1)} %bitcast.147, bf16[32,2,2,2,10,512]{5,0,3,4,2,1:T(8,128)(2,1)} %fusion.24), kind=kOutput, calls=%fused_computation.24 | convolution fusion | flops 5373952000 | bytes 21495808 | tf_op jit(solution)/shard_map/serjcf,ejfd->serjcd/dot_general | solution.py:174
  371.8 10.0 %copy.72 = bf16[32,2,2,2,10,2048]{5,0,4,3,2,1:T(8,128)(2,1)} copy(bf16[32,2,2,2,10,2048]{5,0,4,2,3,1:T(8,128)(2,1)} %convert_bitcast_fusion) | data formatting | bytes 20971520 | tf_op jit(solution)/shard_map/convert_element_type | solution.py:176
  381.8 14.7 %copy.73 = bf16[32,4,2,10,2048]{4,1,3,2,0:T(4,128)(2,1)} copy(bf16[32,4,2,10,2048]{4,0,3,2,1:T(8,128)(2,1)} %bitcast.122) | data formatting | bytes 20971520 | tf_op jit(solution)/shard_map/reshape | solution.py:178
  396.5 4.0 all-to-all-start.1
  403.6 8.1 %scatter_fusion.1 = bf16[64,2,16,256]{3,2,1,0:T(8,128)(2,1)} fusion(bf16[64,2,16,256]{3,2,1,0:T(8,128)(2,1)} %broadcast.337, s32[64]{0:T(128)S(1)} %compare_select_fusion.8, bf16[64,2,16,256]{3,2,1,0:T(8,128)(2,1)S(1)} %bitcast.126), kind=kCustom, calls=%fused_computation.5 | custom fusion | bytes 3145984 | tf_op jit(solution)/shard_map/scatter | solution.py:94
  411.8 220.8 %all-to-all-done.1 = bf16[32,4,2,10,2048]{4,1,3,2,0:T(4,128)(2,1)} async-done(((bf16[32,4,2,10,2048]{4,1,3,2,0:T(4,128)(2,1)}), bf16[32,4,2,10,2048]{4,1,3,2,0:T(4,128)(2,1)}, u32[]{:S(2)}, u32[]{:S(2)}) %all-to-all-start.1) | async-done | bytes 10485792 | tf_op jit(solution)/shard_map/all_to_all | solution.py:177
  632.5 20.2 %copy.74 = bf16[32,4,2,10,2048]{4,2,3,1,0:T(2,128)(2,1)} copy(bf16[32,4,2,10,2048]{4,1,3,2,0:T(4,128)(2,1)} %all-to-all-done.1) | data formatting | bytes 20971520 | tf_op jit(solution)/shard_map/all_to_all | solution.py:177
  652.7 26.2 %gather_fusion.1 = bf16[1024,2048]{1,0:T(8,128)(2,1)} fusion(bf16[128,2,10,2048]{3,1,2,0:T(2,128)(2,1)} %bitcast.118, s32[1024]{0:T(1024)S(1)} %bitcast.121), kind=kCustom, calls=%fused_computation.1 | custom fusion | bytes 8400896 | tf_op jit(solution)/shard_map/gather | solution.py:185
  678.9 26.2 %gather_fusion = bf16[1024,2048]{1,0:T(8,128)(2,1)} fusion(bf16[128,2,10,2048]{3,1,2,0:T(2,128)(2,1)} %bitcast.119, s32[1024]{0:T(1024)S(1)} %bitcast.120), kind=kCustom, calls=%fused_computation | custom fusion | bytes 8400896 | tf_op jit(solution)/shard_map/gather | solution.py:185
  705.1 7.7 %fusion.23 = f32[128,2048]{1,0:T(8,128)S(1)} fusion(bf16[1024,2048]{1,0:T(8,128)(2,1)} %gather_fusion.1, bf16[1024,2048]{1,0:T(8,128)(2,1)} %gather_fusion, f32[128,8]{1,0:T(8,128)S(1)} %copy.75), kind=kLoop, calls=%fused_computation.26 | loop fusion | flops 10223616 | bytes 9441280 | tf_op jit(solution)/shard_map/reduce_sum | solution.py:189
  (95 shorter events, 24.6 us)
Async XLA Ops:
  7.2 15.4 %copy-start = (bf16[256,2048]{1,0:T(8,128)(2,1)S(1)}, bf16[256,2048]{1,0:T(8,128)(2,1)}, u32[]{:S(2)}) copy-start(bf16[256,2048]{1,0:T(8,128)(2,1)} %param.19) | copy-start | bytes 3145732
  7.2 4.5 copy-start.6
  7.2 171.9 %reduce-scatter.2.cloned.1.call-start = ((), (), s32[]{:S(2)}) async-start(), calls=%async_computation.4 | async-start | bytes 9437184 | tf_op jit(solution)/shard_map/reduce_scatter | solution.py:136
  27.1 0.7 copy-start.7
  27.1 152.0 %copy-start.3 = (bf16[128,2048]{1,0:T(8,128)(2,1)S(1)}, bf16[128,2048]{1,0:T(8,128)(2,1)}, u32[]{:S(2)}) copy-start(bf16[128,2048]{1,0:T(8,128)(2,1)} %param.15) | copy-start | bytes 1572868
  27.1 153.4 %copy-start.8 = (f32[2048]{0:T(1024)S(1)}, f32[2048]{0:T(1024)}, u32[]{:S(2)}) copy-start(f32[2048]{0:T(1024)} %param.20) | copy-start | bytes 24580
  212.1 3.7 copy-start.9
  212.1 4.2 copy-start.4
  212.1 4.2 copy-start.5
  212.1 121.4 %all-to-all-start = ((bf16[32,4,10,2048]{3,1,2,0:T(4,128)(2,1)}), bf16[32,4,10,2048]{3,1,2,0:T(4,128)(2,1)}, u32[]{:S(2)}, u32[]{:S(2)}) async-start(bf16[32,4,10,2048]{3,1,2,0:T(4,128)(2,1)} %copy.69), calls=%async_computation.1 | async-start | bytes 10485760 | tf_op jit(solution)/shard_map/all_to_all | solution.py:160
  333.5 63.0 %all-to-all-start.2 = ((bf16[4,16,2,16,256]{4,3,2,1,0:T(8,128)(2,1)}), bf16[4,16,2,16,256]{4,3,2,1,0:T(8,128)(2,1)S(1)}, u32[]{:S(2)}, u32[]{:S(2)}) async-start(bf16[4,16,2,16,256]{4,3,2,1,0:T(8,128)(2,1)} %bitcast.40), calls=%async_computation.3 | async-start | bytes 2097152 | tf_op jit(solution)/shard_map/all_to_all | solution.py:76
  337.2 15.2 %slice-start = ((s8[8388608]{0:T(1024)(128)(4,1)}), s8[4194304]{0:T(1024)(128)(4,1)S(1)}, s32[]{:S(2)}) async-start(s8[8388608]{0:T(1024)(128)(4,1)} %bitcast.142), calls=%async_computation.5 | async-start | bytes 8388608
  342.8 9.7 %slice-start.1 = ((s8[8388608]{0:T(1024)(128)(4,1)}), s8[4194304]{0:T(1024)(128)(4,1)S(1)}, s32[]{:S(2)}) async-start(s8[8388608]{0:T(1024)(128)(4,1)} %bitcast.142), calls=%async_computation.6 | async-start | bytes 8388608
  342.8 19.0 %slice-start.2 = ((s8[8388608]{0:T(1024)(128)(4,1)}), s8[4194304]{0:T(1024)(128)(4,1)S(1)}, s32[]{:S(2)}) async-start(s8[8388608]{0:T(1024)(128)(4,1)} %bitcast.145), calls=%async_computation.7 | async-start | bytes 8388608
  352.4 9.4 %slice-start.3 = ((s8[8388608]{0:T(1024)(128)(4,1)}), s8[4194304]{0:T(1024)(128)(4,1)S(1)}, s32[]{:S(2)}) async-start(s8[8388608]{0:T(1024)(128)(4,1)} %bitcast.145), calls=%async_computation.8 | async-start | bytes 8388608
  396.5 4.1 copy-start.10
  396.5 236.0 %all-to-all-start.1 = ((bf16[32,4,2,10,2048]{4,1,3,2,0:T(4,128)(2,1)}), bf16[32,4,2,10,2048]{4,1,3,2,0:T(4,128)(2,1)}, u32[]{:S(2)}, u32[]{:S(2)}) async-start(bf16[32,4,2,10,2048]{4,1,3,2,0:T(4,128)(2,1)} %copy.73), calls=%async_computation.2 | async-start | bytes 20971520 | tf_op jit(solution)/shard_map/all_to_all | solution.py:177
  678.9 34.9 %copy-start.1 = (bf16[256,2048]{1,0:T(8,128)(2,1)S(1)}, bf16[256,2048]{1,0:T(8,128)(2,1)}, u32[]{:S(2)}) copy-start(bf16[256,2048]{1,0:T(8,128)(2,1)} %param.19) | copy-start | bytes 3145732
  705.1 7.7 %copy-start.2 = (f32[128,2048]{1,0:T(8,128)S(1)}, f32[128,2048]{1,0:T(8,128)}, u32[]{:S(2)}) copy-start(f32[128,2048]{1,0:T(8,128)} %reduce-scatter.2.cloned.1.call-done) | copy-start | bytes 3145732
Sparse Core Ops, SparseCore 0:
  27.2 151.7 reduce-scatter.1
where the time goes:
time: 734 us; the launch traced here: 721 us
  waiting for transfers between devices  461 us (63%)
  local copies, waits for them, and re-layouts  161 us (22%)
  matrix products  37.9 us (5%)
  other arithmetic  34 us (5%)
  between operations  14.8 us (2%)
  starting transfers between devices  11.5 us (2%)
    all_to_all x1, waiting for transfers between devices, on_device(): lax.all_to_all(halves_out.reshape(devices, local_halves, 2, count, D), ('...  221 us
    reduce_scatter x1, waiting for transfers between devices, on_device(): lax.psum_scatter(jnp.dot(attended, out_weight, preferred_element_type=jnp...  132 us
    all_to_all x1, waiting for transfers between devices, on_device(): lax.all_to_all(outgoing.reshape(devices, local_halves, slots, D), ('req',...  108 us
    gather x1, local copies, waits for them, and re-layouts, on_device(): flat_back[holder, 1, position].astype(jnp.float32)  26.2 us
    gather x1, local copies, waits for them, and re-layouts, on_device(): flat_back[holder, 0, position].astype(jnp.float32)  26.2 us
    reshape x2, local copies, waits for them, and re-layouts, on_device(): outgoing.reshape(devices, local_halves, slots, D)  20.3 us
    all_to_all x1, local copies, waits for them, and re-layouts, on_device(): lax.all_to_all(halves_out.reshape(devices, local_halves, 2, count, D), ('...  20.2 us
    another operation x3, other arithmetic  18.2 us
  transfers between devices with their start and end apart: 4, of which 3 were waited for; matrix products, arithmetic and copies ran while one was open for 14% of the time, Pallas kernels for 0%

commit v1 on v0

--- a/solution.py
+++ b/solution.py
@@ -2,7 +2,11 @@
 
 import jax
 import jax.numpy as jnp
+import numpy as np
 from jax import lax
+from jax.experimental import pallas as pl
+from jax.experimental.pallas import tpu as pltpu
+from jax.sharding import Mesh
 from jax.sharding import PartitionSpec as P
 
 D = 2048
@@ -115,7 +119,7 @@
     return (gate_full, up_full, down_full, 2)
 
 
-def on_device(
+def on_device_split(
     stream_in,
     queries,
     keys,
@@ -191,25 +195,277 @@
     return (layer_out, kv_cache)
 
 
+PLANES = 4
+
+
+def strictly_lower(size):
+    return jnp.asarray(np.tril(np.ones((size, size), np.float32), -1), jnp.bfloat16)
+
+
+def count_before(flags):
+    return jnp.dot(
+        strictly_lower(flags.shape[0]),
+        flags.astype(jnp.bfloat16),
+        preferred_element_type=jnp.float32,
+    )
+
+
+def move_pages(keys, values, page_table):
+    rows = keys.shape[0]
+    width = keys.shape[1]
+    page_rows = rows // PAGE
+    groups = lax.axis_size("req")
+    per_group = page_rows // groups
+    myself = lax.axis_index("req")
+    whole_table = page_table.reshape(groups, page_rows)
+    own_table = lax.dynamic_slice_in_dim(page_table, myself * page_rows, page_rows, 0)
+    target = own_table // page_rows
+    picked = target[:, None] == jnp.arange(groups, dtype=jnp.int32)[None, :]
+    ranking = jnp.sum(jnp.where(picked, count_before(picked), 0.0), axis=1).astype(jnp.int32)
+    slot = target * per_group + ranking
+    within = jnp.arange(PAGE, dtype=jnp.int32)
+    lines = jnp.arange(rows, dtype=jnp.int32)
+    target_line = (slot[:, None] * PAGE + within[None, :]).reshape(-1)
+    spread = (target_line[None, :] == lines[:, None]).astype(jnp.bfloat16)
+    sent = [
+        jnp.dot(spread, block, preferred_element_type=jnp.float32)
+        .astype(jnp.bfloat16)
+        .reshape(groups, rows // groups, width)
+        for block in (keys, values)
+    ]
+    incoming = lax.all_to_all(
+        jnp.stack(sent, axis=1), "req", split_axis=0, concat_axis=0, tiled=True
+    )
+    arriving = whole_table // page_rows == myself
+    arrival = count_before(arriving.T).T.astype(jnp.int32)
+    source = jnp.arange(groups, dtype=jnp.int32)[:, None] * per_group + arrival
+    landing = jnp.where(arriving, whole_table % page_rows, -1).reshape(-1)
+    slots = jnp.arange(page_rows, dtype=jnp.int32)
+    source_page = jnp.sum(
+        jnp.where(landing[None, :] == slots[:, None], source.reshape(-1)[None, :], 0), axis=1
+    )
+    source_line = (source_page[:, None] * PAGE + within[None, :]).reshape(-1)
+    collect = (source_line[:, None] == lines[None, :]).astype(jnp.bfloat16)
+    placed = [
+        jnp.dot(
+            collect, incoming[:, part].reshape(rows, width), preferred_element_type=jnp.float32
+        )
+        .astype(jnp.bfloat16)
+        .reshape(page_rows, PAGE, width)
+        for part in range(2)
+    ]
+    return jnp.stack(placed, axis=1)
+
+
+def project_rows(attended, out_weight):
+    groups = lax.axis_size("req")
+    members = lax.axis_size("z") * lax.axis_size("x")
+    tok_rows = attended.shape[0] // members
+    strip = out_weight.shape[1] // groups
+    start = lax.axis_index("req") * strip
+    piece = lax.dynamic_slice_in_dim(out_weight, start, strip, 1)
+    strips = lax.all_gather(piece, ("req", "z", "x"), axis=0, tiled=True)
+    strips = strips.reshape(groups, members * out_weight.shape[0], strip)
+    shares = lax.all_to_all(
+        attended.reshape(members, tok_rows, attended.shape[1]),
+        ("z", "x"),
+        split_axis=0,
+        concat_axis=0,
+        tiled=True,
+    )
+    whole_rows = jnp.transpose(shares, (1, 0, 2)).reshape(tok_rows, -1)
+    return jnp.concatenate(
+        [
+            jnp.dot(whole_rows, strips[index], preferred_element_type=jnp.float32)
+            for index in range(groups)
+        ],
+        axis=1,
+    )
+
+
+def expert_kernel(rows_ref, order_ref, back_ref, gate_ref, up_ref, down_ref, out_ref, sorted_rows, total, outs):
+    step = pl.program_id(0)
+    count = sorted_rows.shape[0] // 2
+
+    @pl.when(step == 0)
+    def _():
+        sorted_rows[...] = jnp.dot(
+            order_ref[...], rows_ref[...], preferred_element_type=jnp.float32
+        ).astype(jnp.bfloat16)
+
+    first = pl.multiple_of((step // 2) * count, 16)
+    tokens = sorted_rows[pl.ds(first, count), :]
+    gate_val = jnp.dot(tokens, gate_ref[0], preferred_element_type=jnp.float32)
+    up_val = jnp.dot(tokens, up_ref[0], preferred_element_type=jnp.float32)
+    activated = (gate_val / (1.0 + jnp.exp(-gate_val)) * up_val).astype(jnp.bfloat16)
+    half_out = jnp.dot(activated, down_ref[0], preferred_element_type=jnp.float32)
+
+    @pl.when(step % 2 == 0)
+    def _():
+        total[...] = half_out
+
+    @pl.when(step % 2 == 1)
+    def _():
+        outs[pl.ds(first, count), :] = (total[...] + half_out).astype(jnp.bfloat16)
+
+    @pl.when(step == 3)
+    def _():
+        out_ref[...] = jnp.dot(
+            back_ref[...], outs[...], preferred_element_type=jnp.float32
+        ).astype(jnp.bfloat16)
+
+
+def run_experts(rows, sources, w_gate, w_up, w_down):
+    height, depth = rows.shape
+    units = w_gate.shape[2]
+    slots = height // (sources * 2)
+    index = np.arange(height)
+    wanted = (
+        index % (height // 2) // slots * (2 * slots)
+        + index // (height // 2) * slots
+        + index % slots
+    )
+    order = (wanted[:, None] == index[None, :]).astype(np.float32)
+    fixed = lambda i: (0, 0)
+    return pl.pallas_call(
+        expert_kernel,
+        grid=(4,),
+        in_specs=[
+            pl.BlockSpec((height, depth), fixed),
+            pl.BlockSpec((height, height), fixed),
+            pl.BlockSpec((height, height), fixed),
+            pl.BlockSpec((1, depth, units), lambda i: (i, 0, 0)),
+            pl.BlockSpec((1, depth, units), lambda i: (i, 0, 0)),
+            pl.BlockSpec((1, units, depth), lambda i: (i, 0, 0)),
+        ],
+        out_specs=pl.BlockSpec((height, depth), fixed),
+        out_shape=jax.ShapeDtypeStruct((height, depth), jnp.bfloat16),
+        scratch_shapes=[
+            pltpu.VMEM((height, depth), jnp.bfloat16),
+            pltpu.VMEM((height // 2, depth), jnp.float32),
+            pltpu.VMEM((height, depth), jnp.bfloat16),
+        ],
+        compiler_params=pltpu.CompilerParams(vmem_limit_bytes=40 * 1024 * 1024),
+        cost_estimate=pl.CostEstimate(
+            flops=12 * height * depth * units + 4 * height * height * depth,
+            bytes_accessed=12 * depth * units * 2 + 4 * height * depth,
+            transcendentals=2 * height * units,
+        ),
+    )(
+        rows,
+        jnp.asarray(order, jnp.bfloat16),
+        jnp.asarray(order.T, jnp.bfloat16),
+        w_gate,
+        w_up,
+        w_down,
+    )
+
+
+def on_device_whole(
+    stream_in,
+    queries,
+    keys,
+    values,
+    out_weight,
+    norm_gain,
+    w_gate,
+    w_up,
+    w_down,
+    combine,
+    segment_ids,
+    routes,
+    page_table,
+):
+    tok_rows = stream_in.shape[0]
+    groups = lax.axis_size("req")
+    lanes = lax.axis_size("x")
+    sources = groups * lanes
+    plane_experts = 2 * sources
+    height = plane_experts * MOST
+    level = lax.axis_index("z")
+
+    matched = routes[:, :, None] == jnp.arange(EXPERTS, dtype=jnp.int32)[None, None, :]
+    named = jnp.any(matched, axis=1)
+    weight_of = jnp.sum(jnp.where(matched, combine[:, :, None], 0.0), axis=1)
+    place = jnp.arange(EXPERTS, dtype=jnp.int32)
+    in_plane = place // (PLANES * 2 * lanes) * (2 * lanes) + place % (2 * lanes)
+    slot_of = jnp.where(named, count_before(named) + (in_plane * MOST)[None, :], -1.0)
+    tables = jnp.stack([slot_of.T, weight_of.T])
+    tables = tables.reshape(2, groups, PLANES, 2 * lanes, tok_rows)
+    tables = jnp.transpose(tables, (2, 0, 1, 3, 4)).reshape(PLANES, 2, plane_experts, tok_rows)
+    tables = lax.all_to_all(tables, "z", split_axis=0, concat_axis=0, tiled=True)
+
+    attended = attend_rows(queries, keys, values, segment_ids[0])
+    residual = stream_in.astype(jnp.float32) + project_rows(attended, out_weight)
+    scale_rows = lax.rsqrt(jnp.mean(residual * residual, axis=1, keepdims=True) + 1e-06)
+    normed = (residual * scale_rows * norm_gain).astype(jnp.bfloat16)
+    kv_cache = move_pages(keys, values, page_table)
+
+    lines = jnp.arange(height, dtype=jnp.float32)
+    total = residual
+    for turn in range(PLANES):
+        pairs = [(low, low ^ turn) for low in range(PLANES)]
+        table = lax.dynamic_index_in_dim(tables, level ^ turn, 0, keepdims=False)
+        hits = table[0][:, None, :] == lines[None, :, None]
+        picking = jnp.sum(hits.astype(jnp.float32), axis=0).astype(jnp.bfloat16)
+        mixing = jnp.sum(jnp.where(hits, table[1][:, None, :], 0.0), axis=0)
+        mixing_high = mixing.astype(jnp.bfloat16)
+        mixing_low = (mixing - mixing_high.astype(jnp.float32)).astype(jnp.bfloat16)
+        block = normed if turn == 0 else lax.ppermute(normed, "z", pairs)
+        packed = jnp.dot(picking, block, preferred_element_type=jnp.float32).astype(jnp.bfloat16)
+        arrived = lax.all_to_all(
+            packed.reshape(sources, 2 * MOST, D),
+            ("req", "x"),
+            split_axis=0,
+            concat_axis=0,
+            tiled=True,
+        )
+        outs = run_experts(arrived.reshape(height, D), sources, w_gate, w_up, w_down)
+        returned = lax.all_to_all(
+            outs.reshape(sources, 2 * MOST, D),
+            ("req", "x"),
+            split_axis=0,
+            concat_axis=0,
+            tiled=True,
+        ).reshape(height, D)
+        share = sum(
+            lax.dot_general(
+                part, returned, (((0,), (0,)), ((), ())), preferred_element_type=jnp.float32
+            )
+            for part in (mixing_high, mixing_low)
+        )
+        if turn:
+            share = lax.ppermute(share.astype(jnp.bfloat16), "z", pairs).astype(jnp.float32)
+        total = total + share
+    return (total.astype(jnp.bfloat16), kv_cache)
+
+
 def solution(mesh):
+    requests, members = mesh.shape["req"], mesh.shape["exp"]
+    whole = 2 * EXPERTS == 4 * requests * members
+    if whole:
+        grid = mesh.devices.reshape(requests, PLANES, members // PLANES)
+        mesh = Mesh(grid, ("req", "z", "x"))
+    exp = ("z", "x") if whole else "exp"
+    every = ("req", "z", "x") if whole else ("req", "exp")
     return jax.shard_map(
-        on_device,
+        on_device_whole if whole else on_device_split,
         mesh=mesh,
         in_specs=(
-            P(("req", "exp"), None),
-            P("req", "exp"),
-            P("req", "exp"),
-            P("req", "exp"),
-            P("exp", None),
+            P(every, None),
+            P("req", exp),
+            P("req", exp),
+            P("req", exp),
+            P(exp, None),
             P(),
-            P(("req", "exp"), None, None),
-            P(("req", "exp"), None, None),
-            P(("req", "exp"), None, None),
-            P(("req", "exp"), None),
+            P(every, None, None),
+            P(every, None, None),
+            P(every, None, None),
+            P(every, None),
             P("req", None),
-            P(("req", "exp"), None),
+            P(every, None),
             P(),
         ),
-        out_specs=(P(("req", "exp"), None), P("req", None, None, "exp")),
+        out_specs=(P(every, None), P("req", None, None, exp)),
         check_vma=False,
     )

time: 734 us -> 353 us (0.48); the launches traced: 721 us -> 351 us
  waiting for transfers between devices: 461 us -> 140 us
  local copies, waits for them, and re-layouts: 161 us -> 30.2 us
  starting transfers between devices: 11.5 us -> 66.5 us
  Pallas kernels: 0 us -> 46 us
  other arithmetic: 34 us -> 12.9 us
    all_to_all x3 -> x11, waiting for transfers between devices: 329 us -> 31.1 us  [the longest x1 19.9 us: project_rows(): lax.all_to_all(attended.reshape(members, tok_rows, attended.shape[1]), ('...]
    reduce_scatter x1 -> x0, waiting for transfers between devices: 132 us -> none  [on_device(): lax.psum_scatter(jnp.dot(attended, out_weight, preferred_element_type=jnp...]
    ppermute x0 -> x6, waiting for transfers between devices: none -> 69.2 us  [the longest x3 48.5 us: on_device_whole(): block = normed if turn == 0 else lax.ppermute(normed, 'z', pairs)]
    gather x2 -> x0, local copies, waits for them, and re-layouts: 52.4 us -> none  [the longest x1 26.2 us: on_device(): flat_back[holder, 1, position].astype(jnp.float32)]
    pallas_call x0 -> x4, Pallas kernels: none -> 46 us  [run_experts(): pl.pallas_call(expert_kernel, grid=(4,), in_specs=[pl.BlockSpec((height,...]
    all_gather x0 -> x1, waiting for transfers between devices: none -> 40.2 us  [project_rows(): strips = lax.all_gather(piece, ('req', 'z', 'x'), axis=0, tiled=True)]
    all_to_all x3 -> x11, starting transfers between devices: 11.4 us -> 48.6 us  [the longest x4 16.6 us: on_device_whole(): lax.all_to_all(outs.reshape(sources, 2 * MOST, D), ('req', 'x'), split_ax...]
    reshape x4 -> x1, local copies, waits for them, and re-layouts: 35.1 us -> 0.76 us  [move_pages(): whole_table = page_table.reshape(groups, page_rows)]
  transfers between devices with their start and end apart: 4 -> 18, of which waited for: 3 -> 10; matrix products, arithmetic and copies ran while one was open for 14% -> 17% of each run, Pallas kernels for 0% -> 13%
where the time goes in v1:
time: 353 us; the launch traced here: 351 us
  waiting for transfers between devices  140 us (40%)
  starting transfers between devices  66.5 us (19%)
  Pallas kernels  46 us (13%)
  matrix products  39.2 us (11%)
  local copies, waits for them, and re-layouts  30.2 us (9%)
  between operations  14.5 us (4%)
  other arithmetic  12.9 us (4%)
    ppermute x3, waiting for transfers between devices, on_device_whole(): block = normed if turn == 0 else lax.ppermute(normed, 'z', pairs)  48.5 us
    pallas_call x4, Pallas kernels, run_experts(): pl.pallas_call(expert_kernel, grid=(4,), in_specs=[pl.BlockSpec((height,...  46 us
    all_gather x1, waiting for transfers between devices, project_rows(): strips = lax.all_gather(piece, ('req', 'z', 'x'), axis=0, tiled=True)  40.2 us
    ppermute x3, waiting for transfers between devices, on_device_whole(): lax.ppermute(share.astype(jnp.bfloat16), 'z', pairs).astype(jnp.float32)  20.7 us
    all_to_all x1, waiting for transfers between devices, project_rows(): lax.all_to_all(attended.reshape(members, tok_rows, attended.shape[1]), ('...  19.9 us
    unnamed x57, local copies, waits for them, and re-layouts  18.5 us
    all_to_all x4, starting transfers between devices, on_device_whole(): lax.all_to_all(outs.reshape(sources, 2 * MOST, D), ('req', 'x'), split_ax...  16.6 us
    all_to_all x4, starting transfers between devices, on_device_whole(): lax.all_to_all(packed.reshape(sources, 2 * MOST, D), ('req', 'x'), split_...  16.1 us
  transfers between devices with their start and end apart: 18, of which 10 were waited for; matrix products, arithmetic and copies ran while one was open for 17% of the time, Pallas kernels for 13%

profile of v1, /device:TPU:0, one launch (start us, length us, event | category | flops | bytes accessed | tf_op | source)
XLA Modules:
  0.0 351.0 jit_solution(14453837967233608188)
XLA Ops:
  13.0 6.3 %all-to-all-start.1 = ((f32[4,2,16,128]{3,2,1,0:T(8,128)}), f32[4,2,16,128]{3,2,1,0:T(8,128)S(1)}, u32[]{:S(2)}, u32[]{:S(2)}) async-start(f32[4,2,16,128]{3,2,1,0:T(8,128)} %bitcast.16), calls=%async_computation.1 | async-start | bytes 131072 | tf_op jit(solution)/shard_map/all_to_all | solution.py:396
  21.7 12.3 %while.10 = (s32[]{:T(128)}, bf16[2,512,2,128]{3,2,1,0:T(2,128)(2,1)}, s32[2]{0:T(128)S(1)}, s32[1024]{0:T(1024)S(1)}, s32[1,1024]{1,0:T(1,128)S(1)}, /*index=5*...) while((s32[]{:T(128)}, ...), condition=%wide.region_3.4_spmd, body=%wide.region_0.3_spmd.sunk | while | flops 549189632 | bytes 21002492 | solution.py:61
  36.5 6.0 %all-to-all-start = ((bf16[8,128,256]{2,1,0:T(8,128)(2,1)}), bf16[8,128,256]{2,1,0:T(8,128)(2,1)S(1)}, u32[]{:S(2)}, u32[]{:S(2)}) async-start(bf16[8,128,256]{2,1,0:T(8,128)(2,1)} %reshape_reshape.3), calls=%async_computation | async-start | bytes 1048576 | tf_op jit(solution)/shard_map/all_to_all | solution.py:269
  45.7 19.9 %all-to-all-done = bf16[8,128,256]{2,1,0:T(8,128)(2,1)S(1)} async-done(((bf16[8,128,256]{2,1,0:T(8,128)(2,1)}), bf16[8,128,256]{2,1,0:T(8,128)(2,1)S(1)}, u32[]{:S(2)}, u32[]{:S(2)}) %all-to-all-start) | async-done | bytes 524320 | tf_op jit(solution)/shard_map/all_to_all | solution.py:269
  65.6 3.5 %all-to-all-start.10 = ((bf16[4,2,256,256]{3,2,1,0:T(8,128)(2,1)}), bf16[4,2,256,256]{3,2,1,0:T(8,128)(2,1)S(1)}, u32[]{:S(2)}, u32[]{:S(2)}) async-start(bf16[4,2,256,256]{3,2,1,0:T(8,128)(2,1)} %pad_maximum_fusion), calls=%async_computation.10 | async-start | bytes 2097152 | tf_op jit(solution)/shard_map/all_to_all | solution.py:236
  69.4 40.2 %all-gather.2.cloned.1.call-done = bf16[8192,512]{1,0:T(8,128)(2,1)} async-done(((bf16[256,512]{1,0:T(8,128)(2,1)}), bf16[8192,512]{1,0:T(8,128)(2,1)}) %all-gather.2.cloned.1.call-update) | async-done | bytes 8388624 | tf_op jit(solution)/shard_map/all_gather | solution.py:267
  121.1 3.7 %all-to-all-start.2 = ((bf16[8,40,2048]{2,1,0:T(8,128)(2,1)}), bf16[8,40,2048]{2,1,0:T(8,128)(2,1)S(1)}, u32[]{:S(2)}, u32[]{:S(2)}) async-start(bf16[8,40,2048]{2,1,0:T(8,128)(2,1)} %bitcast.19), calls=%async_computation.2 | async-start | bytes 2621440 | tf_op jit(solution)/shard_map/all_to_all | solution.py:416
  128.4 12.5 %collective-permute-done.4 = bf16[128,2048]{1,0:T(8,128)(2,1)S(1)} collective-permute-done((bf16[128,2048]{1,0:T(8,128)(2,1)S(1)}, bf16[128,2048]{1,0:T(8,128)(2,1)S(1)}, u32[]{:S(2)}, u32[]{:S(2)}) %collective-permute-start.4) | collective-permute-done | bytes 524320 | tf_op jit(solution)/shard_map/ppermute | solution.py:414
  142.4 3.8 %all-to-all-start.8 = ((bf16[8,40,2048]{2,1,0:T(8,128)(2,1)}), bf16[8,40,2048]{2,1,0:T(8,128)(2,1)S(1)}, u32[]{:S(2)}, u32[]{:S(2)}) async-start(bf16[8,40,2048]{2,1,0:T(8,128)(2,1)} %bitcast.131), calls=%async_computation.8 | async-start | bytes 2621440 | tf_op jit(solution)/shard_map/all_to_all | solution.py:416
  146.3 11.0 %collective-permute-start.2 = (bf16[128,2048]{1,0:T(8,128)(2,1)}, bf16[128,2048]{1,0:T(8,128)(2,1)S(1)}, u32[]{:S(2)}, u32[]{:S(2)}) collective-permute-start(bf16[128,2048]{1,0:T(8,128)(2,1)} %copy-done.15), channel_id=1, source_target_pairs={{0,4},{2,6},{4,0},{6,2},{1,5},{3,7},{5,1},{7,3},{8,12},{10,14},{12... | collective-permute-start | bytes 1572872 | tf_op jit(solution)/shard_map/ppermute | solution.py:414
  158.4 22.9 %collective-permute-done.2 = bf16[128,2048]{1,0:T(8,128)(2,1)S(1)} collective-permute-done((bf16[128,2048]{1,0:T(8,128)(2,1)}, bf16[128,2048]{1,0:T(8,128)(2,1)S(1)}, u32[]{:S(2)}, u32[]{:S(2)}) %collective-permute-start.2) | collective-permute-done | bytes 524320 | tf_op jit(solution)/shard_map/ppermute | solution.py:414
  182.9 4.3 %all-to-all-start.6 = ((bf16[8,40,2048]{2,1,0:T(8,128)(2,1)}), bf16[8,40,2048]{2,1,0:T(8,128)(2,1)}, u32[]{:S(2)}, u32[]{:S(2)}) async-start(bf16[8,40,2048]{2,1,0:T(8,128)(2,1)} %bitcast.130), calls=%async_computation.6 | async-start | bytes 2621440 | tf_op jit(solution)/shard_map/all_to_all | solution.py:416
  188.4 13.2 %collective-permute-done = bf16[128,2048]{1,0:T(8,128)(2,1)S(1)} collective-permute-done((bf16[128,2048]{1,0:T(8,128)(2,1)}, bf16[128,2048]{1,0:T(8,128)(2,1)S(1)}, u32[]{:S(2)}, u32[]{:S(2)}) %collective-permute-start) | collective-permute-done | bytes 524320 | tf_op jit(solution)/shard_map/ppermute | solution.py:414
  204.9 4.3 %all-to-all-start.4 = ((bf16[8,40,2048]{2,1,0:T(8,128)(2,1)}), bf16[8,40,2048]{2,1,0:T(8,128)(2,1)}, u32[]{:S(2)}, u32[]{:S(2)}) async-start(bf16[8,40,2048]{2,1,0:T(8,128)(2,1)} %bitcast.132), calls=%async_computation.4 | async-start | bytes 2621440 | tf_op jit(solution)/shard_map/all_to_all | solution.py:416
  213.3 10.5 %shard_map.242 = bf16[320,2048]{1,0:T(8,128)(2,1)S(1)} custom-call(bf16[320,2048]{1,0:T(8,128)(2,1)S(1)} %bitcast.119, bf16[320,320]{1,0:T(8,128)(2,1)S(1)} %copy-done.7, bf16[320,320]{1,0:T(8,128)(2,1)S(1)} %copy-done.8, bf16[4,2048,512]{2,1,0:T(8,128)(2,1)S(1)} %copy-done.2, bf16[4,2048,512]{2,1,0:T(8,128)(2,1)} %up_ref.7, bf16[4,512,2048]{2,1,0:T(8,128)(2,1)} %down_ref.7), custom_call_target="tpu_custom_call" | custom-call | flops 4865392640 | bytes 27787264 | tf_op jit(solution)/shard_map/pallas_call | solution.py:330
  226.9 3.6 %all-to-all-start.9 = ((bf16[8,40,2048]{2,1,0:T(8,128)(2,1)}), bf16[8,40,2048]{2,1,0:T(8,128)(2,1)S(1)}, u32[]{:S(2)}, u32[]{:S(2)}) async-start(bf16[8,40,2048]{2,1,0:T(8,128)(2,1)} %bitcast.120), calls=%async_computation.9 | async-start | bytes 2621440 | tf_op jit(solution)/shard_map/all_to_all | solution.py:424
  235.0 11.9 %shard_map.241 = bf16[320,2048]{1,0:T(8,128)(2,1)} custom-call(bf16[320,2048]{1,0:T(8,128)(2,1)} %bitcast.32.rows_ref, bf16[320,320]{1,0:T(8,128)(2,1)S(1)} %copy-done.7, bf16[320,320]{1,0:T(8,128)(2,1)S(1)} %copy-done.8, bf16[4,2048,512]{2,1,0:T(8,128)(2,1)S(1)} %copy-done.3, bf16[4,2048,512]{2,1,0:T(8,128)(2,1)} %up_ref.7, bf16[4,512,2048]{2,1,0:T(8,128)(2,1)} %down_ref.7), custom_call_target="tpu_custom_call" | custom-call | flops 4865392640 | bytes 27787264 | tf_op jit(solution)/shard_map/pallas_call | solution.py:330
  248.2 4.3 %all-to-all-start.7 = ((bf16[8,40,2048]{2,1,0:T(8,128)(2,1)}), bf16[8,40,2048]{2,1,0:T(8,128)(2,1)}, u32[]{:S(2)}, u32[]{:S(2)}) async-start(bf16[8,40,2048]{2,1,0:T(8,128)(2,1)} %bitcast.33), calls=%async_computation.7 | async-start | bytes 2621440 | tf_op jit(solution)/shard_map/all_to_all | solution.py:424
  261.1 12.0 %shard_map.240 = bf16[320,2048]{1,0:T(8,128)(2,1)} custom-call(bf16[320,2048]{1,0:T(8,128)(2,1)} %bitcast.26.rows_ref, bf16[320,320]{1,0:T(8,128)(2,1)S(1)} %copy-done.7, bf16[320,320]{1,0:T(8,128)(2,1)S(1)} %copy-done.8, bf16[4,2048,512]{2,1,0:T(8,128)(2,1)S(1)} %copy-done.4, bf16[4,2048,512]{2,1,0:T(8,128)(2,1)} %up_ref.7, bf16[4,512,2048]{2,1,0:T(8,128)(2,1)} %down_ref.7), custom_call_target="tpu_custom_call" | custom-call | flops 4865392640 | bytes 27787264 | tf_op jit(solution)/shard_map/pallas_call | solution.py:330
  273.0 4.5 %all-to-all-start.5 = ((bf16[8,40,2048]{2,1,0:T(8,128)(2,1)}), bf16[8,40,2048]{2,1,0:T(8,128)(2,1)}, u32[]{:S(2)}, u32[]{:S(2)}) async-start(bf16[8,40,2048]{2,1,0:T(8,128)(2,1)} %bitcast.27), calls=%async_computation.5 | async-start | bytes 2621440 | tf_op jit(solution)/shard_map/all_to_all | solution.py:424
  280.9 11.6 %shard_map.239 = bf16[320,2048]{1,0:T(8,128)(2,1)} custom-call(bf16[320,2048]{1,0:T(8,128)(2,1)S(1)} %bitcast.118, bf16[320,320]{1,0:T(8,128)(2,1)S(1)} %copy-done.7, bf16[320,320]{1,0:T(8,128)(2,1)S(1)} %copy-done.8, bf16[4,2048,512]{2,1,0:T(8,128)(2,1)S(1)} %copy-done.5, bf16[4,2048,512]{2,1,0:T(8,128)(2,1)} %up_ref.7, bf16[4,512,2048]{2,1,0:T(8,128)(2,1)} %down_ref.7), custom_call_target="tpu_custom_call" | custom-call | flops 4865392640 | bytes 27787264 | tf_op jit(solution)/shard_map/pallas_call | solution.py:330
  298.0 4.2 %all-to-all-start.3 = ((bf16[8,40,2048]{2,1,0:T(8,128)(2,1)}), bf16[8,40,2048]{2,1,0:T(8,128)(2,1)S(1)}, u32[]{:S(2)}, u32[]{:S(2)}) async-start(bf16[8,40,2048]{2,1,0:T(8,128)(2,1)} %bitcast.21), calls=%async_computation.3 | async-start | bytes 2621440 | tf_op jit(solution)/shard_map/all_to_all | solution.py:424
  313.8 6.2 %all-to-all-done.3 = bf16[8,40,2048]{2,1,0:T(8,128)(2,1)S(1)} async-done(((bf16[8,40,2048]{2,1,0:T(8,128)(2,1)}), bf16[8,40,2048]{2,1,0:T(8,128)(2,1)S(1)}, u32[]{:S(2)}, u32[]{:S(2)}) %all-to-all-start.3) | async-done | bytes 1310752 | tf_op jit(solution)/shard_map/all_to_all | solution.py:424
  320.4 20.7 %collective-permute-done.3 = bf16[128,2048]{1,0:T(8,128)(2,1)} collective-permute-done((bf16[128,2048]{1,0:T(8,128)(2,1)}, bf16[128,2048]{1,0:T(8,128)(2,1)}, u32[]{:S(2)}, u32[]{:S(2)}) %collective-permute-start.3) | collective-permute-done | bytes 524320 | tf_op jit(solution)/shard_map/ppermute | solution.py:438
  (154 shorter events, 94.3 us)
Async XLA Ops:
  7.2 13.9 %copy-start.19 = (bf16[1024,256]{1,0:T(8,128)(2,1)S(1)}, bf16[1024,256]{1,0:T(8,128)(2,1)}, u32[]{:S(2)}) copy-start(bf16[1024,256]{1,0:T(8,128)(2,1)} %param.29) | copy-start | bytes 1572868
  7.2 102.3 %all-gather.2.cloned.1.call-start = ((), (), s32[]{:S(2)}) async-start(), calls=%async_computation.11 | async-start | bytes 8650752 | tf_op jit(solution)/shard_map/all_gather | solution.py:267
  13.0 23.5 %all-to-all-start.1 = ((f32[4,2,16,128]{3,2,1,0:T(8,128)}), f32[4,2,16,128]{3,2,1,0:T(8,128)S(1)}, u32[]{:S(2)}, u32[]{:S(2)}) async-start(f32[4,2,16,128]{3,2,1,0:T(8,128)} %bitcast.16), calls=%async_computation.1 | async-start | bytes 131072 | tf_op jit(solution)/shard_map/all_to_all | solution.py:396
  36.5 29.1 %all-to-all-start = ((bf16[8,128,256]{2,1,0:T(8,128)(2,1)}), bf16[8,128,256]{2,1,0:T(8,128)(2,1)S(1)}, u32[]{:S(2)}, u32[]{:S(2)}) async-start(bf16[8,128,256]{2,1,0:T(8,128)(2,1)} %reshape_reshape.3), calls=%async_computation | async-start | bytes 1048576 | tf_op jit(solution)/shard_map/all_to_all | solution.py:269
  65.6 54.6 %all-to-all-start.10 = ((bf16[4,2,256,256]{3,2,1,0:T(8,128)(2,1)}), bf16[4,2,256,256]{3,2,1,0:T(8,128)(2,1)S(1)}, u32[]{:S(2)}, u32[]{:S(2)}) async-start(bf16[4,2,256,256]{3,2,1,0:T(8,128)(2,1)} %pad_maximum_fusion), calls=%async_computation.10 | async-start | bytes 2097152 | tf_op jit(solution)/shard_map/all_to_all | solution.py:236
  118.6 23.9 %copy-start.15 = (bf16[128,2048]{1,0:T(8,128)(2,1)}, bf16[128,2048]{1,0:T(8,128)(2,1)S(1)}, u32[]{:S(2)}) copy-start(bf16[128,2048]{1,0:T(8,128)(2,1)S(1)} %multiply_convert_fusion) | copy-start | bytes 1572868
  121.1 21.3 %all-to-all-start.2 = ((bf16[8,40,2048]{2,1,0:T(8,128)(2,1)}), bf16[8,40,2048]{2,1,0:T(8,128)(2,1)S(1)}, u32[]{:S(2)}, u32[]{:S(2)}) async-start(bf16[8,40,2048]{2,1,0:T(8,128)(2,1)} %bitcast.19), calls=%async_computation.2 | async-start | bytes 2621440 | tf_op jit(solution)/shard_map/all_to_all | solution.py:416
  124.9 16.0 %collective-permute-start.4 = (bf16[128,2048]{1,0:T(8,128)(2,1)S(1)}, bf16[128,2048]{1,0:T(8,128)(2,1)S(1)}, u32[]{:S(2)}, u32[]{:S(2)}) collective-permute-start(bf16[128,2048]{1,0:T(8,128)(2,1)S(1)} %multiply_convert_fusion), channel_id=1, source_target_pairs={{0,6},{2,4},{4,2},{6,0},{1,7},{3,5},{5,3},{7,1},{8,14},{10,12},{12... | collective-permute-start | bytes 1572872 | tf_op jit(solution)/shard_map/ppermute | solution.py:414
  142.4 40.4 %all-to-all-start.8 = ((bf16[8,40,2048]{2,1,0:T(8,128)(2,1)}), bf16[8,40,2048]{2,1,0:T(8,128)(2,1)S(1)}, u32[]{:S(2)}, u32[]{:S(2)}) async-start(bf16[8,40,2048]{2,1,0:T(8,128)(2,1)} %bitcast.131), calls=%async_computation.8 | async-start | bytes 2621440 | tf_op jit(solution)/shard_map/all_to_all | solution.py:416
  146.3 35.1 %collective-permute-start.2 = (bf16[128,2048]{1,0:T(8,128)(2,1)}, bf16[128,2048]{1,0:T(8,128)(2,1)S(1)}, u32[]{:S(2)}, u32[]{:S(2)}) collective-permute-start(bf16[128,2048]{1,0:T(8,128)(2,1)} %copy-done.15), channel_id=1, source_target_pairs={{0,4},{2,6},{4,0},{6,2},{1,5},{3,7},{5,1},{7,3},{8,12},{10,14},{12... | collective-permute-start | bytes 1572872 | tf_op jit(solution)/shard_map/ppermute | solution.py:414
  182.9 22.0 %all-to-all-start.6 = ((bf16[8,40,2048]{2,1,0:T(8,128)(2,1)}), bf16[8,40,2048]{2,1,0:T(8,128)(2,1)}, u32[]{:S(2)}, u32[]{:S(2)}) async-start(bf16[8,40,2048]{2,1,0:T(8,128)(2,1)} %bitcast.130), calls=%async_computation.6 | async-start | bytes 2621440 | tf_op jit(solution)/shard_map/all_to_all | solution.py:416
  187.2 22.8 %copy-start.7 = (bf16[320,320]{1,0:T(8,128)(2,1)S(1)}, bf16[320,320]{1,0:T(8,128)(2,1)}, u32[]{:S(2)}) copy-start(bf16[320,320]{1,0:T(8,128)(2,1)} %constant.146.clone.order_ref) | copy-start | bytes 614404
  187.2 22.8 %copy-start.8 = (bf16[320,320]{1,0:T(8,128)(2,1)S(1)}, bf16[320,320]{1,0:T(8,128)(2,1)}, u32[]{:S(2)}) copy-start(bf16[320,320]{1,0:T(8,128)(2,1)} %constant.147.clone.back_ref) | copy-start | bytes 614404
  187.2 14.4 %collective-permute-start = (bf16[128,2048]{1,0:T(8,128)(2,1)}, bf16[128,2048]{1,0:T(8,128)(2,1)S(1)}, u32[]{:S(2)}, u32[]{:S(2)}) collective-permute-start(bf16[128,2048]{1,0:T(8,128)(2,1)} %copy-done.15), channel_id=1, source_target_pairs={{0,2},{2,0},{4,6},{6,4},{1,3},{3,1},{5,7},{7,5},{8,10},{10,8},{12,... | collective-permute-start | bytes 1572872 | tf_op jit(solution)/shard_map/ppermute | solution.py:414
  204.9 22.0 %all-to-all-start.4 = ((bf16[8,40,2048]{2,1,0:T(8,128)(2,1)}), bf16[8,40,2048]{2,1,0:T(8,128)(2,1)}, u32[]{:S(2)}, u32[]{:S(2)}) async-start(bf16[8,40,2048]{2,1,0:T(8,128)(2,1)} %bitcast.132), calls=%async_computation.4 | async-start | bytes 2621440 | tf_op jit(solution)/shard_map/all_to_all | solution.py:416
  226.9 21.2 %all-to-all-start.9 = ((bf16[8,40,2048]{2,1,0:T(8,128)(2,1)}), bf16[8,40,2048]{2,1,0:T(8,128)(2,1)S(1)}, u32[]{:S(2)}, u32[]{:S(2)}) async-start(bf16[8,40,2048]{2,1,0:T(8,128)(2,1)} %bitcast.120), calls=%async_computation.9 | async-start | bytes 2621440 | tf_op jit(solution)/shard_map/all_to_all | solution.py:424
  248.2 24.9 %all-to-all-start.7 = ((bf16[8,40,2048]{2,1,0:T(8,128)(2,1)}), bf16[8,40,2048]{2,1,0:T(8,128)(2,1)}, u32[]{:S(2)}, u32[]{:S(2)}) async-start(bf16[8,40,2048]{2,1,0:T(8,128)(2,1)} %bitcast.33), calls=%async_computation.7 | async-start | bytes 2621440 | tf_op jit(solution)/shard_map/all_to_all | solution.py:424
  273.0 24.9 %all-to-all-start.5 = ((bf16[8,40,2048]{2,1,0:T(8,128)(2,1)}), bf16[8,40,2048]{2,1,0:T(8,128)(2,1)}, u32[]{:S(2)}, u32[]{:S(2)}) async-start(bf16[8,40,2048]{2,1,0:T(8,128)(2,1)} %bitcast.27), calls=%async_computation.5 | async-start | bytes 2621440 | tf_op jit(solution)/shard_map/all_to_all | solution.py:424
  294.3 26.1 %collective-permute-start.5 = (bf16[128,2048]{1,0:T(8,128)(2,1)}, bf16[128,2048]{1,0:T(8,128)(2,1)}, u32[]{:S(2)}, u32[]{:S(2)}) collective-permute-start(bf16[128,2048]{1,0:T(8,128)(2,1)} %fusion.30), channel_id=1, source_target_pairs={{0,6},{2,4},{4,2},{6,0},{1,7},{3,5},{5,3},{7,1},{8,14},{10,12},{12... | collective-permute-start | bytes 1572872 | tf_op jit(solution)/shard_map/ppermute | solution.py:438
  298.0 22.0 %all-to-all-start.3 = ((bf16[8,40,2048]{2,1,0:T(8,128)(2,1)}), bf16[8,40,2048]{2,1,0:T(8,128)(2,1)S(1)}, u32[]{:S(2)}, u32[]{:S(2)}) async-start(bf16[8,40,2048]{2,1,0:T(8,128)(2,1)} %bitcast.21), calls=%async_computation.3 | async-start | bytes 2621440 | tf_op jit(solution)/shard_map/all_to_all | solution.py:424
  304.8 36.3 %collective-permute-start.3 = (bf16[128,2048]{1,0:T(8,128)(2,1)}, bf16[128,2048]{1,0:T(8,128)(2,1)}, u32[]{:S(2)}, u32[]{:S(2)}) collective-permute-start(bf16[128,2048]{1,0:T(8,128)(2,1)} %fusion.29), channel_id=1, source_target_pairs={{0,4},{2,6},{4,0},{6,2},{1,5},{3,7},{5,1},{7,3},{8,12},{10,14},{12... | collective-permute-start | bytes 1572872 | tf_op jit(solution)/shard_map/ppermute | solution.py:438
  309.3 31.8 %collective-permute-start.1 = (bf16[128,2048]{1,0:T(8,128)(2,1)}, bf16[128,2048]{1,0:T(8,128)(2,1)}, u32[]{:S(2)}, u32[]{:S(2)}) collective-permute-start(bf16[128,2048]{1,0:T(8,128)(2,1)} %fusion.28), channel_id=1, source_target_pairs={{0,2},{2,0},{4,6},{6,4},{1,3},{3,1},{5,7},{7,5},{8,10},{10,8},{12,... | collective-permute-start | bytes 1572872 | tf_op jit(solution)/shard_map/ppermute | solution.py:438
  312.7 28.4 %copy-start.10 = (bf16[128,2048]{1,0:T(8,128)(2,1)S(1)}, bf16[128,2048]{1,0:T(8,128)(2,1)}, u32[]{:S(2)}) copy-start(bf16[128,2048]{1,0:T(8,128)(2,1)} %param.26) | copy-start | bytes 1572868
  319.9 24.3 %copy-start.1 = (bf16[256,2048]{1,0:T(8,128)(2,1)S(1)}, bf16[256,2048]{1,0:T(8,128)(2,1)}, u32[]{:S(2)}) copy-start(bf16[256,2048]{1,0:T(8,128)(2,1)} %param.30) | copy-start | bytes 3145732
  (25 other events, 96.6 us)
Sparse Core Ops, SparseCore 0:
  11.0 98.4 all-gather.1

commit v2 on v1

--- a/solution.py
+++ b/solution.py
@@ -1,3 +1,4 @@
+import functools
 import math
 
 import jax
@@ -257,41 +258,161 @@
     return jnp.stack(placed, axis=1)
 
 
-def project_rows(attended, out_weight):
+def gather_strips(out_weight):
     groups = lax.axis_size("req")
-    members = lax.axis_size("z") * lax.axis_size("x")
-    tok_rows = attended.shape[0] // members
     strip = out_weight.shape[1] // groups
     start = lax.axis_index("req") * strip
     piece = lax.dynamic_slice_in_dim(out_weight, start, strip, 1)
     strips = lax.all_gather(piece, ("req", "z", "x"), axis=0, tiled=True)
-    strips = strips.reshape(groups, members * out_weight.shape[0], strip)
-    shares = lax.all_to_all(
-        attended.reshape(members, tok_rows, attended.shape[1]),
+    return strips.reshape(groups, -1, strip)
+
+
+def share_attended(attended, tok_rows):
+    lanes = lax.axis_size("x")
+    width = attended.shape[1]
+    columns = jnp.transpose(attended.reshape(PLANES, lanes, tok_rows, width), (1, 0, 2, 3))
+    sent = jnp.broadcast_to(columns[None], (PLANES,) + columns.shape)
+    return lax.all_to_all(
+        sent.reshape(PLANES * lanes, PLANES * tok_rows, width),
         ("z", "x"),
         split_axis=0,
         concat_axis=0,
         tiled=True,
     )
-    whole_rows = jnp.transpose(shares, (1, 0, 2)).reshape(tok_rows, -1)
-    return jnp.concatenate(
-        [
-            jnp.dot(whole_rows, strips[index], preferred_element_type=jnp.float32)
-            for index in range(groups)
-        ],
-        axis=1,
-    )
-
-
-def expert_kernel(rows_ref, order_ref, back_ref, gate_ref, up_ref, down_ref, out_ref, sorted_rows, total, outs):
+
+
+def pack_rows(picking, block, shape):
+    rows = jnp.dot(picking, block, preferred_element_type=jnp.float32)
+    return rows.reshape(shape).astype(jnp.bfloat16)
+
+
+def project_kernel(turns_ref, shares_ref, strip_ref, s0_ref, s1_ref, s2_ref, s3_ref, gain_ref, picking_ref,
+                   normed_ref, residual_ref, packed_ref, rows, whole, squares):
     step = pl.program_id(0)
-    count = sorted_rows.shape[0] // 2
+    steps = pl.num_programs(0)
+    tok_rows = s0_ref.shape[0]
+    members, _, width = shares_ref.shape
+    strip = strip_ref.shape[2]
+    depth = normed_ref.shape[2]
 
     @pl.when(step == 0)
     def _():
+        squares[...] = jnp.zeros_like(squares)
+        for turn in range(PLANES):
+            first = pl.multiple_of(turns_ref[turn] * tok_rows, tok_rows)
+            for member in range(members):
+                rows[turn * tok_rows:(turn + 1) * tok_rows, member * width:(member + 1) * width] = (
+                    shares_ref[member, pl.ds(first, tok_rows), :]
+                )
+
+    for turn, stream_ref in enumerate((s0_ref, s1_ref, s2_ref, s3_ref)):
+        span = slice(turn * tok_rows, (turn + 1) * tok_rows)
+        part = jnp.dot(rows[span, :], strip_ref[0], preferred_element_type=jnp.float32)
+        part = part + stream_ref[...].astype(jnp.float32)
+        whole[step, span, :] = part
+        squares[span, :] += jnp.sum(part * part, axis=1, keepdims=True)
+
+    @pl.when(step == steps - 1)
+    def _():
+        scale = lax.rsqrt(squares[...] * (1.0 / depth) + 1e-06)
+        for index in range(depth // strip):
+            span = slice(index * strip, (index + 1) * strip)
+            residual_ref[:, span] = whole[index, :tok_rows, :]
+            scaled = whole[index] * scale * gain_ref[:, span]
+            normed_ref[:, :, span] = scaled.astype(jnp.bfloat16).reshape(PLANES, tok_rows, strip)
+        packed_ref[:, 0] = pack_rows(
+            picking_ref[...], normed_ref[PLANES - 1], (packed_ref.shape[0],) + packed_ref.shape[2:]
+        )
+
+
+def project_tokens(turns, shares, strips, streams, norm_gain, picking, sources):
+    members, rows, width = shares.shape
+    steps, depth, strip = strips.shape
+    tok_rows = rows // PLANES
+    height = picking.shape[0]
+    return pl.pallas_call(
+        project_kernel,
+        grid_spec=pltpu.PrefetchScalarGridSpec(
+            num_scalar_prefetch=1,
+            grid=(steps,),
+            in_specs=[
+                pl.BlockSpec((members, rows, width), lambda i, t: (0, 0, 0)),
+                pl.BlockSpec((1, depth, strip), lambda i, t: (i, 0, 0)),
+            ]
+            + [pl.BlockSpec((tok_rows, strip), lambda i, t: (0, i))] * PLANES
+            + [
+                pl.BlockSpec((1, D), lambda i, t: (0, 0)),
+                pl.BlockSpec((height, tok_rows), lambda i, t: (0, 0)),
+            ],
+            out_specs=[
+                pl.BlockSpec((PLANES, tok_rows, D), lambda i, t: (0, 0, 0)),
+                pl.BlockSpec((tok_rows, D), lambda i, t: (0, 0)),
+                pl.BlockSpec((sources, 1, height // sources, D), lambda i, t: (0, 0, 0, 0)),
+            ],
+            scratch_shapes=[
+                pltpu.VMEM((rows, depth), jnp.bfloat16),
+                pltpu.VMEM((steps, rows, strip), jnp.float32),
+                pltpu.VMEM((rows, 1), jnp.float32),
+            ],
+        ),
+        out_shape=[
+            jax.ShapeDtypeStruct((PLANES, tok_rows, D), jnp.bfloat16),
+            jax.ShapeDtypeStruct((tok_rows, D), jnp.float32),
+            jax.ShapeDtypeStruct((sources, 1, height // sources, D), jnp.bfloat16),
+        ],
+        compiler_params=pltpu.CompilerParams(vmem_limit_bytes=56 * 1024 * 1024),
+        cost_estimate=pl.CostEstimate(
+            flops=2 * rows * depth * D + 2 * height * tok_rows * D,
+            bytes_accessed=2 * depth * D + 12 * rows * D,
+            transcendentals=rows,
+        ),
+    )(turns, shares, strips, *streams, norm_gain.reshape(1, D), picking)
+
+
+def pack_kernel(after_ref, picking_ref, block_ref, out_ref):
+    out_ref[:, 0] = pack_rows(
+        picking_ref[...], block_ref[0], (out_ref.shape[0],) + out_ref.shape[2:]
+    )
+
+
+def pack_after(after, picking, normed, turn, sources):
+    height, tok_rows = picking.shape
+    return pl.pallas_call(
+        pack_kernel,
+        grid=(1,),
+        in_specs=[
+            pl.BlockSpec(memory_space=pl.ANY),
+            pl.BlockSpec((height, tok_rows), lambda i: (0, 0)),
+            pl.BlockSpec((1, tok_rows, D), lambda i: (turn, 0, 0)),
+        ],
+        out_specs=pl.BlockSpec((sources, 1, height // sources, D), lambda i: (0, 0, 0, 0)),
+        out_shape=jax.ShapeDtypeStruct((sources, 1, height // sources, D), jnp.bfloat16),
+        cost_estimate=pl.CostEstimate(
+            flops=2 * height * tok_rows * D, bytes_accessed=4 * height * D, transcendentals=0
+        ),
+    )(after, picking, normed)
+
+
+def expert_kernel(packs, *refs):
+    (rows_ref, order_ref, back_ref, gate_ref, up_ref, down_ref, picking_ref, block_ref) = refs[-12:-4]
+    out_ref, sorted_rows, total, outs = refs[-4:]
+    step = pl.program_id(0)
+    height, depth = sorted_rows.shape
+    count = height // 2
+    shape = (out_ref.shape[0],) + out_ref.shape[2:]
+
+    @pl.when(step == 0)
+    def _():
+        rows = rows_ref[:, 0].astype(jnp.float32).reshape(height, depth).astype(jnp.bfloat16)
         sorted_rows[...] = jnp.dot(
-            order_ref[...], rows_ref[...], preferred_element_type=jnp.float32
+            order_ref[...], rows, preferred_element_type=jnp.float32
         ).astype(jnp.bfloat16)
+
+    if packs:
+
+        @pl.when(step == 1)
+        def _():
+            out_ref[:, 1] = pack_rows(picking_ref[...], block_ref[0], shape)
 
     first = pl.multiple_of((step // 2) * count, 16)
     tokens = sorted_rows[pl.ds(first, count), :]
@@ -310,54 +431,62 @@
 
     @pl.when(step == 3)
     def _():
-        out_ref[...] = jnp.dot(
-            back_ref[...], outs[...], preferred_element_type=jnp.float32
-        ).astype(jnp.bfloat16)
-
-
-def run_experts(rows, sources, w_gate, w_up, w_down):
-    height, depth = rows.shape
+        out_ref[:, 0] = pack_rows(back_ref[...], outs[...], shape)
+
+
+def run_experts(after, arrived, w_gate, w_up, w_down, picking, normed, turn):
+    sources, parts, slots, depth = arrived.shape
     units = w_gate.shape[2]
-    slots = height // (sources * 2)
+    height = sources * slots
+    tok_rows = picking.shape[1]
+    packs = turn is not None
     index = np.arange(height)
     wanted = (
-        index % (height // 2) // slots * (2 * slots)
-        + index // (height // 2) * slots
-        + index % slots
+        index % (height // 2) // (slots // 2) * slots
+        + index // (height // 2) * (slots // 2)
+        + index % (slots // 2)
     )
     order = (wanted[:, None] == index[None, :]).astype(np.float32)
     fixed = lambda i: (0, 0)
+    out_parts = 2 if packs else 1
+    taken = turn if packs else 0
     return pl.pallas_call(
-        expert_kernel,
+        functools.partial(expert_kernel, packs),
         grid=(4,),
-        in_specs=[
-            pl.BlockSpec((height, depth), fixed),
+        in_specs=[pl.BlockSpec(memory_space=pl.ANY)] * len(after)
+        + [
+            pl.BlockSpec((sources, 1, slots, depth), lambda i: (0, parts - 1, 0, 0)),
             pl.BlockSpec((height, height), fixed),
             pl.BlockSpec((height, height), fixed),
             pl.BlockSpec((1, depth, units), lambda i: (i, 0, 0)),
             pl.BlockSpec((1, depth, units), lambda i: (i, 0, 0)),
             pl.BlockSpec((1, units, depth), lambda i: (i, 0, 0)),
+            pl.BlockSpec((height, tok_rows), fixed),
+            pl.BlockSpec((1, tok_rows, depth), lambda i: (taken, 0, 0)),
         ],
-        out_specs=pl.BlockSpec((height, depth), fixed),
-        out_shape=jax.ShapeDtypeStruct((height, depth), jnp.bfloat16),
+        out_specs=pl.BlockSpec((sources, out_parts, slots, depth), lambda i: (0, 0, 0, 0)),
+        out_shape=jax.ShapeDtypeStruct((sources, out_parts, slots, depth), jnp.bfloat16),
         scratch_shapes=[
             pltpu.VMEM((height, depth), jnp.bfloat16),
             pltpu.VMEM((height // 2, depth), jnp.float32),
             pltpu.VMEM((height, depth), jnp.bfloat16),
         ],
-        compiler_params=pltpu.CompilerParams(vmem_limit_bytes=40 * 1024 * 1024),
+        compiler_params=pltpu.CompilerParams(vmem_limit_bytes=56 * 1024 * 1024),
         cost_estimate=pl.CostEstimate(
             flops=12 * height * depth * units + 4 * height * height * depth,
             bytes_accessed=12 * depth * units * 2 + 4 * height * depth,
             transcendentals=2 * height * units,
         ),
     )(
-        rows,
+        *after,
+        arrived,
         jnp.asarray(order, jnp.bfloat16),
         jnp.asarray(order.T, jnp.bfloat16),
         w_gate,
         w_up,
         w_down,
+        picking,
+        normed,
     )
 
 
@@ -383,6 +512,10 @@
     plane_experts = 2 * sources
     height = plane_experts * MOST
     level = lax.axis_index("z")
+    pairs = [[(low, low ^ turn) for low in range(PLANES)] for turn in range(PLANES)]
+
+    strips = gather_strips(out_weight)
+    streams = [stream_in] + [lax.ppermute(stream_in, "z", pairs[turn]) for turn in range(1, PLANES)]
 
     matched = routes[:, :, None] == jnp.arange(EXPERTS, dtype=jnp.int32)[None, None, :]
     named = jnp.any(matched, axis=1)
@@ -394,49 +527,63 @@
     tables = tables.reshape(2, groups, PLANES, 2 * lanes, tok_rows)
     tables = jnp.transpose(tables, (2, 0, 1, 3, 4)).reshape(PLANES, 2, plane_experts, tok_rows)
     tables = lax.all_to_all(tables, "z", split_axis=0, concat_axis=0, tiled=True)
-
-    attended = attend_rows(queries, keys, values, segment_ids[0])
-    residual = stream_in.astype(jnp.float32) + project_rows(attended, out_weight)
-    scale_rows = lax.rsqrt(jnp.mean(residual * residual, axis=1, keepdims=True) + 1e-06)
-    normed = (residual * scale_rows * norm_gain).astype(jnp.bfloat16)
-    kv_cache = move_pages(keys, values, page_table)
-
     lines = jnp.arange(height, dtype=jnp.float32)
-    total = residual
+    pickings, mixings = [], []
     for turn in range(PLANES):
-        pairs = [(low, low ^ turn) for low in range(PLANES)]
         table = lax.dynamic_index_in_dim(tables, level ^ turn, 0, keepdims=False)
         hits = table[0][:, None, :] == lines[None, :, None]
-        picking = jnp.sum(hits.astype(jnp.float32), axis=0).astype(jnp.bfloat16)
+        pickings.append(jnp.sum(hits.astype(jnp.float32), axis=0).astype(jnp.bfloat16))
         mixing = jnp.sum(jnp.where(hits, table[1][:, None, :], 0.0), axis=0)
-        mixing_high = mixing.astype(jnp.bfloat16)
-        mixing_low = (mixing - mixing_high.astype(jnp.float32)).astype(jnp.bfloat16)
-        block = normed if turn == 0 else lax.ppermute(normed, "z", pairs)
-        packed = jnp.dot(picking, block, preferred_element_type=jnp.float32).astype(jnp.bfloat16)
-        arrived = lax.all_to_all(
-            packed.reshape(sources, 2 * MOST, D),
-            ("req", "x"),
-            split_axis=0,
-            concat_axis=0,
-            tiled=True,
+        high = mixing.astype(jnp.bfloat16)
+        mixings.append((high, (mixing - high.astype(jnp.float32)).astype(jnp.bfloat16)))
+
+    attended = attend_rows(queries, keys, values, segment_ids[0])
+    shares = share_attended(attended, tok_rows)
+    kv_cache = move_pages(keys, values, page_table)
+    turns = level ^ jnp.arange(PLANES, dtype=jnp.int32)
+    normed, residual, packed = project_tokens(
+        turns, shares, strips, streams, norm_gain, pickings[3], sources
+    )
+
+    def exchange(block):
+        return lax.all_to_all(block, ("req", "x"), split_axis=0, concat_axis=0, tiled=True)
+
+    def experts(after, arrived, turn):
+        picking = pickings[0 if turn is None else turn]
+        return run_experts(after, arrived, w_gate, w_up, w_down, picking, normed, turn)
+
+    def mixed(turn, returned):
+        return sum(
+            lax.dot_general(
+                part,
+                returned.reshape(height, D),
+                (((0,), (0,)), ((), ())),
+                preferred_element_type=jnp.float32,
+            )
+            for part in mixings[turn]
         )
-        outs = run_experts(arrived.reshape(height, D), sources, w_gate, w_up, w_down)
-        returned = lax.all_to_all(
-            outs.reshape(sources, 2 * MOST, D),
-            ("req", "x"),
-            split_axis=0,
-            concat_axis=0,
-            tiled=True,
-        ).reshape(height, D)
-        share = sum(
-            lax.dot_general(
-                part, returned, (((0,), (0,)), ((), ())), preferred_element_type=jnp.float32
-            )
-            for part in (mixing_high, mixing_low)
-        )
-        if turn:
-            share = lax.ppermute(share.astype(jnp.bfloat16), "z", pairs).astype(jnp.float32)
-        total = total + share
+
+    def to_plane(turn, share):
+        return lax.ppermute(share, "z", pairs[turn])
+
+    third = exchange(packed)
+    packed_second = pack_after(third, pickings[2], normed, 2, sources)
+    second = exchange(packed_second)
+    outs_third = experts([packed_second], third, 1)
+    first = exchange(outs_third)
+    outs_second = experts([outs_third], second, 0)
+    own = exchange(outs_second)
+    share_third = mixed(3, first[:, 0]).astype(jnp.bfloat16)
+    outs_first = experts([outs_second, share_third], first, None)
+    back_first = exchange(outs_first)
+    got_third = to_plane(3, share_third)
+    share_second = mixed(2, own[:, 0]).astype(jnp.bfloat16)
+    outs_own = experts([outs_first, share_second, got_third], own, None)
+    back_own = exchange(outs_own)
+    share_first = mixed(1, back_first[:, 0]).astype(jnp.bfloat16)
+    total = residual + got_third.astype(jnp.float32) + to_plane(2, share_second).astype(jnp.float32)
+    total = total + to_plane(1, share_first).astype(jnp.float32)
+    total = total + mixed(0, back_own[:, 0])
     return (total.astype(jnp.bfloat16), kv_cache)
 
 

time: 353 us -> 392 us (1.11)
  waiting for transfers between devices: 140 us -> 197 us
  Pallas kernels: 46 us -> 72.6 us
  matrix products: 39.2 us -> 19.2 us
  local copies, waits for them, and re-layouts: 30.2 us -> 16.2 us
  starting transfers between devices: 66.5 us -> 57.8 us
    ppermute x6, waiting for transfers between devices: 69.2 us -> 139 us  [the longest x3 110 us: on_device_whole(): lax.ppermute(stream_in, 'z', pairs[turn])]
    all_gather x1, waiting for transfers between devices: 40.2 us -> 0.02 us  [gather_strips(): strips = lax.all_gather(piece, ('req', 'z', 'x'), axis=0, tiled=True)]
    pallas_call x4 -> x6, Pallas kernels: 46 us -> 72.6 us  [the longest x4 57.7 us: run_experts(): pl.pallas_call(functools.partial(expert_kernel, packs), grid=(4,), in_spe...]
    dot_general x16 -> x8, matrix products: 28.8 us -> 10.3 us  [mixed(): lax.dot_general(part, returned.reshape(height, D), (((0,), (0,)), ((), ()...]
    all_to_all x9 -> x7, waiting for transfers between devices: 31.1 us -> 47.2 us  [the longest x6 47.2 us: exchange(): lax.all_to_all(block, ('req', 'x'), split_axis=0, concat_axis=0, tiled=True)]
    unnamed x57 -> x49, local copies, waits for them, and re-layouts: 18.5 us -> 6.05 us
    all_to_all x1, waiting for transfers between devices: 0.01 us -> 10.4 us  [move_pages(): lax.all_to_all(jnp.stack(sent, axis=1), 'req', split_axis=0, concat_axis=...]
    all_to_all x9 -> x7, starting transfers between devices: 38.7 us -> 30.5 us  [the longest x6 24.3 us: exchange(): lax.all_to_all(block, ('req', 'x'), split_axis=0, concat_axis=0, tiled=True)]
  transfers between devices with their start and end apart: 18 -> 16, of which waited for: 10 -> 11; matrix products, arithmetic and copies ran while one was open for 17% -> 10% of each run, Pallas kernels for 13% -> 15%
where the time goes in v2:
time: 392 us; the launch traced here: 391 us
  waiting for transfers between devices  197 us (50%)
  Pallas kernels  72.6 us (19%)
  starting transfers between devices  57.8 us (15%)
  matrix products  19.2 us (5%)
  local copies, waits for them, and re-layouts  16.2 us (4%)
  between operations  14.4 us (4%)
  other arithmetic  13.2 us (3%)
    ppermute x3, waiting for transfers between devices, on_device_whole(): lax.ppermute(stream_in, 'z', pairs[turn])  110 us
    pallas_call x4, Pallas kernels, run_experts(): pl.pallas_call(functools.partial(expert_kernel, packs), grid=(4,), in_spe...  57.7 us
    all_to_all x6, waiting for transfers between devices, exchange(): lax.all_to_all(block, ('req', 'x'), split_axis=0, concat_axis=0, tiled=True)  47.2 us
    ppermute x3, waiting for transfers between devices, to_plane(): return lax.ppermute(share, 'z', pairs[turn])  29 us
    all_to_all x6, starting transfers between devices, exchange(): lax.all_to_all(block, ('req', 'x'), split_axis=0, concat_axis=0, tiled=True)  24.3 us
    ppermute x3, starting transfers between devices, to_plane(): return lax.ppermute(share, 'z', pairs[turn])  12.8 us
    pallas_call x1, Pallas kernels, project_tokens(): pl.pallas_call(project_kernel, grid_spec=pltpu.PrefetchScalarGridSpec(num...  12.3 us
    all_to_all x1, waiting for transfers between devices, move_pages(): lax.all_to_all(jnp.stack(sent, axis=1), 'req', split_axis=0, concat_axis=...  10.4 us
  transfers between devices with their start and end apart: 16, of which 11 were waited for; matrix products, arithmetic and copies ran while one was open for 10% of the time, Pallas kernels for 15%

profile of v2, /device:TPU:0, one launch (start us, length us, event | category | flops | bytes accessed | tf_op | source)
XLA Modules:
  0.0 391.1 jit_solution(13199222411155682853)
XLA Ops:
  13.0 6.3 %all-to-all-start.1 = ((f32[4,2,16,128]{3,2,1,0:T(8,128)}), f32[4,2,16,128]{3,2,1,0:T(8,128)S(1)}, u32[]{:S(2)}, u32[]{:S(2)}) async-start(f32[4,2,16,128]{3,2,1,0:T(8,128)} %bitcast.18), calls=%async_computation.1 | async-start | bytes 131072 | tf_op jit(solution)/shard_map/all_to_all | solution.py:529
  21.6 10.7 %while.10 = (s32[]{:T(128)}, bf16[2,512,2,128]{3,2,1,0:T(2,128)(2,1)S(1)}, s32[2]{0:T(128)S(1)}, s32[1024]{0:T(1024)S(1)}, s32[1,1024]{1,0:T(1,128)S(1)}, /*inde...) while((s32[]{:T(128)}, ...), condition=%wide.region_3.4_spmd, body=%wide.region_0.3_spmd.sunk | while | flops 549189632 | bytes 16808124 | solution.py:62
  34.4 6.2 %all-to-all-start = ((bf16[8,512,256]{2,1,0:T(8,128)(2,1)}), bf16[8,512,256]{2,1,0:T(8,128)(2,1)S(1)}, u32[]{:S(2)}, u32[]{:S(2)}) async-start(bf16[8,512,256]{2,1,0:T(8,128)(2,1)} %bitcast.10), calls=%async_computation | async-start | bytes 4194304 | tf_op jit(solution)/shard_map/all_to_all | solution.py:275
  46.7 61.7 %collective-permute-done.s1_ref = bf16[128,2048]{1,0:T(8,128)(2,1)S(1)} collective-permute-done((bf16[128,2048]{1,0:T(8,128)(2,1)S(1)}, bf16[128,2048]{1,0:T(8,128)(2,1)S(1)}, u32[]{:S(2)}, u32[]{:S(2)}) %collective-permute-start) | collective-permute-done | bytes 524320 | tf_op jit(solution)/shard_map/ppermute | solution.py:518
  108.4 48.1 %collective-permute-done.1.s2_ref = bf16[128,2048]{1,0:T(8,128)(2,1)} collective-permute-done((bf16[128,2048]{1,0:T(8,128)(2,1)S(1)}, bf16[128,2048]{1,0:T(8,128)(2,1)}, u32[]{:S(2)}, u32[]{:S(2)}) %collective-permute-start.1) | collective-permute-done | bytes 524320 | tf_op jit(solution)/shard_map/ppermute | solution.py:518
  157.9 12.3 %shard_map.239 = (bf16[4,128,2048]{2,1,0:T(8,128)(2,1)}, f32[128,2048]{1,0:T(8,128)}, bf16[8,1,40,2048]{3,2,1,0:T(8,128)(2,1)}) custom-call(s32[4]{0:T(128)} %iota_xor_fusion.turns_ref, bf16[8,512,256]{2,1,0:T(8,128)(2,1)} %copy-done.7, bf16[4,2048,512]{2,1,0:T(8,128)(2,1)} %bitcast.119, bf16[128,2048]{1,0:T(8,128)(2,1)} %s0_ref.1, ...), custom_call_target="tpu_custom_call" | custom-call | flops 4462739456 | bytes 20971520 | tf_op jit(solution)/shard_map/pallas_call | solution.py:333
  170.2 3.7 all-to-all-start.2
  176.9 14.6 %all-to-all-done.2.after_ref.refs_1_ = bf16[8,1,40,2048]{3,2,1,0:T(8,128)(2,1)S(1)} async-done(((bf16[8,1,40,2048]{3,2,1,0:T(8,128)(2,1)}), bf16[8,1,40,2048]{3,2,1,0:T(8,128)(2,1)S(1)}, u32[]{:S(2)}, u32[]{:S(2)}) %all-to-all-start.2) | async-done | bytes 1310752 | tf_op jit(solution)/shard_map/all_to_all | solution.py:549
  191.5 3.7 all-to-all-start.8
  199.1 10.4 %all-to-all-done.8 = bf16[4,2,256,256]{3,2,1,0:T(8,128)(2,1)S(1)} async-done(((bf16[4,2,256,256]{3,2,1,0:T(8,128)(2,1)}), bf16[4,2,256,256]{3,2,1,0:T(8,128)(2,1)S(1)}, u32[]{:S(2)}, u32[]{:S(2)}) %all-to-all-start.8) | async-done | bytes 1048608 | tf_op jit(solution)/shard_map/all_to_all | solution.py:237
  209.5 3.6 all-to-all-start.4
  214.2 15.0 %shard_map.241.refs_0_ = bf16[8,2,40,2048]{3,2,1,0:T(8,128)(2,1)} custom-call(bf16[8,1,40,2048]{3,2,1,0:T(8,128)(2,1)} %shard_map.240.refs_0_, bf16[8,1,40,2048]{3,2,1,0:T(8,128)(2,1)} %copy-done.2, bf16[320,320]{1,0:T(8,128)(2,1)} %constant.141.clone.refs_2_.refs_3_.refs_4_, bf16[320,320]{1,0:T(8,128)(2,1)} %constant.142.clone.refs_3_.refs_4_.refs_5_, ...), custom_call_target="tpu_custom_call" | custom-call | flops 4865392640 | bytes 27787264 | tf_op jit(solution)/shard_map/pallas_call | solution.py:453
  231.8 4.4 %all-to-all-start.3 = ((bf16[8,2,40,2048]{3,2,1,0:T(8,128)(2,1)}), bf16[8,2,40,2048]{3,2,1,0:T(8,128)(2,1)}, u32[]{:S(2)}, u32[]{:S(2)}) async-start(bf16[8,2,40,2048]{3,2,1,0:T(8,128)(2,1)} %shard_map.241.refs_0_), calls=%async_computation.3 | async-start | bytes 5242880 | tf_op jit(solution)/shard_map/all_to_all | solution.py:549
  237.4 14.9 %shard_map.242.refs_0_ = bf16[8,2,40,2048]{3,2,1,0:T(8,128)(2,1)} custom-call(bf16[8,2,40,2048]{3,2,1,0:T(8,128)(2,1)} %shard_map.241.refs_0_, bf16[8,1,40,2048]{3,2,1,0:T(8,128)(2,1)} %copy-done.3, bf16[320,320]{1,0:T(8,128)(2,1)} %constant.141.clone.refs_2_.refs_3_.refs_4_, bf16[320,320]{1,0:T(8,128)(2,1)} %constant.142.clone.refs_3_.refs_4_.refs_5_, ...), custom_call_target="tpu_custom_call" | custom-call | flops 4865392640 | bytes 27787264 | tf_op jit(solution)/shard_map/pallas_call | solution.py:453
  252.4 15.6 %all-to-all-done.3.refs_2_ = bf16[8,2,40,2048]{3,2,1,0:T(8,128)(2,1)} async-done(((bf16[8,2,40,2048]{3,2,1,0:T(8,128)(2,1)}), bf16[8,2,40,2048]{3,2,1,0:T(8,128)(2,1)}, u32[]{:S(2)}, u32[]{:S(2)}) %all-to-all-start.3) | async-done | bytes 2621472 | tf_op jit(solution)/shard_map/all_to_all | solution.py:549
  268.0 4.4 %all-to-all-start.5 = ((bf16[8,2,40,2048]{3,2,1,0:T(8,128)(2,1)}), bf16[8,2,40,2048]{3,2,1,0:T(8,128)(2,1)}, u32[]{:S(2)}, u32[]{:S(2)}) async-start(bf16[8,2,40,2048]{3,2,1,0:T(8,128)(2,1)} %shard_map.242.refs_0_), calls=%async_computation.5 | async-start | bytes 5242880 | tf_op jit(solution)/shard_map/all_to_all | solution.py:549
  276.2 13.9 %shard_map.243.refs_0_ = bf16[8,1,40,2048]{3,2,1,0:T(8,128)(2,1)} custom-call(bf16[8,2,40,2048]{3,2,1,0:T(8,128)(2,1)} %shard_map.242.refs_0_, bf16[128,2048]{1,0:T(8,128)(2,1)} %fusion.27.refs_1_, bf16[8,2,40,2048]{3,2,1,0:T(8,128)(2,1)} %all-to-all-done.3.refs_2_, bf16[320,320]{1,0:T(8,128)(2,1)} %constant.141.clone.refs_2_.refs_3_.refs_4_, ...), custom_call_target="tpu_custom_call" | custom-call | flops 4865392640 | bytes 27787264 | tf_op jit(solution)/shard_map/pallas_call | solution.py:453
  290.1 14.1 %all-to-all-done.5.refs_3_ = bf16[8,2,40,2048]{3,2,1,0:T(8,128)(2,1)} async-done(((bf16[8,2,40,2048]{3,2,1,0:T(8,128)(2,1)}), bf16[8,2,40,2048]{3,2,1,0:T(8,128)(2,1)}, u32[]{:S(2)}, u32[]{:S(2)}) %all-to-all-start.5) | async-done | bytes 2621472 | tf_op jit(solution)/shard_map/all_to_all | solution.py:549
  304.2 3.8 all-to-all-start.6
  313.3 11.9 %collective-permute-done.3.refs_2_ = bf16[128,2048]{1,0:T(8,128)(2,1)S(1)} collective-permute-done((bf16[128,2048]{1,0:T(8,128)(2,1)}, bf16[128,2048]{1,0:T(8,128)(2,1)S(1)}, u32[]{:S(2)}, u32[]{:S(2)}) %collective-permute-start.3) | collective-permute-done | bytes 524320 | tf_op jit(solution)/shard_map/ppermute | solution.py:567
  326.0 13.9 %shard_map.244 = bf16[8,1,40,2048]{3,2,1,0:T(8,128)(2,1)} custom-call(bf16[8,1,40,2048]{3,2,1,0:T(8,128)(2,1)} %shard_map.243.refs_0_, bf16[128,2048]{1,0:T(8,128)(2,1)} %fusion.28.refs_1_, bf16[128,2048]{1,0:T(8,128)(2,1)} %copy-done.5, bf16[8,2,40,2048]{3,2,1,0:T(8,128)(2,1)} %all-to-all-done.5.refs_3_, ...), custom_call_target="tpu_custom_call" | custom-call | flops 4865392640 | bytes 27787264 | tf_op jit(solution)/shard_map/pallas_call | solution.py:453
  339.9 4.4 %all-to-all-start.7 = ((bf16[8,1,40,2048]{3,2,1,0:T(8,128)(2,1)}), bf16[8,1,40,2048]{3,2,1,0:T(8,128)(2,1)}, u32[]{:S(2)}, u32[]{:S(2)}) async-start(bf16[8,1,40,2048]{3,2,1,0:T(8,128)(2,1)} %shard_map.244), calls=%async_computation.7 | async-start | bytes 2621440 | tf_op jit(solution)/shard_map/all_to_all | solution.py:549
  345.2 11.3 %collective-permute-start.4 = (bf16[128,2048]{1,0:T(8,128)(2,1)S(1)}, bf16[128,2048]{1,0:T(8,128)(2,1)}, u32[]{:S(2)}, u32[]{:S(2)}) collective-permute-start(bf16[128,2048]{1,0:T(8,128)(2,1)S(1)} %copy-done.4), channel_id=1, source_target_pairs={{0,4},{2,6},{4,0},{6,2},{1,5},{3,7},{5,1},{7,3},{8,12},{10,14},{12... | collective-permute-start | bytes 1572872 | tf_op jit(solution)/shard_map/ppermute | solution.py:567
  363.9 16.5 %collective-permute-done.4 = bf16[128,2048]{1,0:T(8,128)(2,1)} collective-permute-done((bf16[128,2048]{1,0:T(8,128)(2,1)S(1)}, bf16[128,2048]{1,0:T(8,128)(2,1)}, u32[]{:S(2)}, u32[]{:S(2)}) %collective-permute-start.4) | collective-permute-done | bytes 524320 | tf_op jit(solution)/shard_map/ppermute | solution.py:567
  (129 shorter events, 60.7 us)
Async XLA Ops:
  7.2 13.7 %copy-start.14 = (bf16[1024,256]{1,0:T(8,128)(2,1)S(1)}, bf16[1024,256]{1,0:T(8,128)(2,1)}, u32[]{:S(2)}) copy-start(bf16[1024,256]{1,0:T(8,128)(2,1)} %param.29) | copy-start | bytes 1572868
  7.2 149.4 %all-gather.2.cloned.1.call-start = ((), (), s32[]{:S(2)}) async-start(), calls=%async_computation.9 | async-start | bytes 8650752 | tf_op jit(solution)/shard_map/all_gather | solution.py:266
  9.1 12.3 %copy-start.12 = (bf16[1024,256]{1,0:T(8,128)(2,1)S(1)}, bf16[1024,256]{1,0:T(8,128)(2,1)}, u32[]{:S(2)}) copy-start(bf16[1024,256]{1,0:T(8,128)(2,1)} %param.27) | copy-start | bytes 1572868
  13.0 19.7 %all-to-all-start.1 = ((f32[4,2,16,128]{3,2,1,0:T(8,128)}), f32[4,2,16,128]{3,2,1,0:T(8,128)S(1)}, u32[]{:S(2)}, u32[]{:S(2)}) async-start(f32[4,2,16,128]{3,2,1,0:T(8,128)} %bitcast.18), calls=%async_computation.1 | async-start | bytes 131072 | tf_op jit(solution)/shard_map/all_to_all | solution.py:529
  34.3 6.2 %copy-start.20 = (bf16[128,2048]{1,0:T(8,128)(2,1)S(1)}, bf16[128,2048]{1,0:T(8,128)(2,1)}, u32[]{:S(2)}) copy-start(bf16[128,2048]{1,0:T(8,128)(2,1)} %s0_ref.1) | copy-start | bytes 1572868
  34.4 122.2 %all-to-all-start = ((bf16[8,512,256]{2,1,0:T(8,128)(2,1)}), bf16[8,512,256]{2,1,0:T(8,128)(2,1)S(1)}, u32[]{:S(2)}, u32[]{:S(2)}) async-start(bf16[8,512,256]{2,1,0:T(8,128)(2,1)} %bitcast.10), calls=%async_computation | async-start | bytes 4194304 | tf_op jit(solution)/shard_map/all_to_all | solution.py:275
  40.5 67.9 %collective-permute-start = (bf16[128,2048]{1,0:T(8,128)(2,1)S(1)}, bf16[128,2048]{1,0:T(8,128)(2,1)S(1)}, u32[]{:S(2)}, u32[]{:S(2)}) collective-permute-start(bf16[128,2048]{1,0:T(8,128)(2,1)S(1)} %copy-done.20), channel_id=1, source_target_pairs={{0,2},{2,0},{4,6},{6,4},{1,3},{3,1},{5,7},{7,5},{8,10},{10,8},{12,... | collective-permute-start | bytes 1572872 | tf_op jit(solution)/shard_map/ppermute | solution.py:518
  42.5 114.0 %collective-permute-start.1 = (bf16[128,2048]{1,0:T(8,128)(2,1)S(1)}, bf16[128,2048]{1,0:T(8,128)(2,1)}, u32[]{:S(2)}, u32[]{:S(2)}) collective-permute-start(bf16[128,2048]{1,0:T(8,128)(2,1)S(1)} %copy-done.20), channel_id=1, source_target_pairs={{0,4},{2,6},{4,0},{6,2},{1,5},{3,7},{5,1},{7,3},{8,12},{10,14},{12... | collective-permute-start | bytes 1572872 | tf_op jit(solution)/shard_map/ppermute | solution.py:518
  44.9 111.7 %collective-permute-start.2 = (bf16[128,2048]{1,0:T(8,128)(2,1)S(1)}, bf16[128,2048]{1,0:T(8,128)(2,1)}, u32[]{:S(2)}, u32[]{:S(2)}) collective-permute-start(bf16[128,2048]{1,0:T(8,128)(2,1)S(1)} %copy-done.20), channel_id=1, source_target_pairs={{0,6},{2,4},{4,2},{6,0},{1,7},{3,5},{5,3},{7,1},{8,14},{10,12},{12... | collective-permute-start | bytes 1572872 | tf_op jit(solution)/shard_map/ppermute | solution.py:518
  108.4 48.2 %copy-start.21 = (bf16[128,2048]{1,0:T(8,128)(2,1)}, bf16[128,2048]{1,0:T(8,128)(2,1)S(1)}, u32[]{:S(2)}) copy-start(bf16[128,2048]{1,0:T(8,128)(2,1)S(1)} %collective-permute-done.s1_ref) | copy-start | bytes 1572868
  170.2 21.4 %all-to-all-start.2 = ((bf16[8,1,40,2048]{3,2,1,0:T(8,128)(2,1)}), bf16[8,1,40,2048]{3,2,1,0:T(8,128)(2,1)S(1)}, u32[]{:S(2)}, u32[]{:S(2)}) async-start(bf16[8,1,40,2048]{3,2,1,0:T(8,128)(2,1)} %get-tuple-element.49), calls=%async_computation.2 | async-start | bytes 2621440 | tf_op jit(solution)/shard_map/all_to_all | solution.py:549
  191.5 18.0 %all-to-all-start.8 = ((bf16[4,2,256,256]{3,2,1,0:T(8,128)(2,1)}), bf16[4,2,256,256]{3,2,1,0:T(8,128)(2,1)S(1)}, u32[]{:S(2)}, u32[]{:S(2)}) async-start(bf16[4,2,256,256]{3,2,1,0:T(8,128)(2,1)} %pad_maximum_fusion), calls=%async_computation.8 | async-start | bytes 2097152 | tf_op jit(solution)/shard_map/all_to_all | solution.py:237
  209.5 21.2 %all-to-all-start.4 = ((bf16[8,1,40,2048]{3,2,1,0:T(8,128)(2,1)}), bf16[8,1,40,2048]{3,2,1,0:T(8,128)(2,1)S(1)}, u32[]{:S(2)}, u32[]{:S(2)}) async-start(bf16[8,1,40,2048]{3,2,1,0:T(8,128)(2,1)} %shard_map.240.refs_0_), calls=%async_computation.4 | async-start | bytes 2621440 | tf_op jit(solution)/shard_map/all_to_all | solution.py:549
  231.8 36.2 %all-to-all-start.3 = ((bf16[8,2,40,2048]{3,2,1,0:T(8,128)(2,1)}), bf16[8,2,40,2048]{3,2,1,0:T(8,128)(2,1)}, u32[]{:S(2)}, u32[]{:S(2)}) async-start(bf16[8,2,40,2048]{3,2,1,0:T(8,128)(2,1)} %shard_map.241.refs_0_), calls=%async_computation.3 | async-start | bytes 5242880 | tf_op jit(solution)/shard_map/all_to_all | solution.py:549
  252.4 20.0 %copy-start.19 = (s32[256]{0:T(256)S(1)}, s32[256]{0:T(256)}, u32[]{:S(2)}) copy-start(s32[256]{0:T(256)} %param.38) | copy-start | bytes 3076
  268.0 36.2 %all-to-all-start.5 = ((bf16[8,2,40,2048]{3,2,1,0:T(8,128)(2,1)}), bf16[8,2,40,2048]{3,2,1,0:T(8,128)(2,1)}, u32[]{:S(2)}, u32[]{:S(2)}) async-start(bf16[8,2,40,2048]{3,2,1,0:T(8,128)(2,1)} %shard_map.242.refs_0_), calls=%async_computation.5 | async-start | bytes 5242880 | tf_op jit(solution)/shard_map/all_to_all | solution.py:549
  304.2 35.7 %all-to-all-start.6 = ((bf16[8,1,40,2048]{3,2,1,0:T(8,128)(2,1)}), bf16[8,1,40,2048]{3,2,1,0:T(8,128)(2,1)S(1)}, u32[]{:S(2)}, u32[]{:S(2)}) async-start(bf16[8,1,40,2048]{3,2,1,0:T(8,128)(2,1)} %shard_map.243.refs_0_), calls=%async_computation.6 | async-start | bytes 2621440 | tf_op jit(solution)/shard_map/all_to_all | solution.py:549
  309.1 16.1 %collective-permute-start.3 = (bf16[128,2048]{1,0:T(8,128)(2,1)}, bf16[128,2048]{1,0:T(8,128)(2,1)S(1)}, u32[]{:S(2)}, u32[]{:S(2)}) collective-permute-start(bf16[128,2048]{1,0:T(8,128)(2,1)} %fusion.27.refs_1_), channel_id=1, source_target_pairs={{0,6},{2,4},{4,2},{6,0},{1,7},{3,5},{5,3},{7,1},{8,14},{10,12},{12... | collective-permute-start | bytes 1572872 | tf_op jit(solution)/shard_map/ppermute | solution.py:567
  339.9 5.3 %copy-start.4 = (bf16[128,2048]{1,0:T(8,128)(2,1)S(1)}, bf16[128,2048]{1,0:T(8,128)(2,1)}, u32[]{:S(2)}) copy-start(bf16[128,2048]{1,0:T(8,128)(2,1)} %fusion.28.refs_1_) | copy-start | bytes 1572868
  339.9 16.6 %copy-start.10 = (f32[320,128]{1,0:T(8,128)S(1)}, f32[320,128]{1,0:T(8,128)}, u32[]{:S(2)}) copy-start(f32[320,128]{1,0:T(8,128)} %get-tuple-element.87) | copy-start | bytes 491524
  339.9 22.2 %all-to-all-start.7 = ((bf16[8,1,40,2048]{3,2,1,0:T(8,128)(2,1)}), bf16[8,1,40,2048]{3,2,1,0:T(8,128)(2,1)}, u32[]{:S(2)}, u32[]{:S(2)}) async-start(bf16[8,1,40,2048]{3,2,1,0:T(8,128)(2,1)} %shard_map.244), calls=%async_computation.7 | async-start | bytes 2621440 | tf_op jit(solution)/shard_map/all_to_all | solution.py:549
  345.2 35.2 %collective-permute-start.4 = (bf16[128,2048]{1,0:T(8,128)(2,1)S(1)}, bf16[128,2048]{1,0:T(8,128)(2,1)}, u32[]{:S(2)}, u32[]{:S(2)}) collective-permute-start(bf16[128,2048]{1,0:T(8,128)(2,1)S(1)} %copy-done.4), channel_id=1, source_target_pairs={{0,4},{2,6},{4,0},{6,2},{1,5},{3,7},{5,1},{7,3},{8,12},{10,14},{12... | collective-permute-start | bytes 1572872 | tf_op jit(solution)/shard_map/ppermute | solution.py:567
  358.3 22.7 %collective-permute-start.5 = (bf16[128,2048]{1,0:T(8,128)(2,1)}, bf16[128,2048]{1,0:T(8,128)(2,1)S(1)}, u32[]{:S(2)}, u32[]{:S(2)}) collective-permute-start(bf16[128,2048]{1,0:T(8,128)(2,1)} %fusion.29), channel_id=1, source_target_pairs={{0,2},{2,0},{4,6},{6,4},{1,3},{3,1},{5,7},{7,5},{8,10},{10,8},{12,... | collective-permute-start | bytes 1572872 | tf_op jit(solution)/shard_map/ppermute | solution.py:567
  359.6 21.4 %copy-start.6 = (bf16[128,2048]{1,0:T(8,128)(2,1)S(1)}, bf16[128,2048]{1,0:T(8,128)(2,1)}, u32[]{:S(2)}) copy-start(bf16[128,2048]{1,0:T(8,128)(2,1)} %copy-done.5) | copy-start | bytes 1572868
  (15 other events, 43.2 us)
Sparse Core Ops, SparseCore 0:
  11.6 136.5 all-gather.1

commit v3 on v1

--- a/solution.py
+++ b/solution.py
@@ -210,9 +210,8 @@
     )
 
 
-def move_pages(keys, values, page_table):
-    rows = keys.shape[0]
-    width = keys.shape[1]
+def move_pages(keys, values, page_table, after):
+    rows, width = keys.shape
     page_rows = rows // PAGE
     groups = lax.axis_size("req")
     per_group = page_rows // groups
@@ -222,75 +221,230 @@
     target = own_table // page_rows
     picked = target[:, None] == jnp.arange(groups, dtype=jnp.int32)[None, :]
     ranking = jnp.sum(jnp.where(picked, count_before(picked), 0.0), axis=1).astype(jnp.int32)
-    slot = target * per_group + ranking
+    slot = (target ^ myself) * per_group + ranking
     within = jnp.arange(PAGE, dtype=jnp.int32)
     lines = jnp.arange(rows, dtype=jnp.int32)
-    target_line = (slot[:, None] * PAGE + within[None, :]).reshape(-1)
+    target_line = (slot[:, None] * PAGE + within[None, :]).reshape(-1, 128)
+    target_line = tie(target_line, after).reshape(-1)
     spread = (target_line[None, :] == lines[:, None]).astype(jnp.bfloat16)
-    sent = [
-        jnp.dot(spread, block, preferred_element_type=jnp.float32)
-        .astype(jnp.bfloat16)
-        .reshape(groups, rows // groups, width)
-        for block in (keys, values)
+    both = jnp.concatenate([keys, values], axis=1)
+    sent = jnp.dot(spread, both, preferred_element_type=jnp.float32).astype(jnp.bfloat16)
+    sent = sent.reshape(groups, rows // groups, 2 * width)
+    incoming = [sent[0]]
+    for apart in range(1, groups):
+        pairs = [(low, low ^ apart) for low in range(groups)]
+        incoming.append(lax.ppermute(sent[apart], "req", pairs))
+
+    def place():
+        arriving = whole_table // page_rows == myself
+        arrival = count_before(arriving.T).T.astype(jnp.int32)
+        apart = jnp.arange(groups, dtype=jnp.int32)[:, None] ^ myself
+        source = apart * per_group + arrival
+        landing = jnp.where(arriving, whole_table % page_rows, -1).reshape(-1)
+        slots = jnp.arange(page_rows, dtype=jnp.int32)
+        source_page = jnp.sum(
+            jnp.where(landing[None, :] == slots[:, None], source.reshape(-1)[None, :], 0), axis=1
+        )
+        source_line = (source_page[:, None] * PAGE + within[None, :]).reshape(-1)
+        collect = (source_line[:, None] == lines[None, :]).astype(jnp.bfloat16)
+        placed = jnp.dot(
+            collect, jnp.concatenate(incoming, axis=0), preferred_element_type=jnp.float32
+        ).astype(jnp.bfloat16)
+        placed = placed.reshape(page_rows, PAGE, 2, width)
+        return jnp.transpose(placed, (0, 2, 1, 3))
+
+    return incoming, place
+
+
+def attend_kernel(query_ref, key_ref, value_ref, line_ref, row_ref, out_ref):
+    allowed = line_ref[...] == row_ref[...]
+    half = out_ref.shape[1]
+    scaling = 1.0 / math.sqrt(HD)
+    for head in range(query_ref.shape[1] // HD):
+        span = slice(head * HD, (head + 1) * HD)
+        scores = lax.dot_general(
+            query_ref[:, span],
+            key_ref[:, span],
+            (((1,), (1,)), ((), ())),
+            preferred_element_type=jnp.float32,
+        )
+        scores = jnp.where(allowed, scores * scaling, jnp.float32(-1e30))
+        weights = jnp.exp(scores - jnp.max(scores, axis=1, keepdims=True))
+        totals = jnp.sum(weights, axis=1, keepdims=True)
+        mixed = jnp.dot(
+            weights.astype(jnp.bfloat16), value_ref[:, span], preferred_element_type=jnp.float32
+        )
+        mixed = (mixed / totals).astype(jnp.bfloat16)
+        out_ref[0, :, span] = mixed[:half]
+        out_ref[1, :, span] = mixed[half:]
+
+
+def attend_columns(queries, keys, values, segments, tok_rows):
+    rows, width = queries.shape
+    block = 2 * tok_rows
+    steps = rows // block
+    return pl.pallas_call(
+        attend_kernel,
+        grid=(steps,),
+        in_specs=[
+            pl.BlockSpec((block, width), lambda i: (i, 0)),
+            pl.BlockSpec((rows, width), lambda i: (0, 0)),
+            pl.BlockSpec((rows, width), lambda i: (0, 0)),
+            pl.BlockSpec((block, 1), lambda i: (i, 0)),
+            pl.BlockSpec((1, rows), lambda i: (0, 0)),
+        ],
+        out_specs=pl.BlockSpec((2, tok_rows, width), lambda i: (0, i, 0)),
+        out_shape=jax.ShapeDtypeStruct((2, rows // 2, width), jnp.bfloat16),
+        compiler_params=pltpu.CompilerParams(vmem_limit_bytes=40 * 1024 * 1024),
+        cost_estimate=pl.CostEstimate(
+            flops=4 * rows * rows * width,
+            bytes_accessed=8 * rows * width,
+            transcendentals=rows * rows * width // HD,
+        ),
+    )(queries, keys, values, segments.reshape(rows, 1), segments.reshape(1, rows))
+
+
+def partial_kernel(place_ref, mine_ref, other_ref, weight_ref, first_ref, rest_ref, out_ref, total):
+    step = pl.program_id(0)
+    total[...] = jnp.dot(mine_ref[0], weight_ref[...], preferred_element_type=jnp.float32)
+
+    @pl.when(step < 2)
+    def _():
+        total[...] += jnp.dot(other_ref[...], first_ref[...], preferred_element_type=jnp.float32)
+
+    @pl.when(step >= 2)
+    def _():
+        total[...] += jnp.dot(other_ref[...], rest_ref[...], preferred_element_type=jnp.float32)
+
+    out_ref[...] = total[...].reshape(out_ref.shape).astype(jnp.bfloat16)
+
+
+def partial_products(place, attended, other, out_weight, other_weight, other_rest):
+    _, rows, width = attended.shape
+    strip = D // 4
+    column_of = lambda i, p: (i // 2 ^ p[1]) * 2 + i % 2
+    return pl.pallas_call(
+        partial_kernel,
+        grid_spec=pltpu.PrefetchScalarGridSpec(
+            num_scalar_prefetch=1,
+            grid=(4,),
+            in_specs=[
+                pl.BlockSpec((1, rows, width), lambda i, p: (p[0], 0, 0)),
+                pl.BlockSpec((rows, width), lambda i, p: (0, 0)),
+                pl.BlockSpec((width, strip), lambda i, p: (0, column_of(i, p))),
+                pl.BlockSpec((width, strip), lambda i, p: (0, jnp.minimum(i, 1))),
+                pl.BlockSpec((width, strip), lambda i, p: (0, jnp.maximum(i - 2, 0))),
+            ],
+            out_specs=pl.BlockSpec(
+                (PLANES, rows // PLANES, strip), lambda i, p: (0, 0, column_of(i, p))
+            ),
+            scratch_shapes=[pltpu.VMEM((rows, strip), jnp.float32)],
+        ),
+        out_shape=jax.ShapeDtypeStruct((PLANES, rows // PLANES, D), jnp.bfloat16),
+        compiler_params=pltpu.CompilerParams(vmem_limit_bytes=40 * 1024 * 1024),
+        cost_estimate=pl.CostEstimate(
+            flops=4 * rows * width * D, bytes_accessed=2 * (rows + 2 * width) * D, transcendentals=0
+        ),
+    )(place, attended, other, out_weight, other_weight, other_rest)
+
+
+def pack_rows(picking, block, shape):
+    rows = jnp.dot(picking, block, preferred_element_type=jnp.float32)
+    return rows.reshape(shape).astype(jnp.bfloat16)
+
+
+def norm_kernel(*refs):
+    stream_ref, parts_ref, gain_ref, picking_ref, normed_ref, residual_ref, packed_ref = refs[-7:]
+    residual = stream_ref[...].astype(jnp.float32)
+    for plane in range(PLANES):
+        residual = residual + parts_ref[plane].astype(jnp.float32)
+    residual_ref[...] = residual
+    scale = lax.rsqrt(jnp.mean(residual * residual, axis=1, keepdims=True) + 1e-06)
+    normed = (residual * scale * gain_ref[...]).astype(jnp.bfloat16)
+    normed_ref[...] = normed
+    packed_ref[:, 0] = pack_rows(
+        picking_ref[...], normed, (packed_ref.shape[0],) + packed_ref.shape[2:]
+    )
+
+
+def norm_and_pack(after, stream_in, parts, norm_gain, picking, sources):
+    tok_rows = stream_in.shape[0]
+    height = picking.shape[0]
+    operands = (stream_in, parts, norm_gain.reshape(1, D), picking)
+    shapes = [
+        jax.ShapeDtypeStruct((tok_rows, D), jnp.bfloat16),
+        jax.ShapeDtypeStruct((tok_rows, D), jnp.float32),
+        jax.ShapeDtypeStruct((sources, 1, height // sources, D), jnp.bfloat16),
     ]
-    incoming = lax.all_to_all(
-        jnp.stack(sent, axis=1), "req", split_axis=0, concat_axis=0, tiled=True
-    )
-    arriving = whole_table // page_rows == myself
-    arrival = count_before(arriving.T).T.astype(jnp.int32)
-    source = jnp.arange(groups, dtype=jnp.int32)[:, None] * per_group + arrival
-    landing = jnp.where(arriving, whole_table % page_rows, -1).reshape(-1)
-    slots = jnp.arange(page_rows, dtype=jnp.int32)
-    source_page = jnp.sum(
-        jnp.where(landing[None, :] == slots[:, None], source.reshape(-1)[None, :], 0), axis=1
-    )
-    source_line = (source_page[:, None] * PAGE + within[None, :]).reshape(-1)
-    collect = (source_line[:, None] == lines[None, :]).astype(jnp.bfloat16)
-    placed = [
-        jnp.dot(
-            collect, incoming[:, part].reshape(rows, width), preferred_element_type=jnp.float32
-        )
-        .astype(jnp.bfloat16)
-        .reshape(page_rows, PAGE, width)
-        for part in range(2)
-    ]
-    return jnp.stack(placed, axis=1)
-
-
-def project_rows(attended, out_weight):
-    groups = lax.axis_size("req")
-    members = lax.axis_size("z") * lax.axis_size("x")
-    tok_rows = attended.shape[0] // members
-    strip = out_weight.shape[1] // groups
-    start = lax.axis_index("req") * strip
-    piece = lax.dynamic_slice_in_dim(out_weight, start, strip, 1)
-    strips = lax.all_gather(piece, ("req", "z", "x"), axis=0, tiled=True)
-    strips = strips.reshape(groups, members * out_weight.shape[0], strip)
-    shares = lax.all_to_all(
-        attended.reshape(members, tok_rows, attended.shape[1]),
-        ("z", "x"),
-        split_axis=0,
-        concat_axis=0,
-        tiled=True,
-    )
-    whole_rows = jnp.transpose(shares, (1, 0, 2)).reshape(tok_rows, -1)
-    return jnp.concatenate(
-        [
-            jnp.dot(whole_rows, strips[index], preferred_element_type=jnp.float32)
-            for index in range(groups)
+    whole = lambda a: pl.BlockSpec(a.shape, lambda i, rank=len(a.shape): (0,) * rank)
+    return pl.pallas_call(
+        norm_kernel,
+        grid=(1,),
+        in_specs=[pl.BlockSpec(memory_space=pl.ANY)] * len(after) + [whole(a) for a in operands],
+        out_specs=[whole(a) for a in shapes],
+        out_shape=shapes,
+        compiler_params=pltpu.CompilerParams(vmem_limit_bytes=40 * 1024 * 1024),
+        cost_estimate=pl.CostEstimate(
+            flops=2 * height * tok_rows * D + 10 * tok_rows * D,
+            bytes_accessed=(16 * tok_rows + 2 * height) * D,
+            transcendentals=tok_rows,
+        ),
+    )(*after, *operands)
+
+
+def pack_kernel(after_ref, picking_ref, block_ref, out_ref):
+    out_ref[:, 0] = pack_rows(
+        picking_ref[...], block_ref[...], (out_ref.shape[0],) + out_ref.shape[2:]
+    )
+
+
+def pack_after(after, picking, block, sources, into=False):
+    height, tok_rows = picking.shape
+    parts = 2 if into else 1
+    return pl.pallas_call(
+        pack_kernel,
+        grid=(1,),
+        in_specs=[
+            pl.BlockSpec(memory_space=pl.ANY),
+            pl.BlockSpec((height, tok_rows), lambda i: (0, 0)),
+            pl.BlockSpec((tok_rows, D), lambda i: (0, 0)),
         ],
-        axis=1,
-    )
-
-
-def expert_kernel(rows_ref, order_ref, back_ref, gate_ref, up_ref, down_ref, out_ref, sorted_rows, total, outs):
+        out_specs=pl.BlockSpec((sources, 1, height // sources, D), lambda i: (0, parts - 1, 0, 0)),
+        out_shape=jax.ShapeDtypeStruct((sources, parts, height // sources, D), jnp.bfloat16),
+        input_output_aliases={0: 0} if into else {},
+        compiler_params=pltpu.CompilerParams(vmem_limit_bytes=40 * 1024 * 1024),
+        cost_estimate=pl.CostEstimate(
+            flops=2 * height * tok_rows * D, bytes_accessed=4 * height * D, transcendentals=0
+        ),
+    )(after, picking, block)
+
+
+def tie_kernel(*refs):
+    del refs
+
+
+def tie(block, *after):
+    return pl.pallas_call(
+        tie_kernel,
+        in_specs=[pl.BlockSpec(memory_space=pl.ANY)] * (1 + len(after)),
+        out_specs=pl.BlockSpec(memory_space=pl.ANY),
+        out_shape=jax.ShapeDtypeStruct(block.shape, block.dtype),
+        input_output_aliases={0: 0},
+    )(block, *after)
+
+
+def expert_kernel(*refs):
+    (rows_ref, order_ref, back_ref, gate_ref, up_ref, down_ref) = refs[-10:-4]
+    out_ref, sorted_rows, total, outs = refs[-4:]
     step = pl.program_id(0)
-    count = sorted_rows.shape[0] // 2
+    height, depth = sorted_rows.shape
+    count = height // 2
 
     @pl.when(step == 0)
     def _():
+        rows = rows_ref[:, 0].astype(jnp.float32).reshape(height, depth).astype(jnp.bfloat16)
         sorted_rows[...] = jnp.dot(
-            order_ref[...], rows_ref[...], preferred_element_type=jnp.float32
+            order_ref[...], rows, preferred_element_type=jnp.float32
         ).astype(jnp.bfloat16)
 
     first = pl.multiple_of((step // 2) * count, 16)
@@ -310,49 +464,49 @@
 
     @pl.when(step == 3)
     def _():
-        out_ref[...] = jnp.dot(
-            back_ref[...], outs[...], preferred_element_type=jnp.float32
-        ).astype(jnp.bfloat16)
-
-
-def run_experts(rows, sources, w_gate, w_up, w_down):
-    height, depth = rows.shape
+        out_ref[:, 0] = pack_rows(back_ref[...], outs[...], (out_ref.shape[0],) + out_ref.shape[2:])
+
+
+def run_experts(after, arrived, w_gate, w_up, w_down, out_parts=1):
+    sources, parts, slots, depth = arrived.shape
     units = w_gate.shape[2]
-    slots = height // (sources * 2)
+    height = sources * slots
     index = np.arange(height)
     wanted = (
-        index % (height // 2) // slots * (2 * slots)
-        + index // (height // 2) * slots
-        + index % slots
+        index % (height // 2) // (slots // 2) * slots
+        + index // (height // 2) * (slots // 2)
+        + index % (slots // 2)
     )
     order = (wanted[:, None] == index[None, :]).astype(np.float32)
     fixed = lambda i: (0, 0)
     return pl.pallas_call(
         expert_kernel,
         grid=(4,),
-        in_specs=[
-            pl.BlockSpec((height, depth), fixed),
+        in_specs=[pl.BlockSpec(memory_space=pl.ANY)] * len(after)
+        + [
+            pl.BlockSpec((sources, 1, slots, depth), lambda i: (0, parts - 1, 0, 0)),
             pl.BlockSpec((height, height), fixed),
             pl.BlockSpec((height, height), fixed),
             pl.BlockSpec((1, depth, units), lambda i: (i, 0, 0)),
             pl.BlockSpec((1, depth, units), lambda i: (i, 0, 0)),
             pl.BlockSpec((1, units, depth), lambda i: (i, 0, 0)),
         ],
-        out_specs=pl.BlockSpec((height, depth), fixed),
-        out_shape=jax.ShapeDtypeStruct((height, depth), jnp.bfloat16),
+        out_specs=pl.BlockSpec((sources, 1, slots, depth), lambda i: (0, 0, 0, 0)),
+        out_shape=jax.ShapeDtypeStruct((sources, out_parts, slots, depth), jnp.bfloat16),
         scratch_shapes=[
             pltpu.VMEM((height, depth), jnp.bfloat16),
             pltpu.VMEM((height // 2, depth), jnp.float32),
             pltpu.VMEM((height, depth), jnp.bfloat16),
         ],
-        compiler_params=pltpu.CompilerParams(vmem_limit_bytes=40 * 1024 * 1024),
+        compiler_params=pltpu.CompilerParams(vmem_limit_bytes=56 * 1024 * 1024),
         cost_estimate=pl.CostEstimate(
             flops=12 * height * depth * units + 4 * height * height * depth,
             bytes_accessed=12 * depth * units * 2 + 4 * height * depth,
             transcendentals=2 * height * units,
         ),
     )(
-        rows,
+        *after,
+        arrived,
         jnp.asarray(order, jnp.bfloat16),
         jnp.asarray(order.T, jnp.bfloat16),
         w_gate,
@@ -383,6 +537,18 @@
     plane_experts = 2 * sources
     height = plane_experts * MOST
     level = lax.axis_index("z")
+    column = lax.axis_index("x")
+    swap = [(0, 1), (1, 0)]
+    pairs = [[(low, low ^ turn) for low in range(PLANES)] for turn in range(PLANES)]
+
+    core = lax.axis_index("req") % 2
+    cores = [(low, low ^ 1) for low in range(groups)]
+    half = lax.dynamic_slice_in_dim(out_weight, core * (D // 2), D // 2, 1)
+    other_weight = lax.ppermute(half, "x", swap)
+    other_rest = lax.ppermute(other_weight, "req", cores)
+    attended = attend_columns(queries, keys, values, segment_ids[0], tok_rows)
+    leaving = lax.dynamic_index_in_dim(attended, 1 - column, 0, keepdims=False)
+    other = lax.ppermute(tie(leaving, other_weight), "x", swap)
 
     matched = routes[:, :, None] == jnp.arange(EXPERTS, dtype=jnp.int32)[None, None, :]
     named = jnp.any(matched, axis=1)
@@ -393,56 +559,81 @@
     tables = jnp.stack([slot_of.T, weight_of.T])
     tables = tables.reshape(2, groups, PLANES, 2 * lanes, tok_rows)
     tables = jnp.transpose(tables, (2, 0, 1, 3, 4)).reshape(PLANES, 2, plane_experts, tok_rows)
-    tables = lax.all_to_all(tables, "z", split_axis=0, concat_axis=0, tiled=True)
-
-    attended = attend_rows(queries, keys, values, segment_ids[0])
-    residual = stream_in.astype(jnp.float32) + project_rows(attended, out_weight)
-    scale_rows = lax.rsqrt(jnp.mean(residual * residual, axis=1, keepdims=True) + 1e-06)
-    normed = (residual * scale_rows * norm_gain).astype(jnp.bfloat16)
-    kv_cache = move_pages(keys, values, page_table)
-
     lines = jnp.arange(height, dtype=jnp.float32)
-    total = residual
+    pickings, mixings = [], []
     for turn in range(PLANES):
-        pairs = [(low, low ^ turn) for low in range(PLANES)]
         table = lax.dynamic_index_in_dim(tables, level ^ turn, 0, keepdims=False)
+        if turn:
+            table = lax.ppermute(table, "z", pairs[turn])
         hits = table[0][:, None, :] == lines[None, :, None]
-        picking = jnp.sum(hits.astype(jnp.float32), axis=0).astype(jnp.bfloat16)
+        pickings.append(jnp.sum(hits.astype(jnp.float32), axis=0).astype(jnp.bfloat16))
         mixing = jnp.sum(jnp.where(hits, table[1][:, None, :], 0.0), axis=0)
-        mixing_high = mixing.astype(jnp.bfloat16)
-        mixing_low = (mixing - mixing_high.astype(jnp.float32)).astype(jnp.bfloat16)
-        block = normed if turn == 0 else lax.ppermute(normed, "z", pairs)
-        packed = jnp.dot(picking, block, preferred_element_type=jnp.float32).astype(jnp.bfloat16)
-        arrived = lax.all_to_all(
-            packed.reshape(sources, 2 * MOST, D),
-            ("req", "x"),
-            split_axis=0,
-            concat_axis=0,
-            tiled=True,
+        high = mixing.astype(jnp.bfloat16)
+        mixings.append((high, (mixing - high.astype(jnp.float32)).astype(jnp.bfloat16)))
+
+    partial = partial_products(
+        jnp.stack([column, core]).astype(jnp.int32),
+        attended,
+        other,
+        out_weight,
+        other_weight,
+        other_rest,
+    )
+    gathered = lax.all_to_all(partial, "z", split_axis=0, concat_axis=0, tiled=True)
+    pages, place_pages = move_pages(keys, values, page_table, partial)
+    normed, residual, packed = norm_and_pack(
+        pages[1:], stream_in, gathered, norm_gain, pickings[0], sources
+    )
+
+    def exchange(block):
+        return lax.all_to_all(block, ("req", "x"), split_axis=0, concat_axis=0, tiled=True)
+
+    def experts(after, arrived, out_parts=1):
+        return run_experts(after, arrived, w_gate, w_up, w_down, out_parts)
+
+    def mixed(turn, returned):
+        return sum(
+            lax.dot_general(
+                part,
+                returned[:, 0].reshape(height, D),
+                (((0,), (0,)), ((), ())),
+                preferred_element_type=jnp.float32,
+            )
+            for part in mixings[turn]
         )
-        outs = run_experts(arrived.reshape(height, D), sources, w_gate, w_up, w_down)
-        returned = lax.all_to_all(
-            outs.reshape(sources, 2 * MOST, D),
-            ("req", "x"),
-            split_axis=0,
-            concat_axis=0,
-            tiled=True,
-        ).reshape(height, D)
-        share = sum(
-            lax.dot_general(
-                part, returned, (((0,), (0,)), ((), ())), preferred_element_type=jnp.float32
-            )
-            for part in (mixing_high, mixing_low)
-        )
-        if turn:
-            share = lax.ppermute(share.astype(jnp.bfloat16), "z", pairs).astype(jnp.float32)
-        total = total + share
-    return (total.astype(jnp.bfloat16), kv_cache)
+
+    def to_plane(turn, block):
+        return lax.ppermute(block, "z", pairs[turn])
+
+    blocks = [normed] + [to_plane(turn, normed) for turn in range(1, PLANES)]
+    own = exchange(packed)
+    packed_third = pack_after(own, pickings[3], blocks[3], sources)
+    third = exchange(packed_third)
+    packed_second = pack_after(third, pickings[2], blocks[2], sources)
+    second = exchange(packed_second)
+    outs_third = experts([packed_second], third, 2)
+    outs_third = pack_after(outs_third, pickings[1], blocks[1], sources, into=True)
+    first = exchange(outs_third)
+    outs_second = experts([outs_third], second)
+    back_second = exchange(outs_second)
+    share_third = mixed(3, first).astype(jnp.bfloat16)
+    outs_first = experts([outs_second, share_third], first)
+    got_third = to_plane(3, share_third)
+    back_first = exchange(outs_first)
+    share_second = mixed(2, tie(back_second, got_third)).astype(jnp.bfloat16)
+    outs_own = experts([share_second], own)
+    got_second = to_plane(2, share_second)
+    back_own = exchange(outs_own)
+    share_first = mixed(1, tie(back_first, got_second)).astype(jnp.bfloat16)
+    total = residual + got_third.astype(jnp.float32) + got_second.astype(jnp.float32)
+    total = total + to_plane(1, share_first).astype(jnp.float32)
+    total = total + mixed(0, back_own)
+    return (total.astype(jnp.bfloat16), place_pages())
 
 
 def solution(mesh):
     requests, members = mesh.shape["req"], mesh.shape["exp"]
-    whole = 2 * EXPERTS == 4 * requests * members
+    whole = 2 * EXPERTS == 4 * requests * members and members == 2 * PLANES
     if whole:
         grid = mesh.devices.reshape(requests, PLANES, members // PLANES)
         mesh = Mesh(grid, ("req", "z", "x"))

time: 353 us -> 328 us (0.929)
  matrix products: 39.2 us -> 13.9 us
  Pallas kernels: 46 us -> 70.9 us
  between operations: 14.5 us -> 1.05 us
  local copies, waits for them, and re-layouts: 30.2 us -> 23 us
  waiting for transfers between devices: 140 us -> 147 us
  other arithmetic: 12.9 us -> 8.06 us
    all_gather x1 -> x0, waiting for transfers between devices: 40.2 us -> none  [project_rows(): strips = lax.all_gather(piece, ('req', 'z', 'x'), axis=0, tiled=True)]
    ppermute x6 -> x15, waiting for transfers between devices: 69.2 us -> 99.8 us  [the longest x3 41 us: on_device_whole(): table = lax.ppermute(table, 'z', pairs[turn])]
    pallas_call x4 -> x14, Pallas kernels: 46 us -> 70.9 us  [the longest x4 56.9 us: run_experts(): pl.pallas_call(expert_kernel, grid=(4,), in_specs=[pl.BlockSpec(memory_sp...]
    dot_general x24 -> x10, matrix products: 37.4 us -> 13.5 us  [the longest x8 8.39 us: mixed(): lax.dot_general(part, returned[:, 0].reshape(height, D), (((0,), (0,)), (...]
    all_to_all x11 -> x8, waiting for transfers between devices: 31.1 us -> 46.8 us  [the longest x1 29.6 us: on_device_whole(): lax.all_to_all(partial, 'z', split_axis=0, concat_axis=0, tiled=True)]
    all_to_all x11 -> x8, starting transfers between devices: 48.6 us -> 33.4 us  [the longest x7 28.1 us: exchange(): lax.all_to_all(block, ('req', 'x'), split_axis=0, concat_axis=0, tiled=True)]
    ppermute x6 -> x15, starting transfers between devices: 17.9 us -> 29.6 us  [the longest x6 20.5 us: to_plane(): return lax.ppermute(block, 'z', pairs[turn])]
    unnamed x57 -> x74, local copies, waits for them, and re-layouts: 18.5 us -> 12.9 us
  transfers between devices with their start and end apart: 18 -> 23, of which waited for: 10 -> 11; matrix products, arithmetic and copies ran while one was open for 17% -> 9% of each run, Pallas kernels for 13% -> 19%
where the time goes in v3:
time: 328 us; the launch traced here: 326 us
  waiting for transfers between devices  147 us (45%)
  Pallas kernels  70.9 us (22%)
  starting transfers between devices  63 us (19%)
  local copies, waits for them, and re-layouts  23 us (7%)
  matrix products  13.9 us (4%)
  other arithmetic  8.06 us (2%)
    pallas_call x4, Pallas kernels, run_experts(): pl.pallas_call(expert_kernel, grid=(4,), in_specs=[pl.BlockSpec(memory_sp...  56.9 us
    ppermute x3, waiting for transfers between devices, on_device_whole(): table = lax.ppermute(table, 'z', pairs[turn])  41 us
    all_to_all x1, waiting for transfers between devices, on_device_whole(): lax.all_to_all(partial, 'z', split_axis=0, concat_axis=0, tiled=True)  29.6 us
    ppermute x6, waiting for transfers between devices, to_plane(): return lax.ppermute(block, 'z', pairs[turn])  28.5 us
    all_to_all x7, starting transfers between devices, exchange(): lax.all_to_all(block, ('req', 'x'), split_axis=0, concat_axis=0, tiled=True)  28.1 us
    ppermute x6, starting transfers between devices, to_plane(): return lax.ppermute(block, 'z', pairs[turn])  20.5 us
    all_to_all x7, waiting for transfers between devices, exchange(): lax.all_to_all(block, ('req', 'x'), split_axis=0, concat_axis=0, tiled=True)  17.2 us
    unnamed x74, local copies, waits for them, and re-layouts  12.9 us
  transfers between devices with their start and end apart: 23, of which 11 were waited for; matrix products, arithmetic and copies ran while one was open for 9% of the time, Pallas kernels for 19%

profile of v3, /device:TPU:0, one launch (start us, length us, event | category | flops | bytes accessed | tf_op | source)
XLA Modules:
  0.0 326.4 jit_solution(11739282377217008181)
XLA Ops:
  4.7 11.9 %collective-permute-done.refs_1_.first_ref = bf16[256,1024]{1,0:T(8,128)(2,1)S(1)} collective-permute-done((bf16[256,1024]{1,0:T(8,128)(2,1)S(1)}, bf16[256,1024]{1,0:T(8,128)(2,1)S(1)}, u32[]{:S(2)}, u32[]{:S(2)}) %collective-permute-start) | collective-permute-done | bytes 524320 | tf_op jit(solution)/shard_map/ppermute | solution.py:547
  21.4 5.0 %shard_map.239.mine_ref = bf16[2,512,256]{2,1,0:T(8,128)(2,1)S(1)} custom-call(bf16[1024,256]{1,0:T(8,128)(2,1)S(1)} %copy-done.13, bf16[1024,256]{1,0:T(8,128)(2,1)S(1)} %copy-done.14, bf16[1024,256]{1,0:T(8,128)(2,1)S(1)} %copy-done.16, s32[1024,1]{1,0:T(8,128)S(1)} %copy.44.line_ref, s32[1,1024]{1,0:T(1,128)S(1)} %copy-done.12), custom_call_target="tpu_custom_call" | custom-call | flops 1073741824 | bytes 2097152 | tf_op jit(solution)/shard_map/pallas_call | solution.py:286
  28.9 7.1 %collective-permute-done.1.other_ref = bf16[512,256]{1,0:T(8,128)(2,1)S(1)} collective-permute-done((bf16[512,256]{1,0:T(8,128)(2,1)}, bf16[512,256]{1,0:T(8,128)(2,1)S(1)}, u32[]{:S(2)}, u32[]{:S(2)}) %collective-permute-start.1) | collective-permute-done | bytes 262176 | tf_op jit(solution)/shard_map/ppermute | solution.py:551
  37.1 4.4 %shard_map.241.refs_1_ = bf16[4,128,2048]{2,1,0:T(8,128)(2,1)} custom-call(s32[2]{0:T(128)S(1)} %pad_add_fusion.place_ref, bf16[2,512,256]{2,1,0:T(8,128)(2,1)S(1)} %shard_map.239.mine_ref, bf16[512,256]{1,0:T(8,128)(2,1)S(1)} %collective-permute-done.1.other_ref, bf16[256,2048]{1,0:T(8,128)(2,1)S(1)} %copy-done.5, bf16[256,1024]{1,0:T(8,128)(2,1)S(1)} %copy-done.7, ...), custom_call_target="tpu_custom_call" | custom-call | flops 1073741824 | bytes 4194304 | tf_op jit(solution)/shard_map/pallas_call | solution.py:326
  41.5 5.2 %all-to-all-start = ((bf16[4,128,2048]{2,1,0:T(8,128)(2,1)}), bf16[4,128,2048]{2,1,0:T(8,128)(2,1)S(1)}, u32[]{:S(2)}, u32[]{:S(2)}) async-start(bf16[4,128,2048]{2,1,0:T(8,128)(2,1)} %shard_map.241.refs_1_), calls=%async_computation | async-start | bytes 4194304 | tf_op jit(solution)/shard_map/all_to_all | solution.py:582
  54.0 5.5 %collective-permute-done.5.refs_2_ = bf16[256,512]{1,0:T(8,128)(2,1)S(1)} collective-permute-done((bf16[256,512]{1,0:T(8,128)(2,1)S(1)}, bf16[256,512]{1,0:T(8,128)(2,1)S(1)}, u32[]{:S(2)}, u32[]{:S(2)}) %collective-permute-start.5) | collective-permute-done | bytes 262176 | tf_op jit(solution)/shard_map/ppermute | solution.py:236
  59.6 5.7 %collective-permute-done.4.refs_1_ = bf16[256,512]{1,0:T(8,128)(2,1)S(1)} collective-permute-done((bf16[256,512]{1,0:T(8,128)(2,1)S(1)}, bf16[256,512]{1,0:T(8,128)(2,1)S(1)}, u32[]{:S(2)}, u32[]{:S(2)}) %collective-permute-start.4) | collective-permute-done | bytes 262176 | tf_op jit(solution)/shard_map/ppermute | solution.py:236
  65.2 29.6 %all-to-all-done.refs_4_ = bf16[4,128,2048]{2,1,0:T(8,128)(2,1)S(1)} async-done(((bf16[4,128,2048]{2,1,0:T(8,128)(2,1)}), bf16[4,128,2048]{2,1,0:T(8,128)(2,1)S(1)}, u32[]{:S(2)}, u32[]{:S(2)}) %all-to-all-start) | async-done | bytes 2097184 | tf_op jit(solution)/shard_map/all_to_all | solution.py:582
  98.7 4.0 %all-to-all-start.1 = ((bf16[8,1,40,2048]{3,2,1,0:T(8,128)(2,1)}), bf16[8,1,40,2048]{3,2,1,0:T(8,128)(2,1)S(1)}, u32[]{:S(2)}, u32[]{:S(2)}) async-start(bf16[8,1,40,2048]{3,2,1,0:T(8,128)(2,1)} %get-tuple-element.6), calls=%async_computation.1 | async-start | bytes 2621440 | tf_op jit(solution)/shard_map/all_to_all | solution.py:589
  106.6 12.6 %collective-permute-done.6 = f32[2,16,128]{2,1,0:T(8,128)S(1)} collective-permute-done((f32[2,16,128]{2,1,0:T(8,128)S(1)}, f32[2,16,128]{2,1,0:T(8,128)S(1)}, u32[]{:S(2)}, u32[]{:S(2)}) %collective-permute-start.6) | collective-permute-done | bytes 16416 | tf_op jit(solution)/shard_map/ppermute | solution.py:567
  125.9 9.3 %collective-permute-start.9 = (bf16[128,2048]{1,0:T(8,128)(2,1)}, bf16[128,2048]{1,0:T(8,128)(2,1)S(1)}, u32[]{:S(2)}, u32[]{:S(2)}) collective-permute-start(bf16[128,2048]{1,0:T(8,128)(2,1)} %copy-done.18), channel_id=1, source_target_pairs={{0,4},{2,6},{4,0},{6,2},{1,5},{3,7},{5,1},{7,3},{8,12},{10,14},{12... | collective-permute-start | bytes 1572872 | tf_op jit(solution)/shard_map/ppermute | solution.py:606
  135.3 24.7 %collective-permute-done.8 = f32[2,16,128]{2,1,0:T(8,128)S(1)} collective-permute-done((f32[2,16,128]{2,1,0:T(8,128)S(1)}, f32[2,16,128]{2,1,0:T(8,128)S(1)}, u32[]{:S(2)}, u32[]{:S(2)}) %collective-permute-start.8) | collective-permute-done | bytes 16416 | tf_op jit(solution)/shard_map/ppermute | solution.py:567
  162.7 4.6 %all-to-all-start.4 = ((bf16[8,1,40,2048]{3,2,1,0:T(8,128)(2,1)}), bf16[8,1,40,2048]{3,2,1,0:T(8,128)(2,1)}, u32[]{:S(2)}, u32[]{:S(2)}) async-start(bf16[8,1,40,2048]{3,2,1,0:T(8,128)(2,1)} %shard_map.245.refs_0_), calls=%async_computation.4 | async-start | bytes 2621440 | tf_op jit(solution)/shard_map/all_to_all | solution.py:589
  172.3 14.4 %shard_map.246.after_ref = bf16[8,2,40,2048]{3,2,1,0:T(8,128)(2,1)} custom-call(bf16[8,1,40,2048]{3,2,1,0:T(8,128)(2,1)} %shard_map.245.refs_0_, bf16[8,1,40,2048]{3,2,1,0:T(8,128)(2,1)} %copy-done.3, bf16[320,320]{1,0:T(8,128)(2,1)} %constant.134.clone.refs_2_.refs_3_, bf16[320,320]{1,0:T(8,128)(2,1)} %constant.135.clone.refs_3_.refs_4_, ...), custom_call_target="tpu_custom_call" | custom-call | flops 4865392640 | bytes 27787264 | tf_op jit(solution)/shard_map/pallas_call | solution.py:482
  190.3 3.8 %all-to-all-start.3 = ((bf16[8,2,40,2048]{3,2,1,0:T(8,128)(2,1)}), bf16[8,2,40,2048]{3,2,1,0:T(8,128)(2,1)S(1)}, u32[]{:S(2)}, u32[]{:S(2)}) async-start(bf16[8,2,40,2048]{3,2,1,0:T(8,128)(2,1)} %copy-done.1), calls=%async_computation.3 | async-start | bytes 5242880 | tf_op jit(solution)/shard_map/all_to_all | solution.py:589
  194.3 14.4 %shard_map.248.refs_0_ = bf16[8,1,40,2048]{3,2,1,0:T(8,128)(2,1)} custom-call(bf16[8,2,40,2048]{3,2,1,0:T(8,128)(2,1)} %copy-done.1, bf16[8,1,40,2048]{3,2,1,0:T(8,128)(2,1)} %all-to-all-done.4.refs_1_, bf16[320,320]{1,0:T(8,128)(2,1)} %constant.134.clone.refs_2_.refs_3_, bf16[320,320]{1,0:T(8,128)(2,1)} %constant.135.clone.refs_3_.refs_4_, ...), custom_call_target="tpu_custom_call" | custom-call | flops 4865392640 | bytes 27787264 | tf_op jit(solution)/shard_map/pallas_call | solution.py:482
  208.8 17.2 %all-to-all-done.3.refs_2_ = bf16[8,2,40,2048]{3,2,1,0:T(8,128)(2,1)S(1)} async-done(((bf16[8,2,40,2048]{3,2,1,0:T(8,128)(2,1)}), bf16[8,2,40,2048]{3,2,1,0:T(8,128)(2,1)S(1)}, u32[]{:S(2)}, u32[]{:S(2)}) %all-to-all-start.3) | async-done | bytes 2621472 | tf_op jit(solution)/shard_map/all_to_all | solution.py:589
  235.8 13.7 %shard_map.250 = bf16[8,1,40,2048]{3,2,1,0:T(8,128)(2,1)} custom-call(bf16[8,1,40,2048]{3,2,1,0:T(8,128)(2,1)} %shard_map.248.refs_0_, bf16[128,2048]{1,0:T(8,128)(2,1)} %fusion.2.refs_1_, bf16[8,2,40,2048]{3,2,1,0:T(8,128)(2,1)} %copy-done.25, bf16[320,320]{1,0:T(8,128)(2,1)} %constant.134.clone.refs_2_.refs_3_, ...), custom_call_target="tpu_custom_call" | custom-call | flops 4865392640 | bytes 27787264 | tf_op jit(solution)/shard_map/pallas_call | solution.py:482
  249.5 4.1 %all-to-all-start.6 = ((bf16[8,1,40,2048]{3,2,1,0:T(8,128)(2,1)}), bf16[8,1,40,2048]{3,2,1,0:T(8,128)(2,1)S(1)}, u32[]{:S(2)}, u32[]{:S(2)}) async-start(bf16[8,1,40,2048]{3,2,1,0:T(8,128)(2,1)} %shard_map.250), calls=%async_computation.6 | async-start | bytes 2621440 | tf_op jit(solution)/shard_map/all_to_all | solution.py:589
  257.1 14.4 %shard_map.252 = bf16[8,1,40,2048]{3,2,1,0:T(8,128)(2,1)} custom-call(bf16[128,2048]{1,0:T(8,128)(2,1)} %fusion.3.refs_0_, bf16[8,1,40,2048]{3,2,1,0:T(8,128)(2,1)} %copy-done.2, bf16[320,320]{1,0:T(8,128)(2,1)} %constant.134.clone.refs_2_.refs_3_, bf16[320,320]{1,0:T(8,128)(2,1)} %constant.135.clone.refs_3_.refs_4_, bf16[4,2048,512]{2,1,0:T(8,128)(2,1)} %refs_4_.6, ...), custom_call_target="tpu_custom_call" | custom-call | flops 4865392640 | bytes 27787264 | tf_op jit(solution)/shard_map/pallas_call | solution.py:482
  271.5 4.2 %all-to-all-start.7 = ((bf16[8,1,40,2048]{3,2,1,0:T(8,128)(2,1)}), bf16[8,1,40,2048]{3,2,1,0:T(8,128)(2,1)S(1)}, u32[]{:S(2)}, u32[]{:S(2)}) async-start(bf16[8,1,40,2048]{3,2,1,0:T(8,128)(2,1)} %shard_map.252), calls=%async_computation.7 | async-start | bytes 2621440 | tf_op jit(solution)/shard_map/all_to_all | solution.py:589
  275.7 8.1 %collective-permute-start.13 = (bf16[128,2048]{1,0:T(8,128)(2,1)}, bf16[128,2048]{1,0:T(8,128)(2,1)}, u32[]{:S(2)}, u32[]{:S(2)}) collective-permute-start(bf16[128,2048]{1,0:T(8,128)(2,1)} %fusion.3.refs_0_), channel_id=1, source_target_pairs={{0,4},{2,6},{4,0},{6,2},{1,5},{3,7},{5,1},{7,3},{8,12},{10,14},{12... | collective-permute-start | bytes 1572872 | tf_op jit(solution)/shard_map/ppermute | solution.py:606
  291.7 16.1 %collective-permute-done.13.refs_1_ = bf16[128,2048]{1,0:T(8,128)(2,1)} collective-permute-done((bf16[128,2048]{1,0:T(8,128)(2,1)}, bf16[128,2048]{1,0:T(8,128)(2,1)}, u32[]{:S(2)}, u32[]{:S(2)}) %collective-permute-start.13) | collective-permute-done | bytes 524320 | tf_op jit(solution)/shard_map/ppermute | solution.py:606
  311.7 12.4 %collective-permute-done.14 = bf16[128,2048]{1,0:T(8,128)(2,1)S(1)} collective-permute-done((bf16[128,2048]{1,0:T(8,128)(2,1)S(1)}, bf16[128,2048]{1,0:T(8,128)(2,1)S(1)}, u32[]{:S(2)}, u32[]{:S(2)}) %collective-permute-start.14) | collective-permute-done | bytes 524320 | tf_op jit(solution)/shard_map/ppermute | solution.py:606
  (161 shorter events, 72.9 us)
Async XLA Ops:
  1.7 14.9 %collective-permute-start = (bf16[256,1024]{1,0:T(8,128)(2,1)S(1)}, bf16[256,1024]{1,0:T(8,128)(2,1)S(1)}, u32[]{:S(2)}, u32[]{:S(2)}) collective-permute-start(bf16[256,1024]{1,0:T(8,128)(2,1)S(1)} %constant_dynamic-slice_fusion), channel_id=1, source_target_pairs={{0,1},{1,0},{2,3},{3,2},{4,5},{5,4},{6,7},{7,6},{8,9},{9,8},{10,11... | collective-permute-start | bytes 1572872 | tf_op jit(solution)/shard_map/ppermute | solution.py:547
  16.7 19.4 %collective-permute-start.2 = (bf16[256,1024]{1,0:T(8,128)(2,1)S(1)}, bf16[256,1024]{1,0:T(8,128)(2,1)S(1)}, u32[]{:S(2)}, u32[]{:S(2)}) collective-permute-start(bf16[256,1024]{1,0:T(8,128)(2,1)S(1)} %collective-permute-done.refs_1_.first_ref), channel_id=1, source_target_pairs={{0,8},{8,0},{16,24},{24,16},{1,9},{9,1},{17,25},{25,17},{2,10},{10... | collective-permute-start | bytes 1572872 | tf_op jit(solution)/shard_map/ppermute | solution.py:548
  27.1 8.9 %collective-permute-start.1 = (bf16[512,256]{1,0:T(8,128)(2,1)}, bf16[512,256]{1,0:T(8,128)(2,1)S(1)}, u32[]{:S(2)}, u32[]{:S(2)}) collective-permute-start(bf16[512,256]{1,0:T(8,128)(2,1)} %shard_map.240), channel_id=1, source_target_pairs={{0,1},{1,0},{2,3},{3,2},{4,5},{5,4},{6,7},{7,6},{8,9},{9,8},{10,11... | collective-permute-start | bytes 786440 | tf_op jit(solution)/shard_map/ppermute | solution.py:551
  41.5 53.3 %all-to-all-start = ((bf16[4,128,2048]{2,1,0:T(8,128)(2,1)}), bf16[4,128,2048]{2,1,0:T(8,128)(2,1)S(1)}, u32[]{:S(2)}, u32[]{:S(2)}) async-start(bf16[4,128,2048]{2,1,0:T(8,128)(2,1)} %shard_map.241.refs_1_), calls=%async_computation | async-start | bytes 4194304 | tf_op jit(solution)/shard_map/all_to_all | solution.py:582
  50.2 44.6 %copy-start.10 = (bf16[128,2048]{1,0:T(8,128)(2,1)S(1)}, bf16[128,2048]{1,0:T(8,128)(2,1)}, u32[]{:S(2)}) copy-start(bf16[128,2048]{1,0:T(8,128)(2,1)} %refs_3_.5) | copy-start | bytes 1572868
  51.0 8.5 %collective-permute-start.5 = (bf16[256,512]{1,0:T(8,128)(2,1)S(1)}, bf16[256,512]{1,0:T(8,128)(2,1)S(1)}, u32[]{:S(2)}, u32[]{:S(2)}) collective-permute-start(bf16[256,512]{1,0:T(8,128)(2,1)S(1)} %get-tuple-element.17), channel_id=1, source_target_pairs={{0,24},{8,16},{16,8},{24,0},{1,25},{9,17},{17,9},{25,1},{2,26},{10... | collective-permute-start | bytes 786440 | tf_op jit(solution)/shard_map/ppermute | solution.py:236
  51.5 13.7 %collective-permute-start.4 = (bf16[256,512]{1,0:T(8,128)(2,1)S(1)}, bf16[256,512]{1,0:T(8,128)(2,1)S(1)}, u32[]{:S(2)}, u32[]{:S(2)}) collective-permute-start(bf16[256,512]{1,0:T(8,128)(2,1)S(1)} %get-tuple-element.18), channel_id=1, source_target_pairs={{0,16},{8,24},{16,0},{24,8},{1,17},{9,25},{17,1},{25,9},{2,18},{10... | collective-permute-start | bytes 786440 | tf_op jit(solution)/shard_map/ppermute | solution.py:236
  52.6 12.7 %collective-permute-start.3 = (bf16[256,512]{1,0:T(8,128)(2,1)S(1)}, bf16[256,512]{1,0:T(8,128)(2,1)S(1)}, u32[]{:S(2)}, u32[]{:S(2)}) collective-permute-start(bf16[256,512]{1,0:T(8,128)(2,1)S(1)} %get-tuple-element.19), channel_id=1, source_target_pairs={{0,8},{8,0},{16,24},{24,16},{1,9},{9,1},{17,25},{25,17},{2,10},{10... | collective-permute-start | bytes 786440 | tf_op jit(solution)/shard_map/ppermute | solution.py:236
  98.7 21.7 %all-to-all-start.1 = ((bf16[8,1,40,2048]{3,2,1,0:T(8,128)(2,1)}), bf16[8,1,40,2048]{3,2,1,0:T(8,128)(2,1)S(1)}, u32[]{:S(2)}, u32[]{:S(2)}) async-start(bf16[8,1,40,2048]{3,2,1,0:T(8,128)(2,1)} %get-tuple-element.6), calls=%async_computation.1 | async-start | bytes 2621440 | tf_op jit(solution)/shard_map/all_to_all | solution.py:589
  102.7 17.7 %collective-permute-start.7 = (bf16[128,2048]{1,0:T(8,128)(2,1)S(1)}, bf16[128,2048]{1,0:T(8,128)(2,1)S(1)}, u32[]{:S(2)}, u32[]{:S(2)}) collective-permute-start(bf16[128,2048]{1,0:T(8,128)(2,1)S(1)} %copy-done.19), channel_id=1, source_target_pairs={{0,6},{2,4},{4,2},{6,0},{1,7},{3,5},{5,3},{7,1},{8,14},{10,12},{12... | collective-permute-start | bytes 1572872 | tf_op jit(solution)/shard_map/ppermute | solution.py:606
  104.2 15.1 %collective-permute-start.6 = (f32[2,16,128]{2,1,0:T(8,128)S(1)}, f32[2,16,128]{2,1,0:T(8,128)S(1)}, u32[]{:S(2)}, u32[]{:S(2)}) collective-permute-start(f32[2,16,128]{2,1,0:T(8,128)S(1)} %get-tuple-element.22), channel_id=1, source_target_pairs={{0,6},{2,4},{4,2},{6,0},{1,7},{3,5},{5,3},{7,1},{8,14},{10,12},{12... | collective-permute-start | bytes 49160 | tf_op jit(solution)/shard_map/ppermute | solution.py:567
  122.0 39.1 %all-to-all-start.2 = ((bf16[8,1,40,2048]{3,2,1,0:T(8,128)(2,1)}), bf16[8,1,40,2048]{3,2,1,0:T(8,128)(2,1)S(1)}, u32[]{:S(2)}, u32[]{:S(2)}) async-start(bf16[8,1,40,2048]{3,2,1,0:T(8,128)(2,1)} %copy-done.4), calls=%async_computation.2 | async-start | bytes 2621440 | tf_op jit(solution)/shard_map/all_to_all | solution.py:589
  125.9 35.2 %collective-permute-start.9 = (bf16[128,2048]{1,0:T(8,128)(2,1)}, bf16[128,2048]{1,0:T(8,128)(2,1)S(1)}, u32[]{:S(2)}, u32[]{:S(2)}) collective-permute-start(bf16[128,2048]{1,0:T(8,128)(2,1)} %copy-done.18), channel_id=1, source_target_pairs={{0,4},{2,6},{4,0},{6,2},{1,5},{3,7},{5,1},{7,3},{8,12},{10,14},{12... | collective-permute-start | bytes 1572872 | tf_op jit(solution)/shard_map/ppermute | solution.py:606
  135.2 24.7 %collective-permute-start.8 = (f32[2,16,128]{2,1,0:T(8,128)S(1)}, f32[2,16,128]{2,1,0:T(8,128)S(1)}, u32[]{:S(2)}, u32[]{:S(2)}) collective-permute-start(f32[2,16,128]{2,1,0:T(8,128)S(1)} %get-tuple-element.21), channel_id=1, source_target_pairs={{0,4},{2,6},{4,0},{6,2},{1,5},{3,7},{5,1},{7,3},{8,12},{10,14},{12... | collective-permute-start | bytes 49160 | tf_op jit(solution)/shard_map/ppermute | solution.py:567
  162.7 27.6 %all-to-all-start.4 = ((bf16[8,1,40,2048]{3,2,1,0:T(8,128)(2,1)}), bf16[8,1,40,2048]{3,2,1,0:T(8,128)(2,1)}, u32[]{:S(2)}, u32[]{:S(2)}) async-start(bf16[8,1,40,2048]{3,2,1,0:T(8,128)(2,1)} %shard_map.245.refs_0_), calls=%async_computation.4 | async-start | bytes 2621440 | tf_op jit(solution)/shard_map/all_to_all | solution.py:589
  167.3 3.8 %collective-permute-start.10 = (f32[2,16,128]{2,1,0:T(8,128)S(1)}, f32[2,16,128]{2,1,0:T(8,128)S(1)}, u32[]{:S(2)}, u32[]{:S(2)}) collective-permute-start(f32[2,16,128]{2,1,0:T(8,128)S(1)} %get-tuple-element.20), channel_id=1, source_target_pairs={{0,2},{2,0},{4,6},{6,4},{1,3},{3,1},{5,7},{7,5},{8,10},{10,8},{12,... | collective-permute-start | bytes 49160 | tf_op jit(solution)/shard_map/ppermute | solution.py:567
  171.1 15.5 %collective-permute-start.11 = (bf16[128,2048]{1,0:T(8,128)(2,1)S(1)}, bf16[128,2048]{1,0:T(8,128)(2,1)S(1)}, u32[]{:S(2)}, u32[]{:S(2)}) collective-permute-start(bf16[128,2048]{1,0:T(8,128)(2,1)S(1)} %copy-done.20), channel_id=1, source_target_pairs={{0,2},{2,0},{4,6},{6,4},{1,3},{3,1},{5,7},{7,5},{8,10},{10,8},{12,... | collective-permute-start | bytes 1572872 | tf_op jit(solution)/shard_map/ppermute | solution.py:606
  190.3 35.6 %all-to-all-start.3 = ((bf16[8,2,40,2048]{3,2,1,0:T(8,128)(2,1)}), bf16[8,2,40,2048]{3,2,1,0:T(8,128)(2,1)S(1)}, u32[]{:S(2)}, u32[]{:S(2)}) async-start(bf16[8,2,40,2048]{3,2,1,0:T(8,128)(2,1)} %copy-done.1), calls=%async_computation.3 | async-start | bytes 5242880 | tf_op jit(solution)/shard_map/all_to_all | solution.py:589
  227.4 22.1 %all-to-all-start.5 = ((bf16[8,1,40,2048]{3,2,1,0:T(8,128)(2,1)}), bf16[8,1,40,2048]{3,2,1,0:T(8,128)(2,1)S(1)}, u32[]{:S(2)}, u32[]{:S(2)}) async-start(bf16[8,1,40,2048]{3,2,1,0:T(8,128)(2,1)} %shard_map.248.refs_0_), calls=%async_computation.5 | async-start | bytes 2621440 | tf_op jit(solution)/shard_map/all_to_all | solution.py:589
  234.3 19.4 %collective-permute-start.12 = (bf16[128,2048]{1,0:T(8,128)(2,1)}, bf16[128,2048]{1,0:T(8,128)(2,1)}, u32[]{:S(2)}, u32[]{:S(2)}) collective-permute-start(bf16[128,2048]{1,0:T(8,128)(2,1)} %fusion.2.refs_1_), channel_id=1, source_target_pairs={{0,6},{2,4},{4,2},{6,0},{1,7},{3,5},{5,3},{7,1},{8,14},{10,12},{12... | collective-permute-start | bytes 1572872 | tf_op jit(solution)/shard_map/ppermute | solution.py:606
  249.5 22.0 %all-to-all-start.6 = ((bf16[8,1,40,2048]{3,2,1,0:T(8,128)(2,1)}), bf16[8,1,40,2048]{3,2,1,0:T(8,128)(2,1)S(1)}, u32[]{:S(2)}, u32[]{:S(2)}) async-start(bf16[8,1,40,2048]{3,2,1,0:T(8,128)(2,1)} %shard_map.250), calls=%async_computation.6 | async-start | bytes 2621440 | tf_op jit(solution)/shard_map/all_to_all | solution.py:589
  271.5 38.8 %all-to-all-start.7 = ((bf16[8,1,40,2048]{3,2,1,0:T(8,128)(2,1)}), bf16[8,1,40,2048]{3,2,1,0:T(8,128)(2,1)S(1)}, u32[]{:S(2)}, u32[]{:S(2)}) async-start(bf16[8,1,40,2048]{3,2,1,0:T(8,128)(2,1)} %shard_map.252), calls=%async_computation.7 | async-start | bytes 2621440 | tf_op jit(solution)/shard_map/all_to_all | solution.py:589
  275.7 32.1 %collective-permute-start.13 = (bf16[128,2048]{1,0:T(8,128)(2,1)}, bf16[128,2048]{1,0:T(8,128)(2,1)}, u32[]{:S(2)}, u32[]{:S(2)}) collective-permute-start(bf16[128,2048]{1,0:T(8,128)(2,1)} %fusion.3.refs_0_), channel_id=1, source_target_pairs={{0,4},{2,6},{4,0},{6,2},{1,5},{3,7},{5,1},{7,3},{8,12},{10,14},{12... | collective-permute-start | bytes 1572872 | tf_op jit(solution)/shard_map/ppermute | solution.py:606
  310.3 13.8 %collective-permute-start.14 = (bf16[128,2048]{1,0:T(8,128)(2,1)S(1)}, bf16[128,2048]{1,0:T(8,128)(2,1)S(1)}, u32[]{:S(2)}, u32[]{:S(2)}) collective-permute-start(bf16[128,2048]{1,0:T(8,128)(2,1)S(1)} %fusion.4), channel_id=1, source_target_pairs={{0,2},{2,0},{4,6},{6,4},{1,3},{3,1},{5,7},{7,5},{8,10},{10,8},{12,... | collective-permute-start | bytes 1572872 | tf_op jit(solution)/shard_map/ppermute | solution.py:606
  (36 other events, 196.4 us)

commit v4 on v3

--- a/solution.py
+++ b/solution.py
@@ -545,11 +545,22 @@
     cores = [(low, low ^ 1) for low in range(groups)]
     half = lax.dynamic_slice_in_dim(out_weight, core * (D // 2), D // 2, 1)
     other_weight = lax.ppermute(half, "x", swap)
-    other_rest = lax.ppermute(other_weight, "req", cores)
     attended = attend_columns(queries, keys, values, segment_ids[0], tok_rows)
     leaving = lax.dynamic_index_in_dim(attended, 1 - column, 0, keepdims=False)
-    other = lax.ppermute(tie(leaving, other_weight), "x", swap)
-
+    other = lax.ppermute(leaving, "x", swap)
+    other_weight = tie(other_weight, attended)
+    other_rest = lax.ppermute(other_weight, "req", cores)
+
+    partial = partial_products(
+        jnp.stack([column, core]).astype(jnp.int32),
+        attended,
+        other,
+        out_weight,
+        other_weight,
+        other_rest,
+    )
+
+    routes = tie(routes, partial)
     matched = routes[:, :, None] == jnp.arange(EXPERTS, dtype=jnp.int32)[None, None, :]
     named = jnp.any(matched, axis=1)
     weight_of = jnp.sum(jnp.where(matched, combine[:, :, None], 0.0), axis=1)
@@ -571,14 +582,6 @@
         high = mixing.astype(jnp.bfloat16)
         mixings.append((high, (mixing - high.astype(jnp.float32)).astype(jnp.bfloat16)))
 
-    partial = partial_products(
-        jnp.stack([column, core]).astype(jnp.int32),
-        attended,
-        other,
-        out_weight,
-        other_weight,
-        other_rest,
-    )
     gathered = lax.all_to_all(partial, "z", split_axis=0, concat_axis=0, tiled=True)
     pages, place_pages = move_pages(keys, values, page_table, partial)
     normed, residual, packed = norm_and_pack(
@@ -607,27 +610,27 @@
 
     blocks = [normed] + [to_plane(turn, normed) for turn in range(1, PLANES)]
     own = exchange(packed)
-    packed_third = pack_after(own, pickings[3], blocks[3], sources)
+    packed_first = pack_after(own, pickings[1], blocks[1], sources)
+    first = exchange(packed_first)
+    outs_own = experts([packed_first], own)
+    packed_third = pack_after(first, pickings[3], blocks[3], sources)
     third = exchange(packed_third)
-    packed_second = pack_after(third, pickings[2], blocks[2], sources)
-    second = exchange(packed_second)
-    outs_third = experts([packed_second], third, 2)
-    outs_third = pack_after(outs_third, pickings[1], blocks[1], sources, into=True)
-    first = exchange(outs_third)
-    outs_second = experts([outs_third], second)
+    outs_first = experts([outs_own, packed_third], first, 2)
+    outs_first = pack_after(outs_first, pickings[2], blocks[2], sources, into=True)
+    second = exchange(outs_first)
+    outs_third = experts([outs_first], third)
+    back_third = exchange(outs_third)
+    share_first = mixed(1, second).astype(jnp.bfloat16)
+    outs_second = experts([outs_third, share_first], second)
+    got_first = to_plane(1, share_first)
     back_second = exchange(outs_second)
-    share_third = mixed(3, first).astype(jnp.bfloat16)
-    outs_first = experts([outs_second, share_third], first)
+    share_third = mixed(3, tie(back_third, got_first)).astype(jnp.bfloat16)
     got_third = to_plane(3, share_third)
-    back_first = exchange(outs_first)
+    back_own = exchange(tie(outs_own, back_second))
     share_second = mixed(2, tie(back_second, got_third)).astype(jnp.bfloat16)
-    outs_own = experts([share_second], own)
     got_second = to_plane(2, share_second)
-    back_own = exchange(outs_own)
-    share_first = mixed(1, tie(back_first, got_second)).astype(jnp.bfloat16)
-    total = residual + got_third.astype(jnp.float32) + got_second.astype(jnp.float32)
-    total = total + to_plane(1, share_first).astype(jnp.float32)
-    total = total + mixed(0, back_own)
+    total = residual + got_first.astype(jnp.float32) + got_third.astype(jnp.float32)
+    total = total + mixed(0, back_own) + got_second.astype(jnp.float32)
     return (total.astype(jnp.bfloat16), place_pages())
 
 

time: 328 us -> 328 us (level)
  waiting for transfers between devices: 147 us -> 139 us
    ppermute x6, waiting for transfers between devices: 28.5 us -> 45.6 us  [to_plane(): return lax.ppermute(block, 'z', pairs[turn])]
    ppermute x3, waiting for transfers between devices: 41 us -> 26.6 us  [on_device_whole(): table = lax.ppermute(table, 'z', pairs[turn])]
    ppermute x1, waiting for transfers between devices: 11.9 us -> 1.4 us  [on_device_whole(): other_weight = lax.ppermute(half, 'x', swap)]
    unnamed x74 -> x79, local copies, waits for them, and re-layouts: 12.9 us -> 16.3 us
  transfers between devices with their start and end apart: 23 -> 23, of which waited for: 11 -> 14; matrix products, arithmetic and copies ran while one was open for 9% -> 9% of each run, Pallas kernels for 19% -> 20%
where the time goes in v4:
time: 328 us; the launch traced here: 326 us
  waiting for transfers between devices  139 us (42%)
  Pallas kernels  72.1 us (22%)
  starting transfers between devices  64.8 us (20%)
  local copies, waits for them, and re-layouts  25.8 us (8%)
  matrix products  16.1 us (5%)
  other arithmetic  7.94 us (2%)
    pallas_call x4, Pallas kernels, run_experts(): pl.pallas_call(expert_kernel, grid=(4,), in_specs=[pl.BlockSpec(memory_sp...  56.9 us
    ppermute x6, waiting for transfers between devices, to_plane(): return lax.ppermute(block, 'z', pairs[turn])  45.6 us
    all_to_all x1, waiting for transfers between devices, on_device_whole(): lax.all_to_all(partial, 'z', split_axis=0, concat_axis=0, tiled=True)  29 us
    all_to_all x7, starting transfers between devices, exchange(): lax.all_to_all(block, ('req', 'x'), split_axis=0, concat_axis=0, tiled=True)  27 us
    ppermute x3, waiting for transfers between devices, on_device_whole(): table = lax.ppermute(table, 'z', pairs[turn])  26.6 us
    ppermute x6, starting transfers between devices, to_plane(): return lax.ppermute(block, 'z', pairs[turn])  21.4 us
    all_to_all x7, waiting for transfers between devices, exchange(): lax.all_to_all(block, ('req', 'x'), split_axis=0, concat_axis=0, tiled=True)  19.9 us
    unnamed x79, local copies, waits for them, and re-layouts  16.3 us
  transfers between devices with their start and end apart: 23, of which 14 were waited for; matrix products, arithmetic and copies ran while one was open for 9% of the time, Pallas kernels for 20%

profile of v4, /device:TPU:0, one launch (start us, length us, event | category | flops | bytes accessed | tf_op | source)
XLA Modules:
  0.0 326.3 jit_solution(3128675407755666722)
XLA Ops:
  9.5 5.0 %shard_map.239.refs_1_.mine_ref = bf16[2,512,256]{2,1,0:T(8,128)(2,1)S(1)} custom-call(bf16[1024,256]{1,0:T(8,128)(2,1)S(1)} %copy-done.14, bf16[1024,256]{1,0:T(8,128)(2,1)S(1)} %copy-done.15, bf16[1024,256]{1,0:T(8,128)(2,1)S(1)} %copy-done.17, s32[1024,1]{1,0:T(8,128)S(1)} %copy.46.line_ref, s32[1,1024]{1,0:T(1,128)S(1)} %copy-done.13), custom_call_target="tpu_custom_call" | custom-call | flops 1073741824 | bytes 2097152 | tf_op jit(solution)/shard_map/pallas_call | solution.py:286
  20.4 6.8 %collective-permute-done.other_ref = bf16[512,256]{1,0:T(8,128)(2,1)S(1)} collective-permute-done((bf16[512,256]{1,0:T(8,128)(2,1)S(1)}, bf16[512,256]{1,0:T(8,128)(2,1)S(1)}, u32[]{:S(2)}, u32[]{:S(2)}) %collective-permute-start) | collective-permute-done | bytes 262176 | tf_op jit(solution)/shard_map/ppermute | solution.py:550
  28.3 4.4 %shard_map.241.refs_1_ = bf16[4,128,2048]{2,1,0:T(8,128)(2,1)} custom-call(s32[2]{0:T(128)S(1)} %pad_add_fusion.place_ref, bf16[2,512,256]{2,1,0:T(8,128)(2,1)S(1)} %copy-done.5, bf16[512,256]{1,0:T(8,128)(2,1)S(1)} %collective-permute-done.other_ref, bf16[256,2048]{1,0:T(8,128)(2,1)S(1)} %copy-done.6, bf16[256,1024]{1,0:T(8,128)(2,1)S(1)} %copy-done.8, ...), custom_call_target="tpu_custom_call" | custom-call | flops 1073741824 | bytes 4194304 | tf_op jit(solution)/shard_map/pallas_call | solution.py:326
  32.7 5.3 %all-to-all-start = ((bf16[4,128,2048]{2,1,0:T(8,128)(2,1)}), bf16[4,128,2048]{2,1,0:T(8,128)(2,1)S(1)}, u32[]{:S(2)}, u32[]{:S(2)}) async-start(bf16[4,128,2048]{2,1,0:T(8,128)(2,1)} %shard_map.241.refs_1_), calls=%async_computation | async-start | bytes 4194304 | tf_op jit(solution)/shard_map/all_to_all | solution.py:585
  47.6 4.5 %collective-permute-done.4.refs_1_ = bf16[256,512]{1,0:T(8,128)(2,1)S(1)} collective-permute-done((bf16[256,512]{1,0:T(8,128)(2,1)}, bf16[256,512]{1,0:T(8,128)(2,1)S(1)}, u32[]{:S(2)}, u32[]{:S(2)}) %collective-permute-start.4) | collective-permute-done | bytes 262176 | tf_op jit(solution)/shard_map/ppermute | solution.py:236
  52.1 4.8 %collective-permute-done.5.refs_2_ = bf16[256,512]{1,0:T(8,128)(2,1)S(1)} collective-permute-done((bf16[256,512]{1,0:T(8,128)(2,1)}, bf16[256,512]{1,0:T(8,128)(2,1)S(1)}, u32[]{:S(2)}, u32[]{:S(2)}) %collective-permute-start.5) | collective-permute-done | bytes 262176 | tf_op jit(solution)/shard_map/ppermute | solution.py:236
  57.0 29.0 %all-to-all-done.refs_4_ = bf16[4,128,2048]{2,1,0:T(8,128)(2,1)S(1)} async-done(((bf16[4,128,2048]{2,1,0:T(8,128)(2,1)}), bf16[4,128,2048]{2,1,0:T(8,128)(2,1)S(1)}, u32[]{:S(2)}, u32[]{:S(2)}) %all-to-all-start) | async-done | bytes 2097184 | tf_op jit(solution)/shard_map/all_to_all | solution.py:585
  89.9 3.9 %all-to-all-start.1 = ((bf16[8,1,40,2048]{3,2,1,0:T(8,128)(2,1)}), bf16[8,1,40,2048]{3,2,1,0:T(8,128)(2,1)S(1)}, u32[]{:S(2)}, u32[]{:S(2)}) async-start(bf16[8,1,40,2048]{3,2,1,0:T(8,128)(2,1)} %get-tuple-element.6), calls=%async_computation.1 | async-start | bytes 2621440 | tf_op jit(solution)/shard_map/all_to_all | solution.py:592
  95.9 12.5 %collective-permute-done.6 = f32[2,16,128]{2,1,0:T(8,128)S(1)} collective-permute-done((f32[2,16,128]{2,1,0:T(8,128)S(1)}, f32[2,16,128]{2,1,0:T(8,128)S(1)}, u32[]{:S(2)}, u32[]{:S(2)}) %collective-permute-start.6) | collective-permute-done | bytes 16416 | tf_op jit(solution)/shard_map/ppermute | solution.py:578
  113.1 3.6 %all-to-all-start.2 = ((bf16[8,1,40,2048]{3,2,1,0:T(8,128)(2,1)}), bf16[8,1,40,2048]{3,2,1,0:T(8,128)(2,1)S(1)}, u32[]{:S(2)}, u32[]{:S(2)}) async-start(bf16[8,1,40,2048]{3,2,1,0:T(8,128)(2,1)} %shard_map.245.refs_0_), calls=%async_computation.2 | async-start | bytes 2621440 | tf_op jit(solution)/shard_map/all_to_all | solution.py:592
  120.5 13.0 %collective-permute-done.8 = f32[2,16,128]{2,1,0:T(8,128)S(1)} collective-permute-done((f32[2,16,128]{2,1,0:T(8,128)S(1)}, f32[2,16,128]{2,1,0:T(8,128)S(1)}, u32[]{:S(2)}, u32[]{:S(2)}) %collective-permute-start.8) | collective-permute-done | bytes 16416 | tf_op jit(solution)/shard_map/ppermute | solution.py:578
  136.3 4.6 %all-to-all-start.4 = ((bf16[8,1,40,2048]{3,2,1,0:T(8,128)(2,1)}), bf16[8,1,40,2048]{3,2,1,0:T(8,128)(2,1)}, u32[]{:S(2)}, u32[]{:S(2)}) async-start(bf16[8,1,40,2048]{3,2,1,0:T(8,128)(2,1)} %shard_map.247.refs_1_), calls=%async_computation.4 | async-start | bytes 2621440 | tf_op jit(solution)/shard_map/all_to_all | solution.py:592
  143.1 8.7 %collective-permute-start.11 = (bf16[128,2048]{1,0:T(8,128)(2,1)S(1)}, bf16[128,2048]{1,0:T(8,128)(2,1)S(1)}, u32[]{:S(2)}, u32[]{:S(2)}) collective-permute-start(bf16[128,2048]{1,0:T(8,128)(2,1)S(1)} %copy-done.21), channel_id=1, source_target_pairs={{0,4},{2,6},{4,0},{6,2},{1,5},{3,7},{5,1},{7,3},{8,12},{10,14},{12... | collective-permute-start | bytes 1572872 | tf_op jit(solution)/shard_map/ppermute | solution.py:609
  151.7 14.3 %shard_map.246.refs_0_ = bf16[8,1,40,2048]{3,2,1,0:T(8,128)(2,1)} custom-call(bf16[8,1,40,2048]{3,2,1,0:T(8,128)(2,1)} %shard_map.245.refs_0_, bf16[8,1,40,2048]{3,2,1,0:T(8,128)(2,1)} %copy-done.2, bf16[320,320]{1,0:T(8,128)(2,1)} %constant.134.clone.refs_2_.refs_3_, bf16[320,320]{1,0:T(8,128)(2,1)} %constant.135.clone.refs_3_.refs_4_, ...), custom_call_target="tpu_custom_call" | custom-call | flops 4865392640 | bytes 27787264 | tf_op jit(solution)/shard_map/pallas_call | solution.py:482
  166.1 14.4 %shard_map.248.after_ref = bf16[8,2,40,2048]{3,2,1,0:T(8,128)(2,1)} custom-call(bf16[8,1,40,2048]{3,2,1,0:T(8,128)(2,1)} %shard_map.246.refs_0_, bf16[8,1,40,2048]{3,2,1,0:T(8,128)(2,1)} %shard_map.247.refs_1_, bf16[8,1,40,2048]{3,2,1,0:T(8,128)(2,1)} %copy-done.3, bf16[320,320]{1,0:T(8,128)(2,1)} %constant.134.clone.refs_2_.refs_3_, ...), custom_call_target="tpu_custom_call" | custom-call | flops 4865392640 | bytes 27787264 | tf_op jit(solution)/shard_map/pallas_call | solution.py:482
  184.2 3.9 %all-to-all-start.3 = ((bf16[8,2,40,2048]{3,2,1,0:T(8,128)(2,1)}), bf16[8,2,40,2048]{3,2,1,0:T(8,128)(2,1)S(1)}, u32[]{:S(2)}, u32[]{:S(2)}) async-start(bf16[8,2,40,2048]{3,2,1,0:T(8,128)(2,1)} %copy-done.1), calls=%async_computation.3 | async-start | bytes 5242880 | tf_op jit(solution)/shard_map/all_to_all | solution.py:592
  188.1 14.4 %shard_map.250.refs_0_ = bf16[8,1,40,2048]{3,2,1,0:T(8,128)(2,1)} custom-call(bf16[8,2,40,2048]{3,2,1,0:T(8,128)(2,1)} %copy-done.1, bf16[8,1,40,2048]{3,2,1,0:T(8,128)(2,1)} %all-to-all-done.4.refs_1_, bf16[320,320]{1,0:T(8,128)(2,1)} %constant.134.clone.refs_2_.refs_3_, bf16[320,320]{1,0:T(8,128)(2,1)} %constant.135.clone.refs_3_.refs_4_, ...), custom_call_target="tpu_custom_call" | custom-call | flops 4865392640 | bytes 27787264 | tf_op jit(solution)/shard_map/pallas_call | solution.py:482
  202.5 17.4 %all-to-all-done.3.refs_2_ = bf16[8,2,40,2048]{3,2,1,0:T(8,128)(2,1)S(1)} async-done(((bf16[8,2,40,2048]{3,2,1,0:T(8,128)(2,1)}), bf16[8,2,40,2048]{3,2,1,0:T(8,128)(2,1)S(1)}, u32[]{:S(2)}, u32[]{:S(2)}) %all-to-all-start.3) | async-done | bytes 2621472 | tf_op jit(solution)/shard_map/all_to_all | solution.py:592
  228.3 13.7 %shard_map.252 = bf16[8,1,40,2048]{3,2,1,0:T(8,128)(2,1)} custom-call(bf16[8,1,40,2048]{3,2,1,0:T(8,128)(2,1)} %shard_map.250.refs_0_, bf16[128,2048]{1,0:T(8,128)(2,1)} %fusion.2.refs_1_, bf16[8,2,40,2048]{3,2,1,0:T(8,128)(2,1)} %copy-done.26, bf16[320,320]{1,0:T(8,128)(2,1)} %constant.134.clone.refs_2_.refs_3_, ...), custom_call_target="tpu_custom_call" | custom-call | flops 4865392640 | bytes 27787264 | tf_op jit(solution)/shard_map/pallas_call | solution.py:482
  246.6 14.4 %collective-permute-done.12.refs_1_ = bf16[128,2048]{1,0:T(8,128)(2,1)} collective-permute-done((bf16[128,2048]{1,0:T(8,128)(2,1)}, bf16[128,2048]{1,0:T(8,128)(2,1)}, u32[]{:S(2)}, u32[]{:S(2)}) %collective-permute-start.12) | collective-permute-done | bytes 524320 | tf_op jit(solution)/shard_map/ppermute | solution.py:609
  265.1 4.0 %all-to-all-start.7 = ((bf16[8,1,40,2048]{3,2,1,0:T(8,128)(2,1)}), bf16[8,1,40,2048]{3,2,1,0:T(8,128)(2,1)S(1)}, u32[]{:S(2)}, u32[]{:S(2)}) async-start(bf16[8,1,40,2048]{3,2,1,0:T(8,128)(2,1)} %shard_map.253), calls=%async_computation.7 | async-start | bytes 2621440 | tf_op jit(solution)/shard_map/all_to_all | solution.py:592
  279.1 9.1 %collective-permute-done.13.refs_1_ = bf16[128,2048]{1,0:T(8,128)(2,1)S(1)} collective-permute-done((bf16[128,2048]{1,0:T(8,128)(2,1)}, bf16[128,2048]{1,0:T(8,128)(2,1)S(1)}, u32[]{:S(2)}, u32[]{:S(2)}) %collective-permute-start.13) | collective-permute-done | bytes 524320 | tf_op jit(solution)/shard_map/ppermute | solution.py:609
  291.3 9.7 %collective-permute-start.14 = (bf16[128,2048]{1,0:T(8,128)(2,1)S(1)}, bf16[128,2048]{1,0:T(8,128)(2,1)S(1)}, u32[]{:S(2)}, u32[]{:S(2)}) collective-permute-start(bf16[128,2048]{1,0:T(8,128)(2,1)S(1)} %fusion.4), channel_id=1, source_target_pairs={{0,4},{2,6},{4,0},{6,2},{1,5},{3,7},{5,1},{7,3},{8,12},{10,14},{12... | collective-permute-start | bytes 1572872 | tf_op jit(solution)/shard_map/ppermute | solution.py:609
  302.0 22.1 %collective-permute-done.14 = bf16[128,2048]{1,0:T(8,128)(2,1)S(1)} collective-permute-done((bf16[128,2048]{1,0:T(8,128)(2,1)S(1)}, bf16[128,2048]{1,0:T(8,128)(2,1)S(1)}, u32[]{:S(2)}, u32[]{:S(2)}) %collective-permute-start.14) | collective-permute-done | bytes 524320 | tf_op jit(solution)/shard_map/ppermute | solution.py:609
  (169 shorter events, 81.9 us)
Async XLA Ops:
  1.7 14.9 %collective-permute-start.1 = (bf16[256,1024]{1,0:T(8,128)(2,1)S(1)}, bf16[256,1024]{1,0:T(8,128)(2,1)S(1)}, u32[]{:S(2)}, u32[]{:S(2)}) collective-permute-start(bf16[256,1024]{1,0:T(8,128)(2,1)S(1)} %constant_dynamic-slice_fusion), channel_id=1, source_target_pairs={{0,1},{1,0},{2,3},{3,2},{4,5},{5,4},{6,7},{7,6},{8,9},{9,8},{10,11... | collective-permute-start | bytes 1572872 | tf_op jit(solution)/shard_map/ppermute | solution.py:547
  17.5 9.8 %collective-permute-start.2 = (bf16[256,1024]{1,0:T(8,128)(2,1)}, bf16[256,1024]{1,0:T(8,128)(2,1)S(1)}, u32[]{:S(2)}, u32[]{:S(2)}) collective-permute-start(bf16[256,1024]{1,0:T(8,128)(2,1)} %shard_map.240.first_ref), channel_id=1, source_target_pairs={{0,8},{8,0},{16,24},{24,16},{1,9},{9,1},{17,25},{25,17},{2,10},{10... | collective-permute-start | bytes 1572872 | tf_op jit(solution)/shard_map/ppermute | solution.py:552
  18.5 8.7 %collective-permute-start = (bf16[512,256]{1,0:T(8,128)(2,1)S(1)}, bf16[512,256]{1,0:T(8,128)(2,1)S(1)}, u32[]{:S(2)}, u32[]{:S(2)}) collective-permute-start(bf16[512,256]{1,0:T(8,128)(2,1)S(1)} %dynamic-slice_bitcast_fusion), channel_id=1, source_target_pairs={{0,1},{1,0},{2,3},{3,2},{4,5},{5,4},{6,7},{7,6},{8,9},{9,8},{10,11... | collective-permute-start | bytes 786440 | tf_op jit(solution)/shard_map/ppermute | solution.py:550
  32.7 53.3 %all-to-all-start = ((bf16[4,128,2048]{2,1,0:T(8,128)(2,1)}), bf16[4,128,2048]{2,1,0:T(8,128)(2,1)S(1)}, u32[]{:S(2)}, u32[]{:S(2)}) async-start(bf16[4,128,2048]{2,1,0:T(8,128)(2,1)} %shard_map.241.refs_1_), calls=%async_computation | async-start | bytes 4194304 | tf_op jit(solution)/shard_map/all_to_all | solution.py:585
  41.8 44.1 %copy-start.11 = (bf16[128,2048]{1,0:T(8,128)(2,1)S(1)}, bf16[128,2048]{1,0:T(8,128)(2,1)}, u32[]{:S(2)}) copy-start(bf16[128,2048]{1,0:T(8,128)(2,1)} %refs_3_.5) | copy-start | bytes 1572868
  42.8 4.8 %collective-permute-start.3 = (bf16[256,512]{1,0:T(8,128)(2,1)}, bf16[256,512]{1,0:T(8,128)(2,1)S(1)}, u32[]{:S(2)}, u32[]{:S(2)}) collective-permute-start(bf16[256,512]{1,0:T(8,128)(2,1)} %get-tuple-element.19), channel_id=1, source_target_pairs={{0,8},{8,0},{16,24},{24,16},{1,9},{9,1},{17,25},{25,17},{2,10},{10... | collective-permute-start | bytes 786440 | tf_op jit(solution)/shard_map/ppermute | solution.py:236
  42.8 9.3 %collective-permute-start.4 = (bf16[256,512]{1,0:T(8,128)(2,1)}, bf16[256,512]{1,0:T(8,128)(2,1)S(1)}, u32[]{:S(2)}, u32[]{:S(2)}) collective-permute-start(bf16[256,512]{1,0:T(8,128)(2,1)} %get-tuple-element.18), channel_id=1, source_target_pairs={{0,16},{8,24},{16,0},{24,8},{1,17},{9,25},{17,1},{25,9},{2,18},{10... | collective-permute-start | bytes 786440 | tf_op jit(solution)/shard_map/ppermute | solution.py:236
  44.3 12.6 %collective-permute-start.5 = (bf16[256,512]{1,0:T(8,128)(2,1)}, bf16[256,512]{1,0:T(8,128)(2,1)S(1)}, u32[]{:S(2)}, u32[]{:S(2)}) collective-permute-start(bf16[256,512]{1,0:T(8,128)(2,1)} %get-tuple-element.17), channel_id=1, source_target_pairs={{0,24},{8,16},{16,8},{24,0},{1,25},{9,17},{17,9},{25,1},{2,26},{10... | collective-permute-start | bytes 786440 | tf_op jit(solution)/shard_map/ppermute | solution.py:236
  89.9 21.6 %all-to-all-start.1 = ((bf16[8,1,40,2048]{3,2,1,0:T(8,128)(2,1)}), bf16[8,1,40,2048]{3,2,1,0:T(8,128)(2,1)S(1)}, u32[]{:S(2)}, u32[]{:S(2)}) async-start(bf16[8,1,40,2048]{3,2,1,0:T(8,128)(2,1)} %get-tuple-element.6), calls=%async_computation.1 | async-start | bytes 2621440 | tf_op jit(solution)/shard_map/all_to_all | solution.py:592
  93.7 15.8 %collective-permute-start.7 = (bf16[128,2048]{1,0:T(8,128)(2,1)S(1)}, bf16[128,2048]{1,0:T(8,128)(2,1)S(1)}, u32[]{:S(2)}, u32[]{:S(2)}) collective-permute-start(bf16[128,2048]{1,0:T(8,128)(2,1)S(1)} %copy-done.20), channel_id=1, source_target_pairs={{0,2},{2,0},{4,6},{6,4},{1,3},{3,1},{5,7},{7,5},{8,10},{10,8},{12,... | collective-permute-start | bytes 1572872 | tf_op jit(solution)/shard_map/ppermute | solution.py:609
  93.8 14.6 %collective-permute-start.6 = (f32[2,16,128]{2,1,0:T(8,128)S(1)}, f32[2,16,128]{2,1,0:T(8,128)S(1)}, u32[]{:S(2)}, u32[]{:S(2)}) collective-permute-start(f32[2,16,128]{2,1,0:T(8,128)S(1)} %get-tuple-element.22), channel_id=1, source_target_pairs={{0,2},{2,0},{4,6},{6,4},{1,3},{3,1},{5,7},{7,5},{8,10},{10,8},{12,... | collective-permute-start | bytes 49160 | tf_op jit(solution)/shard_map/ppermute | solution.py:578
  113.1 21.6 %all-to-all-start.2 = ((bf16[8,1,40,2048]{3,2,1,0:T(8,128)(2,1)}), bf16[8,1,40,2048]{3,2,1,0:T(8,128)(2,1)S(1)}, u32[]{:S(2)}, u32[]{:S(2)}) async-start(bf16[8,1,40,2048]{3,2,1,0:T(8,128)(2,1)} %shard_map.245.refs_0_), calls=%async_computation.2 | async-start | bytes 2621440 | tf_op jit(solution)/shard_map/all_to_all | solution.py:592
  116.7 18.0 %collective-permute-start.9 = (bf16[128,2048]{1,0:T(8,128)(2,1)}, bf16[128,2048]{1,0:T(8,128)(2,1)S(1)}, u32[]{:S(2)}, u32[]{:S(2)}) collective-permute-start(bf16[128,2048]{1,0:T(8,128)(2,1)} %copy-done.19), channel_id=1, source_target_pairs={{0,6},{2,4},{4,2},{6,0},{1,7},{3,5},{5,3},{7,1},{8,14},{10,12},{12... | collective-permute-start | bytes 1572872 | tf_op jit(solution)/shard_map/ppermute | solution.py:609
  118.2 15.4 %collective-permute-start.8 = (f32[2,16,128]{2,1,0:T(8,128)S(1)}, f32[2,16,128]{2,1,0:T(8,128)S(1)}, u32[]{:S(2)}, u32[]{:S(2)}) collective-permute-start(f32[2,16,128]{2,1,0:T(8,128)S(1)} %get-tuple-element.21), channel_id=1, source_target_pairs={{0,6},{2,4},{4,2},{6,0},{1,7},{3,5},{5,3},{7,1},{8,14},{10,12},{12... | collective-permute-start | bytes 49160 | tf_op jit(solution)/shard_map/ppermute | solution.py:578
  120.5 21.4 %collective-permute-start.10 = (f32[2,16,128]{2,1,0:T(8,128)S(1)}, f32[2,16,128]{2,1,0:T(8,128)S(1)}, u32[]{:S(2)}, u32[]{:S(2)}) collective-permute-start(f32[2,16,128]{2,1,0:T(8,128)S(1)} %get-tuple-element.20), channel_id=1, source_target_pairs={{0,4},{2,6},{4,0},{6,2},{1,5},{3,7},{5,1},{7,3},{8,12},{10,14},{12... | collective-permute-start | bytes 49160 | tf_op jit(solution)/shard_map/ppermute | solution.py:578
  136.3 48.0 %all-to-all-start.4 = ((bf16[8,1,40,2048]{3,2,1,0:T(8,128)(2,1)}), bf16[8,1,40,2048]{3,2,1,0:T(8,128)(2,1)}, u32[]{:S(2)}, u32[]{:S(2)}) async-start(bf16[8,1,40,2048]{3,2,1,0:T(8,128)(2,1)} %shard_map.247.refs_1_), calls=%async_computation.4 | async-start | bytes 2621440 | tf_op jit(solution)/shard_map/all_to_all | solution.py:592
  143.1 37.5 %collective-permute-start.11 = (bf16[128,2048]{1,0:T(8,128)(2,1)S(1)}, bf16[128,2048]{1,0:T(8,128)(2,1)S(1)}, u32[]{:S(2)}, u32[]{:S(2)}) collective-permute-start(bf16[128,2048]{1,0:T(8,128)(2,1)S(1)} %copy-done.21), channel_id=1, source_target_pairs={{0,4},{2,6},{4,0},{6,2},{1,5},{3,7},{5,1},{7,3},{8,12},{10,14},{12... | collective-permute-start | bytes 1572872 | tf_op jit(solution)/shard_map/ppermute | solution.py:609
  184.2 35.7 %all-to-all-start.3 = ((bf16[8,2,40,2048]{3,2,1,0:T(8,128)(2,1)}), bf16[8,2,40,2048]{3,2,1,0:T(8,128)(2,1)S(1)}, u32[]{:S(2)}, u32[]{:S(2)}) async-start(bf16[8,2,40,2048]{3,2,1,0:T(8,128)(2,1)} %copy-done.1), calls=%async_computation.3 | async-start | bytes 5242880 | tf_op jit(solution)/shard_map/all_to_all | solution.py:592
  221.4 21.2 %all-to-all-start.5 = ((bf16[8,1,40,2048]{3,2,1,0:T(8,128)(2,1)}), bf16[8,1,40,2048]{3,2,1,0:T(8,128)(2,1)S(1)}, u32[]{:S(2)}, u32[]{:S(2)}) async-start(bf16[8,1,40,2048]{3,2,1,0:T(8,128)(2,1)} %shard_map.250.refs_0_), calls=%async_computation.5 | async-start | bytes 2621440 | tf_op jit(solution)/shard_map/all_to_all | solution.py:592
  242.6 21.3 %all-to-all-start.6 = ((bf16[8,1,40,2048]{3,2,1,0:T(8,128)(2,1)}), bf16[8,1,40,2048]{3,2,1,0:T(8,128)(2,1)S(1)}, u32[]{:S(2)}, u32[]{:S(2)}) async-start(bf16[8,1,40,2048]{3,2,1,0:T(8,128)(2,1)} %shard_map.252), calls=%async_computation.6 | async-start | bytes 2621440 | tf_op jit(solution)/shard_map/all_to_all | solution.py:592
  246.4 14.6 %collective-permute-start.12 = (bf16[128,2048]{1,0:T(8,128)(2,1)}, bf16[128,2048]{1,0:T(8,128)(2,1)}, u32[]{:S(2)}, u32[]{:S(2)}) collective-permute-start(bf16[128,2048]{1,0:T(8,128)(2,1)} %fusion.2.refs_1_), channel_id=1, source_target_pairs={{0,2},{2,0},{4,6},{6,4},{1,3},{3,1},{5,7},{7,5},{8,10},{10,8},{12,... | collective-permute-start | bytes 1572872 | tf_op jit(solution)/shard_map/ppermute | solution.py:609
  265.1 35.9 %all-to-all-start.7 = ((bf16[8,1,40,2048]{3,2,1,0:T(8,128)(2,1)}), bf16[8,1,40,2048]{3,2,1,0:T(8,128)(2,1)S(1)}, u32[]{:S(2)}, u32[]{:S(2)}) async-start(bf16[8,1,40,2048]{3,2,1,0:T(8,128)(2,1)} %shard_map.253), calls=%async_computation.7 | async-start | bytes 2621440 | tf_op jit(solution)/shard_map/all_to_all | solution.py:592
  271.7 16.4 %collective-permute-start.13 = (bf16[128,2048]{1,0:T(8,128)(2,1)}, bf16[128,2048]{1,0:T(8,128)(2,1)S(1)}, u32[]{:S(2)}, u32[]{:S(2)}) collective-permute-start(bf16[128,2048]{1,0:T(8,128)(2,1)} %fusion.3), channel_id=1, source_target_pairs={{0,6},{2,4},{4,2},{6,0},{1,7},{3,5},{5,3},{7,1},{8,14},{10,12},{12... | collective-permute-start | bytes 1572872 | tf_op jit(solution)/shard_map/ppermute | solution.py:609
  291.3 32.7 %collective-permute-start.14 = (bf16[128,2048]{1,0:T(8,128)(2,1)S(1)}, bf16[128,2048]{1,0:T(8,128)(2,1)S(1)}, u32[]{:S(2)}, u32[]{:S(2)}) collective-permute-start(bf16[128,2048]{1,0:T(8,128)(2,1)S(1)} %fusion.4), channel_id=1, source_target_pairs={{0,4},{2,6},{4,0},{6,2},{1,5},{3,7},{5,1},{7,3},{8,12},{10,14},{12... | collective-permute-start | bytes 1572872 | tf_op jit(solution)/shard_map/ppermute | solution.py:609
  (38 other events, 223.9 us)

commit v5 on v4

--- a/solution.py
+++ b/solution.py
@@ -235,25 +235,22 @@
         pairs = [(low, low ^ apart) for low in range(groups)]
         incoming.append(lax.ppermute(sent[apart], "req", pairs))
 
-    def place():
-        arriving = whole_table // page_rows == myself
-        arrival = count_before(arriving.T).T.astype(jnp.int32)
-        apart = jnp.arange(groups, dtype=jnp.int32)[:, None] ^ myself
-        source = apart * per_group + arrival
-        landing = jnp.where(arriving, whole_table % page_rows, -1).reshape(-1)
-        slots = jnp.arange(page_rows, dtype=jnp.int32)
-        source_page = jnp.sum(
-            jnp.where(landing[None, :] == slots[:, None], source.reshape(-1)[None, :], 0), axis=1
-        )
-        source_line = (source_page[:, None] * PAGE + within[None, :]).reshape(-1)
-        collect = (source_line[:, None] == lines[None, :]).astype(jnp.bfloat16)
-        placed = jnp.dot(
-            collect, jnp.concatenate(incoming, axis=0), preferred_element_type=jnp.float32
-        ).astype(jnp.bfloat16)
-        placed = placed.reshape(page_rows, PAGE, 2, width)
-        return jnp.transpose(placed, (0, 2, 1, 3))
-
-    return incoming, place
+    arriving = whole_table // page_rows == myself
+    arrival = count_before(arriving.T).T.astype(jnp.int32)
+    apart = jnp.arange(groups, dtype=jnp.int32)[:, None] ^ myself
+    source = apart * per_group + arrival
+    landing = jnp.where(arriving, whole_table % page_rows, -1).reshape(-1)
+    slots = jnp.arange(page_rows, dtype=jnp.int32)
+    source_page = jnp.sum(
+        jnp.where(landing[None, :] == slots[:, None], source.reshape(-1)[None, :], 0), axis=1
+    )
+    source_line = (source_page[:, None] * PAGE + within[None, :]).reshape(-1)
+    collect = (source_line[:, None] == lines[None, :]).astype(jnp.bfloat16)
+    placed = jnp.dot(
+        collect, jnp.concatenate(incoming, axis=0), preferred_element_type=jnp.float32
+    ).astype(jnp.bfloat16)
+    placed = placed.reshape(page_rows, PAGE, 2, width)
+    return jnp.transpose(placed, (0, 2, 1, 3))
 
 
 def attend_kernel(query_ref, key_ref, value_ref, line_ref, row_ref, out_ref):
@@ -295,7 +292,7 @@
         ],
         out_specs=pl.BlockSpec((2, tok_rows, width), lambda i: (0, i, 0)),
         out_shape=jax.ShapeDtypeStruct((2, rows // 2, width), jnp.bfloat16),
-        compiler_params=pltpu.CompilerParams(vmem_limit_bytes=40 * 1024 * 1024),
+        compiler_params=pltpu.CompilerParams(vmem_limit_bytes=56 * 1024 * 1024),
         cost_estimate=pl.CostEstimate(
             flops=4 * rows * rows * width,
             bytes_accessed=8 * rows * width,
@@ -583,9 +580,9 @@
         mixings.append((high, (mixing - high.astype(jnp.float32)).astype(jnp.bfloat16)))
 
     gathered = lax.all_to_all(partial, "z", split_axis=0, concat_axis=0, tiled=True)
-    pages, place_pages = move_pages(keys, values, page_table, partial)
+    kv_cache = move_pages(keys, values, page_table, partial)
     normed, residual, packed = norm_and_pack(
-        pages[1:], stream_in, gathered, norm_gain, pickings[0], sources
+        [kv_cache] + pickings[1:], stream_in, gathered, norm_gain, pickings[0], sources
     )
 
     def exchange(block):
@@ -612,10 +609,9 @@
     own = exchange(packed)
     packed_first = pack_after(own, pickings[1], blocks[1], sources)
     first = exchange(packed_first)
-    outs_own = experts([packed_first], own)
     packed_third = pack_after(first, pickings[3], blocks[3], sources)
     third = exchange(packed_third)
-    outs_first = experts([outs_own, packed_third], first, 2)
+    outs_first = experts([packed_third], first, 2)
     outs_first = pack_after(outs_first, pickings[2], blocks[2], sources, into=True)
     second = exchange(outs_first)
     outs_third = experts([outs_first], third)
@@ -623,15 +619,18 @@
     share_first = mixed(1, second).astype(jnp.bfloat16)
     outs_second = experts([outs_third, share_first], second)
     got_first = to_plane(1, share_first)
+    outs_second = tie(outs_second, got_first)
     back_second = exchange(outs_second)
-    share_third = mixed(3, tie(back_third, got_first)).astype(jnp.bfloat16)
+    share_third = mixed(3, tie(back_third, outs_second)).astype(jnp.bfloat16)
+    outs_own = experts([share_third], own)
     got_third = to_plane(3, share_third)
-    back_own = exchange(tie(outs_own, back_second))
-    share_second = mixed(2, tie(back_second, got_third)).astype(jnp.bfloat16)
+    outs_own = tie(outs_own, got_third)
+    back_own = exchange(outs_own)
+    share_second = mixed(2, tie(back_second, outs_own)).astype(jnp.bfloat16)
     got_second = to_plane(2, share_second)
     total = residual + got_first.astype(jnp.float32) + got_third.astype(jnp.float32)
     total = total + mixed(0, back_own) + got_second.astype(jnp.float32)
-    return (total.astype(jnp.bfloat16), place_pages())
+    return (total.astype(jnp.bfloat16), kv_cache)
 
 
 def solution(mesh):

time: 328 us -> 322 us (0.982)
  waiting for transfers between devices: 139 us -> 134 us
  matrix products: 16.1 us -> 11.5 us
    all_to_all x1, waiting for transfers between devices: 29 us -> 0.01 us  [on_device_whole(): lax.all_to_all(partial, 'z', split_axis=0, concat_axis=0, tiled=True)]
    ppermute x1, waiting for transfers between devices: 1.4 us -> 16.7 us  [on_device_whole(): other_weight = lax.ppermute(half, 'x', swap)]
    ppermute x6, waiting for transfers between devices: 45.6 us -> 57.7 us  [to_plane(): return lax.ppermute(block, 'z', pairs[turn])]
    ppermute x3, waiting for transfers between devices: 9.33 us -> 0.01 us  [move_pages(): incoming.append(lax.ppermute(sent[apart], 'req', pairs))]
    ppermute x1, waiting for transfers between devices: 6.83 us -> 0.01 us  [on_device_whole(): other = lax.ppermute(leaving, 'x', swap)]
    ppermute x3, waiting for transfers between devices: 26.6 us -> 32.7 us  [on_device_whole(): table = lax.ppermute(table, 'z', pairs[turn])]
    all_to_all x7, waiting for transfers between devices: 19.9 us -> 25.7 us  [exchange(): lax.all_to_all(block, ('req', 'x'), split_axis=0, concat_axis=0, tiled=True)]
    dot_general x8, matrix products: 10.6 us -> 6.41 us  [mixed(): lax.dot_general(part, returned[:, 0].reshape(height, D), (((0,), (0,)), (...]
  transfers between devices with their start and end apart: 23 -> 23, of which waited for: 14 -> 12; matrix products, arithmetic and copies ran while one was open for 9% -> 8% of each run, Pallas kernels for 20% -> 18%
where the time goes in v5:
time: 322 us; the launch traced here: 321 us
  waiting for transfers between devices  134 us (42%)
  Pallas kernels  72 us (22%)
  starting transfers between devices  67.8 us (21%)
  local copies, waits for them, and re-layouts  27 us (8%)
  matrix products  11.5 us (4%)
  other arithmetic  6.95 us (2%)
    ppermute x6, waiting for transfers between devices, to_plane(): return lax.ppermute(block, 'z', pairs[turn])  57.7 us
    pallas_call x4, Pallas kernels, run_experts(): pl.pallas_call(expert_kernel, grid=(4,), in_specs=[pl.BlockSpec(memory_sp...  57 us
    ppermute x3, waiting for transfers between devices, on_device_whole(): table = lax.ppermute(table, 'z', pairs[turn])  32.7 us
    all_to_all x7, starting transfers between devices, exchange(): lax.all_to_all(block, ('req', 'x'), split_axis=0, concat_axis=0, tiled=True)  26.9 us
    all_to_all x7, waiting for transfers between devices, exchange(): lax.all_to_all(block, ('req', 'x'), split_axis=0, concat_axis=0, tiled=True)  25.7 us
    ppermute x6, starting transfers between devices, to_plane(): return lax.ppermute(block, 'z', pairs[turn])  22.5 us
    unnamed x79, local copies, waits for them, and re-layouts  17.9 us
    ppermute x1, waiting for transfers between devices, on_device_whole(): other_weight = lax.ppermute(half, 'x', swap)  16.7 us
  transfers between devices with their start and end apart: 23, of which 12 were waited for; matrix products, arithmetic and copies ran while one was open for 8% of the time, Pallas kernels for 18%

profile of v5, /device:TPU:0, one launch (start us, length us, event | category | flops | bytes accessed | tf_op | source)
XLA Modules:
  0.0 320.9 jit_solution(4296574292287376119)
XLA Ops:
  2.3 7.1 %shard_map.239.refs_1_.mine_ref = bf16[2,512,256]{2,1,0:T(8,128)(2,1)} custom-call(bf16[1024,256]{1,0:T(8,128)(2,1)} %query_ref.1, bf16[1024,256]{1,0:T(8,128)(2,1)} %key_ref.1, bf16[1024,256]{1,0:T(8,128)(2,1)} %value_ref.1, s32[1024,1]{1,0:T(8,128)} %copy.46.line_ref, s32[1,1024]{1,0:T(1,128)} %row_ref.1), custom_call_target="tpu_custom_call" | custom-call | flops 1073741824 | bytes 2097152 | tf_op jit(solution)/shard_map/pallas_call | solution.py:283
  14.3 16.7 %collective-permute-done.1.refs_0_ = bf16[256,1024]{1,0:T(8,128)(2,1)S(1)} collective-permute-done((bf16[256,1024]{1,0:T(8,128)(2,1)S(1)}, bf16[256,1024]{1,0:T(8,128)(2,1)S(1)}, u32[]{:S(2)}, u32[]{:S(2)}) %collective-permute-start.1) | collective-permute-done | bytes 524320 | tf_op jit(solution)/shard_map/ppermute | solution.py:544
  35.0 4.4 %shard_map.241.refs_1_ = bf16[4,128,2048]{2,1,0:T(8,128)(2,1)} custom-call(s32[2]{0:T(128)S(1)} %pad_add_fusion.place_ref, bf16[2,512,256]{2,1,0:T(8,128)(2,1)S(1)} %copy-done.6, bf16[512,256]{1,0:T(8,128)(2,1)S(1)} %collective-permute-done.other_ref, bf16[256,2048]{1,0:T(8,128)(2,1)S(1)} %copy-done.7, bf16[256,1024]{1,0:T(8,128)(2,1)S(1)} %copy-done.9, ...), custom_call_target="tpu_custom_call" | custom-call | flops 1073741824 | bytes 4194304 | tf_op jit(solution)/shard_map/pallas_call | solution.py:323
  39.4 5.3 %all-to-all-start = ((bf16[4,128,2048]{2,1,0:T(8,128)(2,1)}), bf16[4,128,2048]{2,1,0:T(8,128)(2,1)S(1)}, u32[]{:S(2)}, u32[]{:S(2)}) async-start(bf16[4,128,2048]{2,1,0:T(8,128)(2,1)} %shard_map.241.refs_1_), calls=%async_computation | async-start | bytes 4194304 | tf_op jit(solution)/shard_map/all_to_all | solution.py:582
  57.9 21.5 %collective-permute-done.6 = f32[2,16,128]{2,1,0:T(8,128)S(1)} collective-permute-done((f32[2,16,128]{2,1,0:T(8,128)S(1)}, f32[2,16,128]{2,1,0:T(8,128)S(1)}, u32[]{:S(2)}, u32[]{:S(2)}) %collective-permute-start.6) | collective-permute-done | bytes 16416 | tf_op jit(solution)/shard_map/ppermute | solution.py:575
  79.4 3.8 %collective-permute-start.8 = (f32[2,16,128]{2,1,0:T(8,128)S(1)}, f32[2,16,128]{2,1,0:T(8,128)S(1)}, u32[]{:S(2)}, u32[]{:S(2)}) collective-permute-start(f32[2,16,128]{2,1,0:T(8,128)S(1)} %get-tuple-element.22), channel_id=1, source_target_pairs={{0,6},{2,4},{4,2},{6,0},{1,7},{3,5},{5,3},{7,1},{8,14},{10,12},{12... | collective-permute-start | bytes 49160 | tf_op jit(solution)/shard_map/ppermute | solution.py:575
  83.1 11.2 %collective-permute-done.7 = f32[2,16,128]{2,1,0:T(8,128)S(1)} collective-permute-done((f32[2,16,128]{2,1,0:T(8,128)S(1)}, f32[2,16,128]{2,1,0:T(8,128)S(1)}, u32[]{:S(2)}, u32[]{:S(2)}) %collective-permute-start.7) | collective-permute-done | bytes 16416 | tf_op jit(solution)/shard_map/ppermute | solution.py:575
  108.2 3.7 %all-to-all-start.1 = ((bf16[8,1,40,2048]{3,2,1,0:T(8,128)(2,1)}), bf16[8,1,40,2048]{3,2,1,0:T(8,128)(2,1)S(1)}, u32[]{:S(2)}, u32[]{:S(2)}) async-start(bf16[8,1,40,2048]{3,2,1,0:T(8,128)(2,1)} %copy-done.10), calls=%async_computation.1 | async-start | bytes 2621440 | tf_op jit(solution)/shard_map/all_to_all | solution.py:589
  111.9 14.5 %collective-permute-done.9.block_ref = bf16[128,2048]{1,0:T(8,128)(2,1)S(1)} collective-permute-done((bf16[128,2048]{1,0:T(8,128)(2,1)}, bf16[128,2048]{1,0:T(8,128)(2,1)S(1)}, u32[]{:S(2)}, u32[]{:S(2)}) %collective-permute-start.9) | collective-permute-done | bytes 524320 | tf_op jit(solution)/shard_map/ppermute | solution.py:606
  136.4 14.8 %collective-permute-done.10.block_ref = bf16[128,2048]{1,0:T(8,128)(2,1)S(1)} collective-permute-done((bf16[128,2048]{1,0:T(8,128)(2,1)}, bf16[128,2048]{1,0:T(8,128)(2,1)S(1)}, u32[]{:S(2)}, u32[]{:S(2)}) %collective-permute-start.10) | collective-permute-done | bytes 524320 | tf_op jit(solution)/shard_map/ppermute | solution.py:606
  154.1 3.9 %all-to-all-start.4 = ((bf16[8,1,40,2048]{3,2,1,0:T(8,128)(2,1)}), bf16[8,1,40,2048]{3,2,1,0:T(8,128)(2,1)S(1)}, u32[]{:S(2)}, u32[]{:S(2)}) async-start(bf16[8,1,40,2048]{3,2,1,0:T(8,128)(2,1)} %shard_map.246.refs_0_), calls=%async_computation.4 | async-start | bytes 2621440 | tf_op jit(solution)/shard_map/all_to_all | solution.py:589
  158.0 7.8 %collective-permute-start.11 = (bf16[128,2048]{1,0:T(8,128)(2,1)S(1)}, bf16[128,2048]{1,0:T(8,128)(2,1)S(1)}, u32[]{:S(2)}, u32[]{:S(2)}) collective-permute-start(bf16[128,2048]{1,0:T(8,128)(2,1)S(1)} %copy-done.16), channel_id=1, source_target_pairs={{0,4},{2,6},{4,0},{6,2},{1,5},{3,7},{5,1},{7,3},{8,12},{10,14},{12... | collective-permute-start | bytes 1572872 | tf_op jit(solution)/shard_map/ppermute | solution.py:606
  165.8 14.4 %shard_map.247.after_ref = bf16[8,2,40,2048]{3,2,1,0:T(8,128)(2,1)} custom-call(bf16[8,1,40,2048]{3,2,1,0:T(8,128)(2,1)} %shard_map.246.refs_0_, bf16[8,1,40,2048]{3,2,1,0:T(8,128)(2,1)} %copy-done.3, bf16[320,320]{1,0:T(8,128)(2,1)} %constant.134.clone.refs_2_.refs_3_, bf16[320,320]{1,0:T(8,128)(2,1)} %constant.135.clone.refs_3_.refs_4_, ...), custom_call_target="tpu_custom_call" | custom-call | flops 4865392640 | bytes 27787264 | tf_op jit(solution)/shard_map/pallas_call | solution.py:479
  180.2 9.3 %collective-permute-done.11.block_ref = bf16[128,2048]{1,0:T(8,128)(2,1)S(1)} collective-permute-done((bf16[128,2048]{1,0:T(8,128)(2,1)S(1)}, bf16[128,2048]{1,0:T(8,128)(2,1)S(1)}, u32[]{:S(2)}, u32[]{:S(2)}) %collective-permute-start.11) | collective-permute-done | bytes 524320 | tf_op jit(solution)/shard_map/ppermute | solution.py:606
  194.3 3.8 %all-to-all-start.3 = ((bf16[8,2,40,2048]{3,2,1,0:T(8,128)(2,1)}), bf16[8,2,40,2048]{3,2,1,0:T(8,128)(2,1)S(1)}, u32[]{:S(2)}, u32[]{:S(2)}) async-start(bf16[8,2,40,2048]{3,2,1,0:T(8,128)(2,1)} %copy-done.1), calls=%async_computation.3 | async-start | bytes 5242880 | tf_op jit(solution)/shard_map/all_to_all | solution.py:589
  198.2 14.4 %shard_map.249.refs_0_ = bf16[8,1,40,2048]{3,2,1,0:T(8,128)(2,1)} custom-call(bf16[8,2,40,2048]{3,2,1,0:T(8,128)(2,1)} %copy-done.1, bf16[8,1,40,2048]{3,2,1,0:T(8,128)(2,1)} %copy-done.22, bf16[320,320]{1,0:T(8,128)(2,1)} %constant.134.clone.refs_2_.refs_3_, bf16[320,320]{1,0:T(8,128)(2,1)} %constant.135.clone.refs_3_.refs_4_, ...), custom_call_target="tpu_custom_call" | custom-call | flops 4865392640 | bytes 27787264 | tf_op jit(solution)/shard_map/pallas_call | solution.py:479
  212.6 17.4 %all-to-all-done.3.refs_2_ = bf16[8,2,40,2048]{3,2,1,0:T(8,128)(2,1)S(1)} async-done(((bf16[8,2,40,2048]{3,2,1,0:T(8,128)(2,1)}), bf16[8,2,40,2048]{3,2,1,0:T(8,128)(2,1)S(1)}, u32[]{:S(2)}, u32[]{:S(2)}) %all-to-all-start.3) | async-done | bytes 2621472 | tf_op jit(solution)/shard_map/all_to_all | solution.py:589
  238.2 13.7 %shard_map.250.refs_0_ = bf16[8,1,40,2048]{3,2,1,0:T(8,128)(2,1)} custom-call(bf16[8,1,40,2048]{3,2,1,0:T(8,128)(2,1)} %shard_map.249.refs_0_, bf16[128,2048]{1,0:T(8,128)(2,1)} %copy-done.24, bf16[8,2,40,2048]{3,2,1,0:T(8,128)(2,1)} %copy-done.21, bf16[320,320]{1,0:T(8,128)(2,1)} %constant.134.clone.refs_2_.refs_3_, ...), custom_call_target="tpu_custom_call" | custom-call | flops 4865392640 | bytes 27787264 | tf_op jit(solution)/shard_map/pallas_call | solution.py:479
  252.8 4.1 %all-to-all-start.7 = ((bf16[8,1,40,2048]{3,2,1,0:T(8,128)(2,1)}), bf16[8,1,40,2048]{3,2,1,0:T(8,128)(2,1)S(1)}, u32[]{:S(2)}, u32[]{:S(2)}) async-start(bf16[8,1,40,2048]{3,2,1,0:T(8,128)(2,1)} %shard_map.251.refs_1_), calls=%async_computation.7 | async-start | bytes 2621440 | tf_op jit(solution)/shard_map/all_to_all | solution.py:589
  262.5 14.4 %shard_map.253.refs_0_ = bf16[8,1,40,2048]{3,2,1,0:T(8,128)(2,1)} custom-call(bf16[128,2048]{1,0:T(8,128)(2,1)} %copy-done.23, bf16[8,1,40,2048]{3,2,1,0:T(8,128)(2,1)} %copy-done.2, bf16[320,320]{1,0:T(8,128)(2,1)} %constant.134.clone.refs_2_.refs_3_, bf16[320,320]{1,0:T(8,128)(2,1)} %constant.135.clone.refs_3_.refs_4_, bf16[4,2048,512]{2,1,0:T(8,128)(2,1)} %refs_4_.8, ...), custom_call_target="tpu_custom_call" | custom-call | flops 4865392640 | bytes 27787264 | tf_op jit(solution)/shard_map/pallas_call | solution.py:479
  277.8 4.2 %all-to-all-start.6 = ((bf16[8,1,40,2048]{3,2,1,0:T(8,128)(2,1)}), bf16[8,1,40,2048]{3,2,1,0:T(8,128)(2,1)S(1)}, u32[]{:S(2)}, u32[]{:S(2)}) async-start(bf16[8,1,40,2048]{3,2,1,0:T(8,128)(2,1)} %shard_map.254.refs_1_), calls=%async_computation.6 | async-start | bytes 2621440 | tf_op jit(solution)/shard_map/all_to_all | solution.py:589
  285.2 10.7 %collective-permute-start.14 = (bf16[128,2048]{1,0:T(8,128)(2,1)S(1)}, bf16[128,2048]{1,0:T(8,128)(2,1)S(1)}, u32[]{:S(2)}, u32[]{:S(2)}) collective-permute-start(bf16[128,2048]{1,0:T(8,128)(2,1)S(1)} %fusion.4), channel_id=1, source_target_pairs={{0,4},{2,6},{4,0},{6,2},{1,5},{3,7},{5,1},{7,3},{8,12},{10,14},{12... | collective-permute-start | bytes 1572872 | tf_op jit(solution)/shard_map/ppermute | solution.py:606
  295.9 3.8 %all-to-all-done.6 = bf16[8,1,40,2048]{3,2,1,0:T(8,128)(2,1)S(1)} async-done(((bf16[8,1,40,2048]{3,2,1,0:T(8,128)(2,1)}), bf16[8,1,40,2048]{3,2,1,0:T(8,128)(2,1)S(1)}, u32[]{:S(2)}, u32[]{:S(2)}) %all-to-all-start.6) | async-done | bytes 1310752 | tf_op jit(solution)/shard_map/all_to_all | solution.py:589
  300.7 19.0 %collective-permute-done.14 = bf16[128,2048]{1,0:T(8,128)(2,1)S(1)} collective-permute-done((bf16[128,2048]{1,0:T(8,128)(2,1)S(1)}, bf16[128,2048]{1,0:T(8,128)(2,1)S(1)}, u32[]{:S(2)}, u32[]{:S(2)}) %collective-permute-start.14) | collective-permute-done | bytes 524320 | tf_op jit(solution)/shard_map/ppermute | solution.py:606
  (170 shorter events, 75.8 us)
Async XLA Ops:
  9.4 24.5 %copy-start.6 = (bf16[2,512,256]{2,1,0:T(8,128)(2,1)S(1)}, bf16[2,512,256]{2,1,0:T(8,128)(2,1)}, u32[]{:S(2)}) copy-start(bf16[2,512,256]{2,1,0:T(8,128)(2,1)} %shard_map.239.refs_1_.mine_ref) | copy-start | bytes 1572868
  10.5 21.8 %collective-permute-start = (bf16[512,256]{1,0:T(8,128)(2,1)S(1)}, bf16[512,256]{1,0:T(8,128)(2,1)S(1)}, u32[]{:S(2)}, u32[]{:S(2)}) collective-permute-start(bf16[512,256]{1,0:T(8,128)(2,1)S(1)} %dynamic-slice_bitcast_fusion), channel_id=1, source_target_pairs={{0,1},{1,0},{2,3},{3,2},{4,5},{5,4},{6,7},{7,6},{8,9},{9,8},{10,11... | collective-permute-start | bytes 786440 | tf_op jit(solution)/shard_map/ppermute | solution.py:547
  13.5 17.5 %collective-permute-start.1 = (bf16[256,1024]{1,0:T(8,128)(2,1)S(1)}, bf16[256,1024]{1,0:T(8,128)(2,1)S(1)}, u32[]{:S(2)}, u32[]{:S(2)}) collective-permute-start(bf16[256,1024]{1,0:T(8,128)(2,1)S(1)} %constant_dynamic-slice_fusion), channel_id=1, source_target_pairs={{0,1},{1,0},{2,3},{3,2},{4,5},{5,4},{6,7},{7,6},{8,9},{9,8},{10,11... | collective-permute-start | bytes 1572872 | tf_op jit(solution)/shard_map/ppermute | solution.py:544
  31.8 2.1 collective-permute-start.2
  39.4 63.5 %all-to-all-start = ((bf16[4,128,2048]{2,1,0:T(8,128)(2,1)}), bf16[4,128,2048]{2,1,0:T(8,128)(2,1)S(1)}, u32[]{:S(2)}, u32[]{:S(2)}) async-start(bf16[4,128,2048]{2,1,0:T(8,128)(2,1)} %shard_map.241.refs_1_), calls=%async_computation | async-start | bytes 4194304 | tf_op jit(solution)/shard_map/all_to_all | solution.py:582
  49.2 48.6 %collective-permute-start.5 = (bf16[256,512]{1,0:T(8,128)(2,1)S(1)}, bf16[256,512]{1,0:T(8,128)(2,1)}, u32[]{:S(2)}, u32[]{:S(2)}) collective-permute-start(bf16[256,512]{1,0:T(8,128)(2,1)S(1)} %get-tuple-element.17), channel_id=1, source_target_pairs={{0,24},{8,16},{16,8},{24,0},{1,25},{9,17},{17,9},{25,1},{2,26},{10... | collective-permute-start | bytes 786440 | tf_op jit(solution)/shard_map/ppermute | solution.py:236
  50.2 47.7 %collective-permute-start.4 = (bf16[256,512]{1,0:T(8,128)(2,1)S(1)}, bf16[256,512]{1,0:T(8,128)(2,1)}, u32[]{:S(2)}, u32[]{:S(2)}) collective-permute-start(bf16[256,512]{1,0:T(8,128)(2,1)S(1)} %get-tuple-element.18), channel_id=1, source_target_pairs={{0,16},{8,24},{16,0},{24,8},{1,17},{9,25},{17,1},{25,9},{2,18},{10... | collective-permute-start | bytes 786440 | tf_op jit(solution)/shard_map/ppermute | solution.py:236
  50.7 47.1 %collective-permute-start.3 = (bf16[256,512]{1,0:T(8,128)(2,1)S(1)}, bf16[256,512]{1,0:T(8,128)(2,1)}, u32[]{:S(2)}, u32[]{:S(2)}) collective-permute-start(bf16[256,512]{1,0:T(8,128)(2,1)S(1)} %get-tuple-element.19), channel_id=1, source_target_pairs={{0,8},{8,0},{16,24},{24,16},{1,9},{9,1},{17,25},{25,17},{2,10},{10... | collective-permute-start | bytes 786440 | tf_op jit(solution)/shard_map/ppermute | solution.py:236
  52.3 27.1 %collective-permute-start.6 = (f32[2,16,128]{2,1,0:T(8,128)S(1)}, f32[2,16,128]{2,1,0:T(8,128)S(1)}, u32[]{:S(2)}, u32[]{:S(2)}) collective-permute-start(f32[2,16,128]{2,1,0:T(8,128)S(1)} %get-tuple-element.24), channel_id=1, source_target_pairs={{0,2},{2,0},{4,6},{6,4},{1,3},{3,1},{5,7},{7,5},{8,10},{10,8},{12,... | collective-permute-start | bytes 49160 | tf_op jit(solution)/shard_map/ppermute | solution.py:575
  54.4 40.0 %collective-permute-start.7 = (f32[2,16,128]{2,1,0:T(8,128)S(1)}, f32[2,16,128]{2,1,0:T(8,128)S(1)}, u32[]{:S(2)}, u32[]{:S(2)}) collective-permute-start(f32[2,16,128]{2,1,0:T(8,128)S(1)} %get-tuple-element.23), channel_id=1, source_target_pairs={{0,4},{2,6},{4,0},{6,2},{1,5},{3,7},{5,1},{7,3},{8,12},{10,14},{12... | collective-permute-start | bytes 49160 | tf_op jit(solution)/shard_map/ppermute | solution.py:575
  79.4 16.2 %collective-permute-start.8 = (f32[2,16,128]{2,1,0:T(8,128)S(1)}, f32[2,16,128]{2,1,0:T(8,128)S(1)}, u32[]{:S(2)}, u32[]{:S(2)}) collective-permute-start(f32[2,16,128]{2,1,0:T(8,128)S(1)} %get-tuple-element.22), channel_id=1, source_target_pairs={{0,6},{2,4},{4,2},{6,0},{1,7},{3,5},{5,3},{7,1},{8,14},{10,12},{12... | collective-permute-start | bytes 49160 | tf_op jit(solution)/shard_map/ppermute | solution.py:575
  108.2 21.5 %all-to-all-start.1 = ((bf16[8,1,40,2048]{3,2,1,0:T(8,128)(2,1)}), bf16[8,1,40,2048]{3,2,1,0:T(8,128)(2,1)S(1)}, u32[]{:S(2)}, u32[]{:S(2)}) async-start(bf16[8,1,40,2048]{3,2,1,0:T(8,128)(2,1)} %copy-done.10), calls=%async_computation.1 | async-start | bytes 2621440 | tf_op jit(solution)/shard_map/all_to_all | solution.py:589
  111.9 14.5 %collective-permute-start.9 = (bf16[128,2048]{1,0:T(8,128)(2,1)}, bf16[128,2048]{1,0:T(8,128)(2,1)S(1)}, u32[]{:S(2)}, u32[]{:S(2)}) collective-permute-start(bf16[128,2048]{1,0:T(8,128)(2,1)} %copy-done.15), channel_id=1, source_target_pairs={{0,2},{2,0},{4,6},{6,4},{1,3},{3,1},{5,7},{7,5},{8,10},{10,8},{12,... | collective-permute-start | bytes 1572872 | tf_op jit(solution)/shard_map/ppermute | solution.py:606
  131.3 21.2 %all-to-all-start.2 = ((bf16[8,1,40,2048]{3,2,1,0:T(8,128)(2,1)}), bf16[8,1,40,2048]{3,2,1,0:T(8,128)(2,1)S(1)}, u32[]{:S(2)}, u32[]{:S(2)}) async-start(bf16[8,1,40,2048]{3,2,1,0:T(8,128)(2,1)} %copy-done.4), calls=%async_computation.2 | async-start | bytes 2621440 | tf_op jit(solution)/shard_map/all_to_all | solution.py:589
  134.8 16.4 %collective-permute-start.10 = (bf16[128,2048]{1,0:T(8,128)(2,1)}, bf16[128,2048]{1,0:T(8,128)(2,1)S(1)}, u32[]{:S(2)}, u32[]{:S(2)}) collective-permute-start(bf16[128,2048]{1,0:T(8,128)(2,1)} %copy-done.15), channel_id=1, source_target_pairs={{0,6},{2,4},{4,2},{6,0},{1,7},{3,5},{5,3},{7,1},{8,14},{10,12},{12... | collective-permute-start | bytes 1572872 | tf_op jit(solution)/shard_map/ppermute | solution.py:606
  154.1 39.1 %all-to-all-start.4 = ((bf16[8,1,40,2048]{3,2,1,0:T(8,128)(2,1)}), bf16[8,1,40,2048]{3,2,1,0:T(8,128)(2,1)S(1)}, u32[]{:S(2)}, u32[]{:S(2)}) async-start(bf16[8,1,40,2048]{3,2,1,0:T(8,128)(2,1)} %shard_map.246.refs_0_), calls=%async_computation.4 | async-start | bytes 2621440 | tf_op jit(solution)/shard_map/all_to_all | solution.py:589
  158.0 31.5 %collective-permute-start.11 = (bf16[128,2048]{1,0:T(8,128)(2,1)S(1)}, bf16[128,2048]{1,0:T(8,128)(2,1)S(1)}, u32[]{:S(2)}, u32[]{:S(2)}) collective-permute-start(bf16[128,2048]{1,0:T(8,128)(2,1)S(1)} %copy-done.16), channel_id=1, source_target_pairs={{0,4},{2,6},{4,0},{6,2},{1,5},{3,7},{5,1},{7,3},{8,12},{10,14},{12... | collective-permute-start | bytes 1572872 | tf_op jit(solution)/shard_map/ppermute | solution.py:606
  194.3 35.6 %all-to-all-start.3 = ((bf16[8,2,40,2048]{3,2,1,0:T(8,128)(2,1)}), bf16[8,2,40,2048]{3,2,1,0:T(8,128)(2,1)S(1)}, u32[]{:S(2)}, u32[]{:S(2)}) async-start(bf16[8,2,40,2048]{3,2,1,0:T(8,128)(2,1)} %copy-done.1), calls=%async_computation.3 | async-start | bytes 5242880 | tf_op jit(solution)/shard_map/all_to_all | solution.py:589
  231.4 21.3 %all-to-all-start.5 = ((bf16[8,1,40,2048]{3,2,1,0:T(8,128)(2,1)}), bf16[8,1,40,2048]{3,2,1,0:T(8,128)(2,1)S(1)}, u32[]{:S(2)}, u32[]{:S(2)}) async-start(bf16[8,1,40,2048]{3,2,1,0:T(8,128)(2,1)} %shard_map.249.refs_0_), calls=%async_computation.5 | async-start | bytes 2621440 | tf_op jit(solution)/shard_map/all_to_all | solution.py:589
  237.4 14.5 %collective-permute-start.12 = (bf16[128,2048]{1,0:T(8,128)(2,1)S(1)}, bf16[128,2048]{1,0:T(8,128)(2,1)S(1)}, u32[]{:S(2)}, u32[]{:S(2)}) collective-permute-start(bf16[128,2048]{1,0:T(8,128)(2,1)S(1)} %fusion.2.refs_1_), channel_id=1, source_target_pairs={{0,2},{2,0},{4,6},{6,4},{1,3},{3,1},{5,7},{7,5},{8,10},{10,8},{12,... | collective-permute-start | bytes 1572872 | tf_op jit(solution)/shard_map/ppermute | solution.py:606
  252.8 25.0 %all-to-all-start.7 = ((bf16[8,1,40,2048]{3,2,1,0:T(8,128)(2,1)}), bf16[8,1,40,2048]{3,2,1,0:T(8,128)(2,1)S(1)}, u32[]{:S(2)}, u32[]{:S(2)}) async-start(bf16[8,1,40,2048]{3,2,1,0:T(8,128)(2,1)} %shard_map.251.refs_1_), calls=%async_computation.7 | async-start | bytes 2621440 | tf_op jit(solution)/shard_map/all_to_all | solution.py:589
  260.1 16.8 %collective-permute-start.13 = (bf16[128,2048]{1,0:T(8,128)(2,1)S(1)}, bf16[128,2048]{1,0:T(8,128)(2,1)S(1)}, u32[]{:S(2)}, u32[]{:S(2)}) collective-permute-start(bf16[128,2048]{1,0:T(8,128)(2,1)S(1)} %fusion.3.refs_0_), channel_id=1, source_target_pairs={{0,6},{2,4},{4,2},{6,0},{1,7},{3,5},{5,3},{7,1},{8,14},{10,12},{12... | collective-permute-start | bytes 1572872 | tf_op jit(solution)/shard_map/ppermute | solution.py:606
  277.8 21.9 %all-to-all-start.6 = ((bf16[8,1,40,2048]{3,2,1,0:T(8,128)(2,1)}), bf16[8,1,40,2048]{3,2,1,0:T(8,128)(2,1)S(1)}, u32[]{:S(2)}, u32[]{:S(2)}) async-start(bf16[8,1,40,2048]{3,2,1,0:T(8,128)(2,1)} %shard_map.254.refs_1_), calls=%async_computation.6 | async-start | bytes 2621440 | tf_op jit(solution)/shard_map/all_to_all | solution.py:589
  285.2 34.5 %collective-permute-start.14 = (bf16[128,2048]{1,0:T(8,128)(2,1)S(1)}, bf16[128,2048]{1,0:T(8,128)(2,1)S(1)}, u32[]{:S(2)}, u32[]{:S(2)}) collective-permute-start(bf16[128,2048]{1,0:T(8,128)(2,1)S(1)} %fusion.4), channel_id=1, source_target_pairs={{0,4},{2,6},{4,0},{6,2},{1,5},{3,7},{5,1},{7,3},{8,12},{10,14},{12... | collective-permute-start | bytes 1572872 | tf_op jit(solution)/shard_map/ppermute | solution.py:606
  (38 other events, 194.4 us)

commit v6 on v5

--- a/solution.py
+++ b/solution.py
@@ -292,7 +292,7 @@
         ],
         out_specs=pl.BlockSpec((2, tok_rows, width), lambda i: (0, i, 0)),
         out_shape=jax.ShapeDtypeStruct((2, rows // 2, width), jnp.bfloat16),
-        compiler_params=pltpu.CompilerParams(vmem_limit_bytes=56 * 1024 * 1024),
+        compiler_params=pltpu.CompilerParams(vmem_limit_bytes=40 * 1024 * 1024),
         cost_estimate=pl.CostEstimate(
             flops=4 * rows * rows * width,
             bytes_accessed=8 * rows * width,
@@ -389,31 +389,30 @@
     )(*after, *operands)
 
 
-def pack_kernel(after_ref, picking_ref, block_ref, out_ref):
+def pack_kernel(*refs):
+    picking_ref, block_ref, out_ref = refs[-3:]
     out_ref[:, 0] = pack_rows(
         picking_ref[...], block_ref[...], (out_ref.shape[0],) + out_ref.shape[2:]
     )
 
 
-def pack_after(after, picking, block, sources, into=False):
+def pack_after(after, picking, block, sources):
     height, tok_rows = picking.shape
-    parts = 2 if into else 1
     return pl.pallas_call(
         pack_kernel,
         grid=(1,),
-        in_specs=[
-            pl.BlockSpec(memory_space=pl.ANY),
+        in_specs=[pl.BlockSpec(memory_space=pl.ANY)] * len(after)
+        + [
             pl.BlockSpec((height, tok_rows), lambda i: (0, 0)),
             pl.BlockSpec((tok_rows, D), lambda i: (0, 0)),
         ],
-        out_specs=pl.BlockSpec((sources, 1, height // sources, D), lambda i: (0, parts - 1, 0, 0)),
-        out_shape=jax.ShapeDtypeStruct((sources, parts, height // sources, D), jnp.bfloat16),
-        input_output_aliases={0: 0} if into else {},
+        out_specs=pl.BlockSpec((sources, 1, height // sources, D), lambda i: (0, 0, 0, 0)),
+        out_shape=jax.ShapeDtypeStruct((sources, 1, height // sources, D), jnp.bfloat16),
         compiler_params=pltpu.CompilerParams(vmem_limit_bytes=40 * 1024 * 1024),
         cost_estimate=pl.CostEstimate(
             flops=2 * height * tok_rows * D, bytes_accessed=4 * height * D, transcendentals=0
         ),
-    )(after, picking, block)
+    )(*after, picking, block)
 
 
 def tie_kernel(*refs):
@@ -464,8 +463,8 @@
         out_ref[:, 0] = pack_rows(back_ref[...], outs[...], (out_ref.shape[0],) + out_ref.shape[2:])
 
 
-def run_experts(after, arrived, w_gate, w_up, w_down, out_parts=1):
-    sources, parts, slots, depth = arrived.shape
+def run_experts(after, arrived, w_gate, w_up, w_down):
+    sources, _, slots, depth = arrived.shape
     units = w_gate.shape[2]
     height = sources * slots
     index = np.arange(height)
@@ -481,7 +480,7 @@
         grid=(4,),
         in_specs=[pl.BlockSpec(memory_space=pl.ANY)] * len(after)
         + [
-            pl.BlockSpec((sources, 1, slots, depth), lambda i: (0, parts - 1, 0, 0)),
+            pl.BlockSpec((sources, 1, slots, depth), lambda i: (0, 0, 0, 0)),
             pl.BlockSpec((height, height), fixed),
             pl.BlockSpec((height, height), fixed),
             pl.BlockSpec((1, depth, units), lambda i: (i, 0, 0)),
@@ -489,7 +488,7 @@
             pl.BlockSpec((1, units, depth), lambda i: (i, 0, 0)),
         ],
         out_specs=pl.BlockSpec((sources, 1, slots, depth), lambda i: (0, 0, 0, 0)),
-        out_shape=jax.ShapeDtypeStruct((sources, out_parts, slots, depth), jnp.bfloat16),
+        out_shape=jax.ShapeDtypeStruct((sources, 1, slots, depth), jnp.bfloat16),
         scratch_shapes=[
             pltpu.VMEM((height, depth), jnp.bfloat16),
             pltpu.VMEM((height // 2, depth), jnp.float32),
@@ -557,7 +556,6 @@
         other_rest,
     )
 
-    routes = tie(routes, partial)
     matched = routes[:, :, None] == jnp.arange(EXPERTS, dtype=jnp.int32)[None, None, :]
     named = jnp.any(matched, axis=1)
     weight_of = jnp.sum(jnp.where(matched, combine[:, :, None], 0.0), axis=1)
@@ -568,11 +566,13 @@
     tables = tables.reshape(2, groups, PLANES, 2 * lanes, tok_rows)
     tables = jnp.transpose(tables, (2, 0, 1, 3, 4)).reshape(PLANES, 2, plane_experts, tok_rows)
     lines = jnp.arange(height, dtype=jnp.float32)
-    pickings, mixings = [], []
+    received = []
     for turn in range(PLANES):
         table = lax.dynamic_index_in_dim(tables, level ^ turn, 0, keepdims=False)
-        if turn:
-            table = lax.ppermute(table, "z", pairs[turn])
+        received.append(lax.ppermute(table, "z", pairs[turn]) if turn else table)
+    partial = tie(partial, *received[1:])
+    pickings, mixings = [], []
+    for table in received:
         hits = table[0][:, None, :] == lines[None, :, None]
         pickings.append(jnp.sum(hits.astype(jnp.float32), axis=0).astype(jnp.bfloat16))
         mixing = jnp.sum(jnp.where(hits, table[1][:, None, :], 0.0), axis=0)
@@ -588,8 +588,8 @@
     def exchange(block):
         return lax.all_to_all(block, ("req", "x"), split_axis=0, concat_axis=0, tiled=True)
 
-    def experts(after, arrived, out_parts=1):
-        return run_experts(after, arrived, w_gate, w_up, w_down, out_parts)
+    def experts(after, arrived):
+        return run_experts(after, arrived, w_gate, w_up, w_down)
 
     def mixed(turn, returned):
         return sum(
@@ -607,26 +607,26 @@
 
     blocks = [normed] + [to_plane(turn, normed) for turn in range(1, PLANES)]
     own = exchange(packed)
-    packed_first = pack_after(own, pickings[1], blocks[1], sources)
+    packed_first = pack_after([own], pickings[1], blocks[1], sources)
     first = exchange(packed_first)
-    packed_third = pack_after(first, pickings[3], blocks[3], sources)
+    outs_own = experts([packed_first], own)
+    packed_third = pack_after([first, outs_own], pickings[3], blocks[3], sources)
     third = exchange(packed_third)
-    outs_first = experts([packed_third], first, 2)
-    outs_first = pack_after(outs_first, pickings[2], blocks[2], sources, into=True)
-    second = exchange(outs_first)
+    outs_first = experts([packed_third], first)
+    back_first = exchange(outs_first)
     outs_third = experts([outs_first], third)
+    packed_second = pack_after([back_first], pickings[2], blocks[2], sources)
+    second = exchange(packed_second)
+    share_first = mixed(1, back_first).astype(jnp.bfloat16)
+    got_first = to_plane(1, share_first)
+    outs_third = tie(outs_third, second, got_first)
     back_third = exchange(outs_third)
-    share_first = mixed(1, second).astype(jnp.bfloat16)
-    outs_second = experts([outs_third, share_first], second)
-    got_first = to_plane(1, share_first)
-    outs_second = tie(outs_second, got_first)
-    back_second = exchange(outs_second)
-    share_third = mixed(3, tie(back_third, outs_second)).astype(jnp.bfloat16)
-    outs_own = experts([share_third], own)
+    outs_second = experts([outs_third], second)
+    share_third = mixed(3, back_third).astype(jnp.bfloat16)
     got_third = to_plane(3, share_third)
-    outs_own = tie(outs_own, got_third)
-    back_own = exchange(outs_own)
-    share_second = mixed(2, tie(back_second, outs_own)).astype(jnp.bfloat16)
+    back_second = exchange(tie(outs_second, back_third))
+    share_second = mixed(2, back_second).astype(jnp.bfloat16)
+    back_own = exchange(tie(outs_own, back_second, got_third))
     got_second = to_plane(2, share_second)
     total = residual + got_first.astype(jnp.float32) + got_third.astype(jnp.float32)
     total = total + mixed(0, back_own) + got_second.astype(jnp.float32)

time: 322 us -> 336 us (1.043)
  blocking collectives: 0 us -> 21.3 us
  starting transfers between devices: 67.8 us -> 64.4 us
    ppermute x3, waiting for transfers between devices: 32.7 us -> 0.01 us  [on_device_whole(): received.append(lax.ppermute(table, 'z', pairs[turn]) if turn else table)]
    all_to_all x1, waiting for transfers between devices: 0.01 us -> 24.7 us  [on_device_whole(): lax.all_to_all(partial, 'z', split_axis=0, concat_axis=0, tiled=True)]
    all_to_all x0 -> x1, blocking collectives: none -> 21.3 us  [exchange(): lax.all_to_all(block, ('req', 'x'), split_axis=0, concat_axis=0, tiled=True)]
    ppermute x6, waiting for transfers between devices: 57.7 us -> 69.8 us  [to_plane(): return lax.ppermute(block, 'z', pairs[turn])]
    all_to_all x7, waiting for transfers between devices: 25.7 us -> 15.1 us  [exchange(): lax.all_to_all(block, ('req', 'x'), split_axis=0, concat_axis=0, tiled=True)]
    ppermute x3, waiting for transfers between devices: 0.01 us -> 10.1 us  [move_pages(): incoming.append(lax.ppermute(sent[apart], 'req', pairs))]
    ppermute x1, waiting for transfers between devices: 16.7 us -> 12.1 us  [on_device_whole(): other_weight = lax.ppermute(half, 'x', swap)]
    ppermute x3, starting transfers between devices: 8.21 us -> 4.7 us  [on_device_whole(): received.append(lax.ppermute(table, 'z', pairs[turn]) if turn else table)]
  transfers between devices with their start and end apart: 23 -> 23, of which waited for: 12 -> 15; matrix products, arithmetic and copies ran while one was open for 8% -> 6% of each run, Pallas kernels for 18% -> 14%
where the time goes in v6:
time: 336 us; the launch traced here: 335 us
  waiting for transfers between devices  134 us (40%)
  Pallas kernels  70.7 us (21%)
  starting transfers between devices  64.4 us (19%)
  local copies, waits for them, and re-layouts  24.9 us (7%)
  blocking collectives  21.3 us (6%)
  matrix products  13.3 us (4%)
  other arithmetic  5.7 us (2%)
    ppermute x6, waiting for transfers between devices, to_plane(): return lax.ppermute(block, 'z', pairs[turn])  69.8 us
    pallas_call x4, Pallas kernels, run_experts(): pl.pallas_call(expert_kernel, grid=(4,), in_specs=[pl.BlockSpec(memory_sp...  57.5 us
    all_to_all x7, starting transfers between devices, exchange(): lax.all_to_all(block, ('req', 'x'), split_axis=0, concat_axis=0, tiled=True)  27.7 us
    all_to_all x1, waiting for transfers between devices, on_device_whole(): lax.all_to_all(partial, 'z', split_axis=0, concat_axis=0, tiled=True)  24.7 us
    ppermute x6, starting transfers between devices, to_plane(): return lax.ppermute(block, 'z', pairs[turn])  21.8 us
    all_to_all x1, blocking collectives, exchange(): lax.all_to_all(block, ('req', 'x'), split_axis=0, concat_axis=0, tiled=True)  21.3 us
    unnamed x98, local copies, waits for them, and re-layouts  20.7 us
    all_to_all x7, waiting for transfers between devices, exchange(): lax.all_to_all(block, ('req', 'x'), split_axis=0, concat_axis=0, tiled=True)  15.1 us
  transfers between devices with their start and end apart: 23, of which 15 were waited for; matrix products, arithmetic and copies ran while one was open for 6% of the time, Pallas kernels for 14%

profile of v6, /device:TPU:0, one launch (start us, length us, event | category | flops | bytes accessed | tf_op | source)
XLA Modules:
  0.0 335.1 jit_solution(3992045642335101239)
XLA Ops:
  5.4 5.0 %shard_map.239.refs_1_.mine_ref = bf16[2,512,256]{2,1,0:T(8,128)(2,1)S(1)} custom-call(bf16[1024,256]{1,0:T(8,128)(2,1)S(1)} %copy-done.17, bf16[1024,256]{1,0:T(8,128)(2,1)S(1)} %copy-done.18, bf16[1024,256]{1,0:T(8,128)(2,1)S(1)} %copy-done.20, s32[1024,1]{1,0:T(8,128)S(1)} %copy.40.line_ref, s32[1,1024]{1,0:T(1,128)S(1)} %copy-done.16), custom_call_target="tpu_custom_call" | custom-call | flops 1073741824 | bytes 2097152 | tf_op jit(solution)/shard_map/pallas_call | solution.py:283
  18.9 12.1 %collective-permute-done.1.refs_0_ = bf16[256,1024]{1,0:T(8,128)(2,1)S(1)} collective-permute-done((bf16[256,1024]{1,0:T(8,128)(2,1)S(1)}, bf16[256,1024]{1,0:T(8,128)(2,1)S(1)}, u32[]{:S(2)}, u32[]{:S(2)}) %collective-permute-start.1) | collective-permute-done | bytes 524320 | tf_op jit(solution)/shard_map/ppermute | solution.py:543
  42.2 5.2 %all-to-all-start = ((bf16[4,128,2048]{2,1,0:T(8,128)(2,1)}), bf16[4,128,2048]{2,1,0:T(8,128)(2,1)S(1)}, u32[]{:S(2)}, u32[]{:S(2)}) async-start(bf16[4,128,2048]{2,1,0:T(8,128)(2,1)} %shard_map.242.refs_1_), calls=%async_computation | async-start | bytes 4194304 | tf_op jit(solution)/shard_map/all_to_all | solution.py:582
  57.3 4.3 %collective-permute-done.8 = bf16[256,512]{1,0:T(8,128)(2,1)S(1)} collective-permute-done((bf16[256,512]{1,0:T(8,128)(2,1)S(1)}, bf16[256,512]{1,0:T(8,128)(2,1)S(1)}, u32[]{:S(2)}, u32[]{:S(2)}) %collective-permute-start.8) | collective-permute-done | bytes 262176 | tf_op jit(solution)/shard_map/ppermute | solution.py:236
  61.6 5.7 %collective-permute-done.7 = bf16[256,512]{1,0:T(8,128)(2,1)S(1)} collective-permute-done((bf16[256,512]{1,0:T(8,128)(2,1)S(1)}, bf16[256,512]{1,0:T(8,128)(2,1)S(1)}, u32[]{:S(2)}, u32[]{:S(2)}) %collective-permute-start.7) | collective-permute-done | bytes 262176 | tf_op jit(solution)/shard_map/ppermute | solution.py:236
  71.2 24.7 %all-to-all-done.refs_5_ = bf16[4,128,2048]{2,1,0:T(8,128)(2,1)S(1)} async-done(((bf16[4,128,2048]{2,1,0:T(8,128)(2,1)}), bf16[4,128,2048]{2,1,0:T(8,128)(2,1)S(1)}, u32[]{:S(2)}, u32[]{:S(2)}) %all-to-all-start) | async-done | bytes 2097184 | tf_op jit(solution)/shard_map/all_to_all | solution.py:582
  100.9 3.8 %all-to-all-start.1 = ((bf16[8,1,40,2048]{3,2,1,0:T(8,128)(2,1)}), bf16[8,1,40,2048]{3,2,1,0:T(8,128)(2,1)S(1)}, u32[]{:S(2)}, u32[]{:S(2)}) async-start(bf16[8,1,40,2048]{3,2,1,0:T(8,128)(2,1)} %copy-done.11), calls=%async_computation.1 | async-start | bytes 2621440 | tf_op jit(solution)/shard_map/all_to_all | solution.py:589
  104.6 14.5 %collective-permute-done.9.refs_2_ = bf16[128,2048]{1,0:T(8,128)(2,1)S(1)} collective-permute-done((bf16[128,2048]{1,0:T(8,128)(2,1)}, bf16[128,2048]{1,0:T(8,128)(2,1)S(1)}, u32[]{:S(2)}, u32[]{:S(2)}) %collective-permute-start.9) | collective-permute-done | bytes 524320 | tf_op jit(solution)/shard_map/ppermute | solution.py:606
  123.9 3.8 %all-to-all-start.2 = ((bf16[8,1,40,2048]{3,2,1,0:T(8,128)(2,1)}), bf16[8,1,40,2048]{3,2,1,0:T(8,128)(2,1)S(1)}, u32[]{:S(2)}, u32[]{:S(2)}) async-start(bf16[8,1,40,2048]{3,2,1,0:T(8,128)(2,1)} %shard_map.245.refs_0_), calls=%async_computation.2 | async-start | bytes 2621440 | tf_op jit(solution)/shard_map/all_to_all | solution.py:589
  129.2 14.4 %shard_map.246.refs_1_.refs_0_ = bf16[8,1,40,2048]{3,2,1,0:T(8,128)(2,1)} custom-call(bf16[8,1,40,2048]{3,2,1,0:T(8,128)(2,1)} %shard_map.245.refs_0_, bf16[8,1,40,2048]{3,2,1,0:T(8,128)(2,1)} %copy-done.2, bf16[320,320]{1,0:T(8,128)(2,1)} %constant.134.clone.refs_2_, bf16[320,320]{1,0:T(8,128)(2,1)} %constant.135.clone.refs_3_, ...), custom_call_target="tpu_custom_call" | custom-call | flops 4865392640 | bytes 27787264 | tf_op jit(solution)/shard_map/pallas_call | solution.py:478
  148.7 14.4 %shard_map.248.refs_0_ = bf16[8,1,40,2048]{3,2,1,0:T(8,128)(2,1)} custom-call(bf16[8,1,40,2048]{3,2,1,0:T(8,128)(2,1)} %copy-done.4, bf16[8,1,40,2048]{3,2,1,0:T(8,128)(2,1)} %copy-done.3, bf16[320,320]{1,0:T(8,128)(2,1)} %constant.134.clone.refs_2_, bf16[320,320]{1,0:T(8,128)(2,1)} %constant.135.clone.refs_3_, bf16[4,2048,512]{2,1,0:T(8,128)(2,1)} %refs_4_.9, ...), custom_call_target="tpu_custom_call" | custom-call | flops 4865392640 | bytes 27787264 | tf_op jit(solution)/shard_map/pallas_call | solution.py:478
  163.0 21.3 %all_to_all.45.refs_0_ = bf16[8,1,40,2048]{3,2,1,0:T(8,128)(2,1)S(1)} all-to-all(bf16[8,1,40,2048]{3,2,1,0:T(8,128)(2,1)} %shard_map.248.refs_0_), channel_id=1, replica_groups=mesh['req'=4,'z'=4,'x'=2] {'req','x'}, dimensions={0} | all-to-all | bytes 2621440 | tf_op jit(solution)/shard_map/all_to_all | solution.py:589
  184.3 4.3 %all-to-all-start.4 = ((bf16[8,1,40,2048]{3,2,1,0:T(8,128)(2,1)}), bf16[8,1,40,2048]{3,2,1,0:T(8,128)(2,1)}, u32[]{:S(2)}, u32[]{:S(2)}) async-start(bf16[8,1,40,2048]{3,2,1,0:T(8,128)(2,1)} %copy-done.4), calls=%async_computation.4 | async-start | bytes 2621440 | tf_op jit(solution)/shard_map/all_to_all | solution.py:589
  188.6 8.1 %collective-permute-start.12 = (bf16[128,2048]{1,0:T(8,128)(2,1)S(1)}, bf16[128,2048]{1,0:T(8,128)(2,1)S(1)}, u32[]{:S(2)}, u32[]{:S(2)}) collective-permute-start(bf16[128,2048]{1,0:T(8,128)(2,1)S(1)} %copy-done.23), channel_id=1, source_target_pairs={{0,4},{2,6},{4,0},{6,2},{1,5},{3,7},{5,1},{7,3},{8,12},{10,14},{12... | collective-permute-start | bytes 1572872 | tf_op jit(solution)/shard_map/ppermute | solution.py:606
  196.7 23.6 %collective-permute-done.12.refs_2_ = bf16[128,2048]{1,0:T(8,128)(2,1)S(1)} collective-permute-done((bf16[128,2048]{1,0:T(8,128)(2,1)S(1)}, bf16[128,2048]{1,0:T(8,128)(2,1)S(1)}, u32[]{:S(2)}, u32[]{:S(2)}) %collective-permute-start.12) | collective-permute-done | bytes 524320 | tf_op jit(solution)/shard_map/ppermute | solution.py:606
  221.9 4.0 %all-to-all-start.5 = ((bf16[8,1,40,2048]{3,2,1,0:T(8,128)(2,1)}), bf16[8,1,40,2048]{3,2,1,0:T(8,128)(2,1)S(1)}, u32[]{:S(2)}, u32[]{:S(2)}) async-start(bf16[8,1,40,2048]{3,2,1,0:T(8,128)(2,1)} %shard_map.250), calls=%async_computation.5 | async-start | bytes 2621440 | tf_op jit(solution)/shard_map/all_to_all | solution.py:589
  227.0 14.4 %shard_map.249.refs_0_ = bf16[8,1,40,2048]{3,2,1,0:T(8,128)(2,1)} custom-call(bf16[8,1,40,2048]{3,2,1,0:T(8,128)(2,1)} %shard_map.248.refs_0_, bf16[8,1,40,2048]{3,2,1,0:T(8,128)(2,1)} %all-to-all-done.4.refs_1_, bf16[320,320]{1,0:T(8,128)(2,1)} %constant.134.clone.refs_2_, bf16[320,320]{1,0:T(8,128)(2,1)} %constant.135.clone.refs_3_, ...), custom_call_target="tpu_custom_call" | custom-call | flops 4865392640 | bytes 27787264 | tf_op jit(solution)/shard_map/pallas_call | solution.py:478
  248.3 14.4 %shard_map.252.refs_0_ = bf16[8,1,40,2048]{3,2,1,0:T(8,128)(2,1)} custom-call(bf16[8,1,40,2048]{3,2,1,0:T(8,128)(2,1)} %shard_map.251.refs_0_, bf16[8,1,40,2048]{3,2,1,0:T(8,128)(2,1)} %copy-done.28, bf16[320,320]{1,0:T(8,128)(2,1)} %constant.134.clone.refs_2_, bf16[320,320]{1,0:T(8,128)(2,1)} %constant.135.clone.refs_3_, bf16[4,2048,512]{2,1,0:T(8,128)(2,1)} %refs_4_.9, ...), custom_call_target="tpu_custom_call" | custom-call | flops 4865392640 | bytes 27787264 | tf_op jit(solution)/shard_map/pallas_call | solution.py:478
  267.1 3.9 %all-to-all-start.7 = ((bf16[8,1,40,2048]{3,2,1,0:T(8,128)(2,1)}), bf16[8,1,40,2048]{3,2,1,0:T(8,128)(2,1)S(1)}, u32[]{:S(2)}, u32[]{:S(2)}) async-start(bf16[8,1,40,2048]{3,2,1,0:T(8,128)(2,1)} %shard_map.253), calls=%async_computation.7 | async-start | bytes 2621440 | tf_op jit(solution)/shard_map/all_to_all | solution.py:589
  275.0 14.4 %collective-permute-done.13.refs_2_ = bf16[128,2048]{1,0:T(8,128)(2,1)S(1)} collective-permute-done((bf16[128,2048]{1,0:T(8,128)(2,1)S(1)}, bf16[128,2048]{1,0:T(8,128)(2,1)S(1)}, u32[]{:S(2)}, u32[]{:S(2)}) %collective-permute-start.13) | collective-permute-done | bytes 524320 | tf_op jit(solution)/shard_map/ppermute | solution.py:606
  291.3 4.4 %all-to-all-start.8 = ((bf16[8,1,40,2048]{3,2,1,0:T(8,128)(2,1)}), bf16[8,1,40,2048]{3,2,1,0:T(8,128)(2,1)}, u32[]{:S(2)}, u32[]{:S(2)}) async-start(bf16[8,1,40,2048]{3,2,1,0:T(8,128)(2,1)} %shard_map.254), calls=%async_computation.8 | async-start | bytes 2621440 | tf_op jit(solution)/shard_map/all_to_all | solution.py:589
  297.9 10.6 %collective-permute-start.14 = (bf16[128,2048]{1,0:T(8,128)(2,1)}, bf16[128,2048]{1,0:T(8,128)(2,1)S(1)}, u32[]{:S(2)}, u32[]{:S(2)}) collective-permute-start(bf16[128,2048]{1,0:T(8,128)(2,1)} %fusion.4), channel_id=1, source_target_pairs={{0,4},{2,6},{4,0},{6,2},{1,5},{3,7},{5,1},{7,3},{8,12},{10,14},{12... | collective-permute-start | bytes 1572872 | tf_op jit(solution)/shard_map/ppermute | solution.py:606
  308.4 5.0 %all-to-all-done.8 = bf16[8,1,40,2048]{3,2,1,0:T(8,128)(2,1)} async-done(((bf16[8,1,40,2048]{3,2,1,0:T(8,128)(2,1)}), bf16[8,1,40,2048]{3,2,1,0:T(8,128)(2,1)}, u32[]{:S(2)}, u32[]{:S(2)}) %all-to-all-start.8) | async-done | bytes 1310752 | tf_op jit(solution)/shard_map/all_to_all | solution.py:589
  315.4 16.9 %collective-permute-done.14 = bf16[128,2048]{1,0:T(8,128)(2,1)S(1)} collective-permute-done((bf16[128,2048]{1,0:T(8,128)(2,1)}, bf16[128,2048]{1,0:T(8,128)(2,1)S(1)}, u32[]{:S(2)}, u32[]{:S(2)}) %collective-permute-start.14) | collective-permute-done | bytes 524320 | tf_op jit(solution)/shard_map/ppermute | solution.py:606
  (186 shorter events, 80.7 us)
Async XLA Ops:
  10.5 21.6 %collective-permute-start = (bf16[512,256]{1,0:T(8,128)(2,1)S(1)}, bf16[512,256]{1,0:T(8,128)(2,1)S(1)}, u32[]{:S(2)}, u32[]{:S(2)}) collective-permute-start(bf16[512,256]{1,0:T(8,128)(2,1)S(1)} %dynamic-slice_bitcast_fusion), channel_id=1, source_target_pairs={{0,1},{1,0},{2,3},{3,2},{4,5},{5,4},{6,7},{7,6},{8,9},{9,8},{10,11... | collective-permute-start | bytes 786440 | tf_op jit(solution)/shard_map/ppermute | solution.py:546
  13.5 17.5 %collective-permute-start.1 = (bf16[256,1024]{1,0:T(8,128)(2,1)S(1)}, bf16[256,1024]{1,0:T(8,128)(2,1)S(1)}, u32[]{:S(2)}, u32[]{:S(2)}) collective-permute-start(bf16[256,1024]{1,0:T(8,128)(2,1)S(1)} %constant_dynamic-slice_fusion), channel_id=1, source_target_pairs={{0,1},{1,0},{2,3},{3,2},{4,5},{5,4},{6,7},{7,6},{8,9},{9,8},{10,11... | collective-permute-start | bytes 1572872 | tf_op jit(solution)/shard_map/ppermute | solution.py:543
  14.1 27.0 %collective-permute-start.3 = (f32[2,16,128]{2,1,0:T(8,128)S(1)}, f32[2,16,128]{2,1,0:T(8,128)S(1)}, u32[]{:S(2)}, u32[]{:S(2)}) collective-permute-start(f32[2,16,128]{2,1,0:T(8,128)S(1)} %get-tuple-element.24), channel_id=1, source_target_pairs={{0,2},{2,0},{4,6},{6,4},{1,3},{3,1},{5,7},{7,5},{8,10},{10,8},{12,... | collective-permute-start | bytes 49160 | tf_op jit(solution)/shard_map/ppermute | solution.py:572
  16.2 24.8 %collective-permute-start.4 = (f32[2,16,128]{2,1,0:T(8,128)S(1)}, f32[2,16,128]{2,1,0:T(8,128)S(1)}, u32[]{:S(2)}, u32[]{:S(2)}) collective-permute-start(f32[2,16,128]{2,1,0:T(8,128)S(1)} %get-tuple-element.23), channel_id=1, source_target_pairs={{0,4},{2,6},{4,0},{6,2},{1,5},{3,7},{5,1},{7,3},{8,12},{10,14},{12... | collective-permute-start | bytes 49160 | tf_op jit(solution)/shard_map/ppermute | solution.py:572
  18.7 22.3 %collective-permute-start.5 = (f32[2,16,128]{2,1,0:T(8,128)S(1)}, f32[2,16,128]{2,1,0:T(8,128)S(1)}, u32[]{:S(2)}, u32[]{:S(2)}) collective-permute-start(f32[2,16,128]{2,1,0:T(8,128)S(1)} %get-tuple-element.22), channel_id=1, source_target_pairs={{0,6},{2,4},{4,2},{6,0},{1,7},{3,5},{5,3},{7,1},{8,14},{10,12},{12... | collective-permute-start | bytes 49160 | tf_op jit(solution)/shard_map/ppermute | solution.py:572
  31.8 2.1 collective-permute-start.2
  42.2 53.7 %all-to-all-start = ((bf16[4,128,2048]{2,1,0:T(8,128)(2,1)}), bf16[4,128,2048]{2,1,0:T(8,128)(2,1)S(1)}, u32[]{:S(2)}, u32[]{:S(2)}) async-start(bf16[4,128,2048]{2,1,0:T(8,128)(2,1)} %shard_map.242.refs_1_), calls=%async_computation | async-start | bytes 4194304 | tf_op jit(solution)/shard_map/all_to_all | solution.py:582
  53.1 8.6 %collective-permute-start.8 = (bf16[256,512]{1,0:T(8,128)(2,1)S(1)}, bf16[256,512]{1,0:T(8,128)(2,1)S(1)}, u32[]{:S(2)}, u32[]{:S(2)}) collective-permute-start(bf16[256,512]{1,0:T(8,128)(2,1)S(1)} %get-tuple-element.17), channel_id=1, source_target_pairs={{0,24},{8,16},{16,8},{24,0},{1,25},{9,17},{17,9},{25,1},{2,26},{10... | collective-permute-start | bytes 786440 | tf_op jit(solution)/shard_map/ppermute | solution.py:236
  54.1 13.2 %collective-permute-start.7 = (bf16[256,512]{1,0:T(8,128)(2,1)S(1)}, bf16[256,512]{1,0:T(8,128)(2,1)S(1)}, u32[]{:S(2)}, u32[]{:S(2)}) collective-permute-start(bf16[256,512]{1,0:T(8,128)(2,1)S(1)} %get-tuple-element.18), channel_id=1, source_target_pairs={{0,16},{8,24},{16,0},{24,8},{1,17},{9,25},{17,1},{25,9},{2,18},{10... | collective-permute-start | bytes 786440 | tf_op jit(solution)/shard_map/ppermute | solution.py:236
  54.7 12.6 %collective-permute-start.6 = (bf16[256,512]{1,0:T(8,128)(2,1)S(1)}, bf16[256,512]{1,0:T(8,128)(2,1)S(1)}, u32[]{:S(2)}, u32[]{:S(2)}) collective-permute-start(bf16[256,512]{1,0:T(8,128)(2,1)S(1)} %get-tuple-element.19), channel_id=1, source_target_pairs={{0,8},{8,0},{16,24},{24,16},{1,9},{9,1},{17,25},{25,17},{2,10},{10... | collective-permute-start | bytes 786440 | tf_op jit(solution)/shard_map/ppermute | solution.py:236
  100.9 21.5 %all-to-all-start.1 = ((bf16[8,1,40,2048]{3,2,1,0:T(8,128)(2,1)}), bf16[8,1,40,2048]{3,2,1,0:T(8,128)(2,1)S(1)}, u32[]{:S(2)}, u32[]{:S(2)}) async-start(bf16[8,1,40,2048]{3,2,1,0:T(8,128)(2,1)} %copy-done.11), calls=%async_computation.1 | async-start | bytes 2621440 | tf_op jit(solution)/shard_map/all_to_all | solution.py:589
  104.6 14.5 %collective-permute-start.9 = (bf16[128,2048]{1,0:T(8,128)(2,1)}, bf16[128,2048]{1,0:T(8,128)(2,1)S(1)}, u32[]{:S(2)}, u32[]{:S(2)}) collective-permute-start(bf16[128,2048]{1,0:T(8,128)(2,1)} %copy-done.22), channel_id=1, source_target_pairs={{0,2},{2,0},{4,6},{6,4},{1,3},{3,1},{5,7},{7,5},{8,10},{10,8},{12,... | collective-permute-start | bytes 1572872 | tf_op jit(solution)/shard_map/ppermute | solution.py:606
  123.9 21.2 %all-to-all-start.2 = ((bf16[8,1,40,2048]{3,2,1,0:T(8,128)(2,1)}), bf16[8,1,40,2048]{3,2,1,0:T(8,128)(2,1)S(1)}, u32[]{:S(2)}, u32[]{:S(2)}) async-start(bf16[8,1,40,2048]{3,2,1,0:T(8,128)(2,1)} %shard_map.245.refs_0_), calls=%async_computation.2 | async-start | bytes 2621440 | tf_op jit(solution)/shard_map/all_to_all | solution.py:589
  127.7 16.2 %collective-permute-start.10 = (bf16[128,2048]{1,0:T(8,128)(2,1)}, bf16[128,2048]{1,0:T(8,128)(2,1)S(1)}, u32[]{:S(2)}, u32[]{:S(2)}) collective-permute-start(bf16[128,2048]{1,0:T(8,128)(2,1)} %copy-done.22), channel_id=1, source_target_pairs={{0,6},{2,4},{4,2},{6,0},{1,7},{3,5},{5,3},{7,1},{8,14},{10,12},{12... | collective-permute-start | bytes 1572872 | tf_op jit(solution)/shard_map/ppermute | solution.py:606
  184.3 37.6 %all-to-all-start.4 = ((bf16[8,1,40,2048]{3,2,1,0:T(8,128)(2,1)}), bf16[8,1,40,2048]{3,2,1,0:T(8,128)(2,1)}, u32[]{:S(2)}, u32[]{:S(2)}) async-start(bf16[8,1,40,2048]{3,2,1,0:T(8,128)(2,1)} %copy-done.4), calls=%async_computation.4 | async-start | bytes 2621440 | tf_op jit(solution)/shard_map/all_to_all | solution.py:589
  188.6 31.7 %collective-permute-start.12 = (bf16[128,2048]{1,0:T(8,128)(2,1)S(1)}, bf16[128,2048]{1,0:T(8,128)(2,1)S(1)}, u32[]{:S(2)}, u32[]{:S(2)}) collective-permute-start(bf16[128,2048]{1,0:T(8,128)(2,1)S(1)} %copy-done.23), channel_id=1, source_target_pairs={{0,4},{2,6},{4,0},{6,2},{1,5},{3,7},{5,1},{7,3},{8,12},{10,14},{12... | collective-permute-start | bytes 1572872 | tf_op jit(solution)/shard_map/ppermute | solution.py:606
  221.9 21.7 %all-to-all-start.5 = ((bf16[8,1,40,2048]{3,2,1,0:T(8,128)(2,1)}), bf16[8,1,40,2048]{3,2,1,0:T(8,128)(2,1)S(1)}, u32[]{:S(2)}, u32[]{:S(2)}) async-start(bf16[8,1,40,2048]{3,2,1,0:T(8,128)(2,1)} %shard_map.250), calls=%async_computation.5 | async-start | bytes 2621440 | tf_op jit(solution)/shard_map/all_to_all | solution.py:589
  226.9 14.5 %collective-permute-start.11 = (bf16[128,2048]{1,0:T(8,128)(2,1)S(1)}, bf16[128,2048]{1,0:T(8,128)(2,1)S(1)}, u32[]{:S(2)}, u32[]{:S(2)}) collective-permute-start(bf16[128,2048]{1,0:T(8,128)(2,1)S(1)} %fusion.2), channel_id=1, source_target_pairs={{0,2},{2,0},{4,6},{6,4},{1,3},{3,1},{5,7},{7,5},{8,10},{10,8},{12,... | collective-permute-start | bytes 1572872 | tf_op jit(solution)/shard_map/ppermute | solution.py:606
  244.8 21.2 %all-to-all-start.6 = ((bf16[8,1,40,2048]{3,2,1,0:T(8,128)(2,1)}), bf16[8,1,40,2048]{3,2,1,0:T(8,128)(2,1)S(1)}, u32[]{:S(2)}, u32[]{:S(2)}) async-start(bf16[8,1,40,2048]{3,2,1,0:T(8,128)(2,1)} %shard_map.251.refs_0_), calls=%async_computation.6 | async-start | bytes 2621440 | tf_op jit(solution)/shard_map/all_to_all | solution.py:589
  267.1 22.3 %all-to-all-start.7 = ((bf16[8,1,40,2048]{3,2,1,0:T(8,128)(2,1)}), bf16[8,1,40,2048]{3,2,1,0:T(8,128)(2,1)S(1)}, u32[]{:S(2)}, u32[]{:S(2)}) async-start(bf16[8,1,40,2048]{3,2,1,0:T(8,128)(2,1)} %shard_map.253), calls=%async_computation.7 | async-start | bytes 2621440 | tf_op jit(solution)/shard_map/all_to_all | solution.py:589
  273.4 16.0 %collective-permute-start.13 = (bf16[128,2048]{1,0:T(8,128)(2,1)S(1)}, bf16[128,2048]{1,0:T(8,128)(2,1)S(1)}, u32[]{:S(2)}, u32[]{:S(2)}) collective-permute-start(bf16[128,2048]{1,0:T(8,128)(2,1)S(1)} %fusion.3), channel_id=1, source_target_pairs={{0,6},{2,4},{4,2},{6,0},{1,7},{3,5},{5,3},{7,1},{8,14},{10,12},{12... | collective-permute-start | bytes 1572872 | tf_op jit(solution)/shard_map/ppermute | solution.py:606
  291.3 22.1 %all-to-all-start.8 = ((bf16[8,1,40,2048]{3,2,1,0:T(8,128)(2,1)}), bf16[8,1,40,2048]{3,2,1,0:T(8,128)(2,1)}, u32[]{:S(2)}, u32[]{:S(2)}) async-start(bf16[8,1,40,2048]{3,2,1,0:T(8,128)(2,1)} %shard_map.254), calls=%async_computation.8 | async-start | bytes 2621440 | tf_op jit(solution)/shard_map/all_to_all | solution.py:589
  296.6 35.7 %copy-start.32 = (bf16[128,2048]{1,0:T(8,128)(2,1)S(1)}, bf16[128,2048]{1,0:T(8,128)(2,1)}, u32[]{:S(2)}) copy-start(bf16[128,2048]{1,0:T(8,128)(2,1)} %copy-done.31) | copy-start | bytes 1572868
  297.9 34.4 %collective-permute-start.14 = (bf16[128,2048]{1,0:T(8,128)(2,1)}, bf16[128,2048]{1,0:T(8,128)(2,1)S(1)}, u32[]{:S(2)}, u32[]{:S(2)}) collective-permute-start(bf16[128,2048]{1,0:T(8,128)(2,1)} %fusion.4), channel_id=1, source_target_pairs={{0,4},{2,6},{4,0},{6,2},{1,5},{3,7},{5,1},{7,3},{8,12},{10,14},{12... | collective-permute-start | bytes 1572872 | tf_op jit(solution)/shard_map/ppermute | solution.py:606
  (48 other events, 341.1 us)

commit v7 on v5

--- a/solution.py
+++ b/solution.py
@@ -292,7 +292,7 @@
         ],
         out_specs=pl.BlockSpec((2, tok_rows, width), lambda i: (0, i, 0)),
         out_shape=jax.ShapeDtypeStruct((2, rows // 2, width), jnp.bfloat16),
-        compiler_params=pltpu.CompilerParams(vmem_limit_bytes=56 * 1024 * 1024),
+        compiler_params=pltpu.CompilerParams(vmem_limit_bytes=40 * 1024 * 1024),
         cost_estimate=pl.CostEstimate(
             flops=4 * rows * rows * width,
             bytes_accessed=8 * rows * width,
@@ -389,7 +389,8 @@
     )(*after, *operands)
 
 
-def pack_kernel(after_ref, picking_ref, block_ref, out_ref):
+def pack_kernel(*refs):
+    picking_ref, block_ref, out_ref = refs[-3:]
     out_ref[:, 0] = pack_rows(
         picking_ref[...], block_ref[...], (out_ref.shape[0],) + out_ref.shape[2:]
     )
@@ -401,8 +402,8 @@
     return pl.pallas_call(
         pack_kernel,
         grid=(1,),
-        in_specs=[
-            pl.BlockSpec(memory_space=pl.ANY),
+        in_specs=[pl.BlockSpec(memory_space=pl.ANY)] * len(after)
+        + [
             pl.BlockSpec((height, tok_rows), lambda i: (0, 0)),
             pl.BlockSpec((tok_rows, D), lambda i: (0, 0)),
         ],
@@ -413,7 +414,7 @@
         cost_estimate=pl.CostEstimate(
             flops=2 * height * tok_rows * D, bytes_accessed=4 * height * D, transcendentals=0
         ),
-    )(after, picking, block)
+    )(*after, picking, block)
 
 
 def tie_kernel(*refs):
@@ -544,7 +545,7 @@
     other_weight = lax.ppermute(half, "x", swap)
     attended = attend_columns(queries, keys, values, segment_ids[0], tok_rows)
     leaving = lax.dynamic_index_in_dim(attended, 1 - column, 0, keepdims=False)
-    other = lax.ppermute(leaving, "x", swap)
+    other = lax.ppermute(tie(leaving, other_weight), "x", swap)
     other_weight = tie(other_weight, attended)
     other_rest = lax.ppermute(other_weight, "req", cores)
 
@@ -557,7 +558,6 @@
         other_rest,
     )
 
-    routes = tie(routes, partial)
     matched = routes[:, :, None] == jnp.arange(EXPERTS, dtype=jnp.int32)[None, None, :]
     named = jnp.any(matched, axis=1)
     weight_of = jnp.sum(jnp.where(matched, combine[:, :, None], 0.0), axis=1)
@@ -568,11 +568,13 @@
     tables = tables.reshape(2, groups, PLANES, 2 * lanes, tok_rows)
     tables = jnp.transpose(tables, (2, 0, 1, 3, 4)).reshape(PLANES, 2, plane_experts, tok_rows)
     lines = jnp.arange(height, dtype=jnp.float32)
-    pickings, mixings = [], []
+    received = []
     for turn in range(PLANES):
         table = lax.dynamic_index_in_dim(tables, level ^ turn, 0, keepdims=False)
-        if turn:
-            table = lax.ppermute(table, "z", pairs[turn])
+        received.append(lax.ppermute(table, "z", pairs[turn]) if turn else table)
+    partial = tie(partial, *received[1:])
+    pickings, mixings = [], []
+    for table in received:
         hits = table[0][:, None, :] == lines[None, :, None]
         pickings.append(jnp.sum(hits.astype(jnp.float32), axis=0).astype(jnp.bfloat16))
         mixing = jnp.sum(jnp.where(hits, table[1][:, None, :], 0.0), axis=0)
@@ -607,12 +609,13 @@
 
     blocks = [normed] + [to_plane(turn, normed) for turn in range(1, PLANES)]
     own = exchange(packed)
-    packed_first = pack_after(own, pickings[1], blocks[1], sources)
+    packed_first = pack_after([own], pickings[1], blocks[1], sources)
     first = exchange(packed_first)
-    packed_third = pack_after(first, pickings[3], blocks[3], sources)
+    outs_own = experts([packed_first], own)
+    packed_third = pack_after([first, outs_own], pickings[3], blocks[3], sources)
     third = exchange(packed_third)
     outs_first = experts([packed_third], first, 2)
-    outs_first = pack_after(outs_first, pickings[2], blocks[2], sources, into=True)
+    outs_first = pack_after([outs_first], pickings[2], blocks[2], sources, into=True)
     second = exchange(outs_first)
     outs_third = experts([outs_first], third)
     back_third = exchange(outs_third)
@@ -622,11 +625,9 @@
     outs_second = tie(outs_second, got_first)
     back_second = exchange(outs_second)
     share_third = mixed(3, tie(back_third, outs_second)).astype(jnp.bfloat16)
-    outs_own = experts([share_third], own)
     got_third = to_plane(3, share_third)
-    outs_own = tie(outs_own, got_third)
-    back_own = exchange(outs_own)
-    share_second = mixed(2, tie(back_second, outs_own)).astype(jnp.bfloat16)
+    back_own = exchange(tie(outs_own, back_second))
+    share_second = mixed(2, tie(back_second, got_third)).astype(jnp.bfloat16)
     got_second = to_plane(2, share_second)
     total = residual + got_first.astype(jnp.float32) + got_third.astype(jnp.float32)
     total = total + mixed(0, back_own) + got_second.astype(jnp.float32)

time: 322 us -> 327 us (1.016)
  waiting for transfers between devices: 134 us -> 139 us
  starting transfers between devices: 67.8 us -> 62.9 us
    ppermute x4, waiting for transfers between devices: 32.7 us -> 8.53 us  [the longest x1 8.52 us: on_device_whole(): other = lax.ppermute(tie(leaving, other_weight), 'x', swap)]
    all_to_all x1, waiting for transfers between devices: 0.01 us -> 24 us  [on_device_whole(): lax.all_to_all(partial, 'z', split_axis=0, concat_axis=0, tiled=True)]
    ppermute x1, waiting for transfers between devices: 16.7 us -> 0.01 us  [on_device_whole(): other_weight = lax.ppermute(half, 'x', swap)]
    all_to_all x7, waiting for transfers between devices: 25.7 us -> 35.9 us  [exchange(): lax.all_to_all(block, ('req', 'x'), split_axis=0, concat_axis=0, tiled=True)]
    ppermute x3, waiting for transfers between devices: 0.01 us -> 10.1 us  [move_pages(): incoming.append(lax.ppermute(sent[apart], 'req', pairs))]
    ppermute x4, starting transfers between devices: 11.2 us -> 4.83 us  [the longest x3 4.45 us: on_device_whole(): received.append(lax.ppermute(table, 'z', pairs[turn]) if turn else table)]
    unnamed x79 -> x92, local copies, waits for them, and re-layouts: 17.9 us -> 20.9 us
  transfers between devices with their start and end apart: 23 -> 23, of which waited for: 12 -> 13; matrix products, arithmetic and copies ran while one was open for 8% -> 9% of each run, Pallas kernels for 18% -> 20%
where the time goes in v7:
time: 327 us; the launch traced here: 326 us
  waiting for transfers between devices  139 us (43%)
  Pallas kernels  70.1 us (21%)
  starting transfers between devices  62.9 us (19%)
  local copies, waits for them, and re-layouts  29.9 us (9%)
  matrix products  13.4 us (4%)
  other arithmetic  8.89 us (3%)
    ppermute x6, waiting for transfers between devices, to_plane(): return lax.ppermute(block, 'z', pairs[turn])  60.7 us
    pallas_call x4, Pallas kernels, run_experts(): pl.pallas_call(expert_kernel, grid=(4,), in_specs=[pl.BlockSpec(memory_sp...  56.8 us
    all_to_all x7, waiting for transfers between devices, exchange(): lax.all_to_all(block, ('req', 'x'), split_axis=0, concat_axis=0, tiled=True)  35.9 us
    all_to_all x7, starting transfers between devices, exchange(): lax.all_to_all(block, ('req', 'x'), split_axis=0, concat_axis=0, tiled=True)  26.2 us
    all_to_all x1, waiting for transfers between devices, on_device_whole(): lax.all_to_all(partial, 'z', split_axis=0, concat_axis=0, tiled=True)  24 us
    ppermute x6, starting transfers between devices, to_plane(): return lax.ppermute(block, 'z', pairs[turn])  21.9 us
    unnamed x92, local copies, waits for them, and re-layouts  20.9 us
    ppermute x3, waiting for transfers between devices, move_pages(): incoming.append(lax.ppermute(sent[apart], 'req', pairs))  10.1 us
  transfers between devices with their start and end apart: 23, of which 13 were waited for; matrix products, arithmetic and copies ran while one was open for 9% of the time, Pallas kernels for 20%

profile of v7, /device:TPU:0, one launch (start us, length us, event | category | flops | bytes accessed | tf_op | source)
XLA Modules:
  0.0 325.7 jit_solution(16257148460982311960)
XLA Ops:
  15.0 5.0 %shard_map.239.refs_1_.mine_ref = bf16[2,512,256]{2,1,0:T(8,128)(2,1)S(1)} custom-call(bf16[1024,256]{1,0:T(8,128)(2,1)S(1)} %copy-done.18, bf16[1024,256]{1,0:T(8,128)(2,1)S(1)} %copy-done.19, bf16[1024,256]{1,0:T(8,128)(2,1)S(1)} %copy-done.20, s32[1024,1]{1,0:T(8,128)S(1)} %copy.43.line_ref, s32[1,1024]{1,0:T(1,128)S(1)} %copy-done.17), custom_call_target="tpu_custom_call" | custom-call | flops 1073741824 | bytes 2097152 | tf_op jit(solution)/shard_map/pallas_call | solution.py:283
  22.5 8.5 %collective-permute-done.1.other_ref = bf16[512,256]{1,0:T(8,128)(2,1)S(1)} collective-permute-done((bf16[512,256]{1,0:T(8,128)(2,1)}, bf16[512,256]{1,0:T(8,128)(2,1)S(1)}, u32[]{:S(2)}, u32[]{:S(2)}) %collective-permute-start.1) | collective-permute-done | bytes 262176 | tf_op jit(solution)/shard_map/ppermute | solution.py:548
  33.1 3.6 %shard_map.242.refs_0_ = bf16[4,128,2048]{2,1,0:T(8,128)(2,1)S(1)} custom-call(s32[2]{0:T(128)S(1)} %pad_add_fusion.place_ref, bf16[2,512,256]{2,1,0:T(8,128)(2,1)S(1)} %copy-done.10, bf16[512,256]{1,0:T(8,128)(2,1)S(1)} %collective-permute-done.1.other_ref, bf16[256,2048]{1,0:T(8,128)(2,1)S(1)} %copy-done.11, bf16[256,1024]{1,0:T(8,128)(2,1)S(1)} %copy-done.7, ...), custom_call_target="tpu_custom_call" | custom-call | flops 1073741824 | bytes 4194304 | tf_op jit(solution)/shard_map/pallas_call | solution.py:323
  39.3 5.0 %all-to-all-start = ((bf16[4,128,2048]{2,1,0:T(8,128)(2,1)}), bf16[4,128,2048]{2,1,0:T(8,128)(2,1)S(1)}, u32[]{:S(2)}, u32[]{:S(2)}) async-start(bf16[4,128,2048]{2,1,0:T(8,128)(2,1)} %shard_map.243.refs_1_), calls=%async_computation | async-start | bytes 4194304 | tf_op jit(solution)/shard_map/all_to_all | solution.py:584
  54.4 4.4 %collective-permute-done.8 = bf16[256,512]{1,0:T(8,128)(2,1)S(1)} collective-permute-done((bf16[256,512]{1,0:T(8,128)(2,1)S(1)}, bf16[256,512]{1,0:T(8,128)(2,1)S(1)}, u32[]{:S(2)}, u32[]{:S(2)}) %collective-permute-start.8) | collective-permute-done | bytes 262176 | tf_op jit(solution)/shard_map/ppermute | solution.py:236
  58.8 5.7 %collective-permute-done.7 = bf16[256,512]{1,0:T(8,128)(2,1)S(1)} collective-permute-done((bf16[256,512]{1,0:T(8,128)(2,1)S(1)}, bf16[256,512]{1,0:T(8,128)(2,1)S(1)}, u32[]{:S(2)}, u32[]{:S(2)}) %collective-permute-start.7) | collective-permute-done | bytes 262176 | tf_op jit(solution)/shard_map/ppermute | solution.py:236
  68.4 24.0 %all-to-all-done.refs_5_ = bf16[4,128,2048]{2,1,0:T(8,128)(2,1)S(1)} async-done(((bf16[4,128,2048]{2,1,0:T(8,128)(2,1)}), bf16[4,128,2048]{2,1,0:T(8,128)(2,1)S(1)}, u32[]{:S(2)}, u32[]{:S(2)}) %all-to-all-start) | async-done | bytes 2097184 | tf_op jit(solution)/shard_map/all_to_all | solution.py:584
  100.9 14.4 %collective-permute-done.9.refs_2_ = bf16[128,2048]{1,0:T(8,128)(2,1)S(1)} collective-permute-done((bf16[128,2048]{1,0:T(8,128)(2,1)}, bf16[128,2048]{1,0:T(8,128)(2,1)S(1)}, u32[]{:S(2)}, u32[]{:S(2)}) %collective-permute-start.9) | collective-permute-done | bytes 524320 | tf_op jit(solution)/shard_map/ppermute | solution.py:608
  120.1 3.8 %all-to-all-start.2 = ((bf16[8,1,40,2048]{3,2,1,0:T(8,128)(2,1)}), bf16[8,1,40,2048]{3,2,1,0:T(8,128)(2,1)S(1)}, u32[]{:S(2)}, u32[]{:S(2)}) async-start(bf16[8,1,40,2048]{3,2,1,0:T(8,128)(2,1)} %shard_map.246.refs_0_), calls=%async_computation.2 | async-start | bytes 2621440 | tf_op jit(solution)/shard_map/all_to_all | solution.py:591
  125.4 14.4 %shard_map.247.refs_1_.refs_0_ = bf16[8,1,40,2048]{3,2,1,0:T(8,128)(2,1)} custom-call(bf16[8,1,40,2048]{3,2,1,0:T(8,128)(2,1)} %shard_map.246.refs_0_, bf16[8,1,40,2048]{3,2,1,0:T(8,128)(2,1)} %copy-done.4, bf16[320,320]{1,0:T(8,128)(2,1)} %constant.134.clone.refs_2_.refs_3_, bf16[320,320]{1,0:T(8,128)(2,1)} %constant.135.clone.refs_3_.refs_4_, ...), custom_call_target="tpu_custom_call" | custom-call | flops 4865392640 | bytes 27787264 | tf_op jit(solution)/shard_map/pallas_call | solution.py:480
  144.3 3.7 %all-to-all-start.4 = ((bf16[8,1,40,2048]{3,2,1,0:T(8,128)(2,1)}), bf16[8,1,40,2048]{3,2,1,0:T(8,128)(2,1)S(1)}, u32[]{:S(2)}, u32[]{:S(2)}) async-start(bf16[8,1,40,2048]{3,2,1,0:T(8,128)(2,1)} %shard_map.248.refs_0_), calls=%async_computation.4 | async-start | bytes 2621440 | tf_op jit(solution)/shard_map/all_to_all | solution.py:591
  148.0 8.0 %collective-permute-start.11 = (bf16[128,2048]{1,0:T(8,128)(2,1)S(1)}, bf16[128,2048]{1,0:T(8,128)(2,1)S(1)}, u32[]{:S(2)}, u32[]{:S(2)}) collective-permute-start(bf16[128,2048]{1,0:T(8,128)(2,1)S(1)} %copy-done.22), channel_id=1, source_target_pairs={{0,4},{2,6},{4,0},{6,2},{1,5},{3,7},{5,1},{7,3},{8,12},{10,14},{12... | collective-permute-start | bytes 1572872 | tf_op jit(solution)/shard_map/ppermute | solution.py:608
  156.0 14.3 %shard_map.249.refs_0_ = bf16[8,2,40,2048]{3,2,1,0:T(8,128)(2,1)} custom-call(bf16[8,1,40,2048]{3,2,1,0:T(8,128)(2,1)} %shard_map.248.refs_0_, bf16[8,1,40,2048]{3,2,1,0:T(8,128)(2,1)} %copy-done.5, bf16[320,320]{1,0:T(8,128)(2,1)} %constant.134.clone.refs_2_.refs_3_, bf16[320,320]{1,0:T(8,128)(2,1)} %constant.135.clone.refs_3_.refs_4_, ...), custom_call_target="tpu_custom_call" | custom-call | flops 4865392640 | bytes 27787264 | tf_op jit(solution)/shard_map/pallas_call | solution.py:480
  170.4 9.4 %collective-permute-done.11.refs_2_ = bf16[128,2048]{1,0:T(8,128)(2,1)S(1)} collective-permute-done((bf16[128,2048]{1,0:T(8,128)(2,1)S(1)}, bf16[128,2048]{1,0:T(8,128)(2,1)S(1)}, u32[]{:S(2)}, u32[]{:S(2)}) %collective-permute-start.11) | collective-permute-done | bytes 524320 | tf_op jit(solution)/shard_map/ppermute | solution.py:608
  184.6 3.8 %all-to-all-start.3 = ((bf16[8,2,40,2048]{3,2,1,0:T(8,128)(2,1)}), bf16[8,2,40,2048]{3,2,1,0:T(8,128)(2,1)S(1)}, u32[]{:S(2)}, u32[]{:S(2)}) async-start(bf16[8,2,40,2048]{3,2,1,0:T(8,128)(2,1)} %copy-done.1), calls=%async_computation.3 | async-start | bytes 5242880 | tf_op jit(solution)/shard_map/all_to_all | solution.py:591
  188.5 14.4 %shard_map.251.refs_0_ = bf16[8,1,40,2048]{3,2,1,0:T(8,128)(2,1)} custom-call(bf16[8,2,40,2048]{3,2,1,0:T(8,128)(2,1)} %copy-done.1, bf16[8,1,40,2048]{3,2,1,0:T(8,128)(2,1)} %copy-done.28, bf16[320,320]{1,0:T(8,128)(2,1)} %constant.134.clone.refs_2_.refs_3_, bf16[320,320]{1,0:T(8,128)(2,1)} %constant.135.clone.refs_3_.refs_4_, ...), custom_call_target="tpu_custom_call" | custom-call | flops 4865392640 | bytes 27787264 | tf_op jit(solution)/shard_map/pallas_call | solution.py:480
  202.9 17.4 %all-to-all-done.3.refs_2_ = bf16[8,2,40,2048]{3,2,1,0:T(8,128)(2,1)S(1)} async-done(((bf16[8,2,40,2048]{3,2,1,0:T(8,128)(2,1)}), bf16[8,2,40,2048]{3,2,1,0:T(8,128)(2,1)S(1)}, u32[]{:S(2)}, u32[]{:S(2)}) %all-to-all-start.3) | async-done | bytes 2621472 | tf_op jit(solution)/shard_map/all_to_all | solution.py:591
  228.5 13.7 %shard_map.252.refs_0_ = bf16[8,1,40,2048]{3,2,1,0:T(8,128)(2,1)} custom-call(bf16[8,1,40,2048]{3,2,1,0:T(8,128)(2,1)} %shard_map.251.refs_0_, bf16[128,2048]{1,0:T(8,128)(2,1)} %copy-done.29, bf16[8,2,40,2048]{3,2,1,0:T(8,128)(2,1)} %copy-done.27, bf16[320,320]{1,0:T(8,128)(2,1)} %constant.134.clone.refs_2_.refs_3_, ...), custom_call_target="tpu_custom_call" | custom-call | flops 4865392640 | bytes 27787264 | tf_op jit(solution)/shard_map/pallas_call | solution.py:480
  243.0 4.1 %all-to-all-start.6 = ((bf16[8,1,40,2048]{3,2,1,0:T(8,128)(2,1)}), bf16[8,1,40,2048]{3,2,1,0:T(8,128)(2,1)S(1)}, u32[]{:S(2)}, u32[]{:S(2)}) async-start(bf16[8,1,40,2048]{3,2,1,0:T(8,128)(2,1)} %shard_map.253.refs_1_), calls=%async_computation.6 | async-start | bytes 2621440 | tf_op jit(solution)/shard_map/all_to_all | solution.py:591
  250.9 14.0 %all-to-all-done.6.refs_1_.refs_0_ = bf16[8,1,40,2048]{3,2,1,0:T(8,128)(2,1)S(1)} async-done(((bf16[8,1,40,2048]{3,2,1,0:T(8,128)(2,1)}), bf16[8,1,40,2048]{3,2,1,0:T(8,128)(2,1)S(1)}, u32[]{:S(2)}, u32[]{:S(2)}) %all-to-all-start.6) | async-done | bytes 1310752 | tf_op jit(solution)/shard_map/all_to_all | solution.py:591
  266.0 3.7 %all-to-all-start.7 = ((bf16[8,1,40,2048]{3,2,1,0:T(8,128)(2,1)}), bf16[8,1,40,2048]{3,2,1,0:T(8,128)(2,1)S(1)}, u32[]{:S(2)}, u32[]{:S(2)}) async-start(bf16[8,1,40,2048]{3,2,1,0:T(8,128)(2,1)} %shard_map.255), calls=%async_computation.7 | async-start | bytes 2621440 | tf_op jit(solution)/shard_map/all_to_all | solution.py:591
  273.0 14.7 %collective-permute-done.13.refs_1_ = bf16[128,2048]{1,0:T(8,128)(2,1)S(1)} collective-permute-done((bf16[128,2048]{1,0:T(8,128)(2,1)S(1)}, bf16[128,2048]{1,0:T(8,128)(2,1)S(1)}, u32[]{:S(2)}, u32[]{:S(2)}) %collective-permute-start.13) | collective-permute-done | bytes 524320 | tf_op jit(solution)/shard_map/ppermute | solution.py:608
  290.9 10.7 %collective-permute-start.14 = (bf16[128,2048]{1,0:T(8,128)(2,1)S(1)}, bf16[128,2048]{1,0:T(8,128)(2,1)S(1)}, u32[]{:S(2)}, u32[]{:S(2)}) collective-permute-start(bf16[128,2048]{1,0:T(8,128)(2,1)S(1)} %fusion.4), channel_id=1, source_target_pairs={{0,4},{2,6},{4,0},{6,2},{1,5},{3,7},{5,1},{7,3},{8,12},{10,14},{12... | collective-permute-start | bytes 1572872 | tf_op jit(solution)/shard_map/ppermute | solution.py:608
  302.6 22.0 %collective-permute-done.14 = bf16[128,2048]{1,0:T(8,128)(2,1)S(1)} collective-permute-done((bf16[128,2048]{1,0:T(8,128)(2,1)S(1)}, bf16[128,2048]{1,0:T(8,128)(2,1)S(1)}, u32[]{:S(2)}, u32[]{:S(2)}) %collective-permute-start.14) | collective-permute-done | bytes 524320 | tf_op jit(solution)/shard_map/ppermute | solution.py:608
  (183 shorter events, 81.7 us)
Async XLA Ops:
  2.7 18.2 %collective-permute-start = (bf16[256,1024]{1,0:T(8,128)(2,1)}, bf16[256,1024]{1,0:T(8,128)(2,1)S(1)}, u32[]{:S(2)}, u32[]{:S(2)}) collective-permute-start(bf16[256,1024]{1,0:T(8,128)(2,1)} %constant_dynamic-slice_fusion), channel_id=1, source_target_pairs={{0,1},{1,0},{2,3},{3,2},{4,5},{5,4},{6,7},{7,6},{8,9},{9,8},{10,11... | collective-permute-start | bytes 1572872 | tf_op jit(solution)/shard_map/ppermute | solution.py:545
  8.8 29.2 %collective-permute-start.3 = (f32[2,16,128]{2,1,0:T(8,128)S(1)}, f32[2,16,128]{2,1,0:T(8,128)S(1)}, u32[]{:S(2)}, u32[]{:S(2)}) collective-permute-start(f32[2,16,128]{2,1,0:T(8,128)S(1)} %get-tuple-element.24), channel_id=1, source_target_pairs={{0,2},{2,0},{4,6},{6,4},{1,3},{3,1},{5,7},{7,5},{8,10},{10,8},{12,... | collective-permute-start | bytes 49160 | tf_op jit(solution)/shard_map/ppermute | solution.py:574
  10.5 27.6 %collective-permute-start.4 = (f32[2,16,128]{2,1,0:T(8,128)S(1)}, f32[2,16,128]{2,1,0:T(8,128)S(1)}, u32[]{:S(2)}, u32[]{:S(2)}) collective-permute-start(f32[2,16,128]{2,1,0:T(8,128)S(1)} %get-tuple-element.23), channel_id=1, source_target_pairs={{0,4},{2,6},{4,0},{6,2},{1,5},{3,7},{5,1},{7,3},{8,12},{10,14},{12... | collective-permute-start | bytes 49160 | tf_op jit(solution)/shard_map/ppermute | solution.py:574
  13.1 25.0 %collective-permute-start.5 = (f32[2,16,128]{2,1,0:T(8,128)S(1)}, f32[2,16,128]{2,1,0:T(8,128)S(1)}, u32[]{:S(2)}, u32[]{:S(2)}) collective-permute-start(f32[2,16,128]{2,1,0:T(8,128)S(1)} %get-tuple-element.22), channel_id=1, source_target_pairs={{0,6},{2,4},{4,2},{6,0},{1,7},{3,5},{5,3},{7,1},{8,14},{10,12},{12... | collective-permute-start | bytes 49160 | tf_op jit(solution)/shard_map/ppermute | solution.py:574
  21.8 9.2 %collective-permute-start.2 = (bf16[256,1024]{1,0:T(8,128)(2,1)}, bf16[256,1024]{1,0:T(8,128)(2,1)S(1)}, u32[]{:S(2)}, u32[]{:S(2)}) collective-permute-start(bf16[256,1024]{1,0:T(8,128)(2,1)} %shard_map.241.first_ref), channel_id=1, source_target_pairs={{0,8},{8,0},{16,24},{24,16},{1,9},{9,1},{17,25},{25,17},{2,10},{10... | collective-permute-start | bytes 1572872 | tf_op jit(solution)/shard_map/ppermute | solution.py:550
  22.0 9.0 %collective-permute-start.1 = (bf16[512,256]{1,0:T(8,128)(2,1)}, bf16[512,256]{1,0:T(8,128)(2,1)S(1)}, u32[]{:S(2)}, u32[]{:S(2)}) collective-permute-start(bf16[512,256]{1,0:T(8,128)(2,1)} %shard_map.240), channel_id=1, source_target_pairs={{0,1},{1,0},{2,3},{3,2},{4,5},{5,4},{6,7},{7,6},{8,9},{9,8},{10,11... | collective-permute-start | bytes 786440 | tf_op jit(solution)/shard_map/ppermute | solution.py:548
  39.3 53.1 %all-to-all-start = ((bf16[4,128,2048]{2,1,0:T(8,128)(2,1)}), bf16[4,128,2048]{2,1,0:T(8,128)(2,1)S(1)}, u32[]{:S(2)}, u32[]{:S(2)}) async-start(bf16[4,128,2048]{2,1,0:T(8,128)(2,1)} %shard_map.243.refs_1_), calls=%async_computation | async-start | bytes 4194304 | tf_op jit(solution)/shard_map/all_to_all | solution.py:584
  50.2 8.6 %collective-permute-start.8 = (bf16[256,512]{1,0:T(8,128)(2,1)S(1)}, bf16[256,512]{1,0:T(8,128)(2,1)S(1)}, u32[]{:S(2)}, u32[]{:S(2)}) collective-permute-start(bf16[256,512]{1,0:T(8,128)(2,1)S(1)} %get-tuple-element.17), channel_id=1, source_target_pairs={{0,24},{8,16},{16,8},{24,0},{1,25},{9,17},{17,9},{25,1},{2,26},{10... | collective-permute-start | bytes 786440 | tf_op jit(solution)/shard_map/ppermute | solution.py:236
  50.8 13.7 %collective-permute-start.7 = (bf16[256,512]{1,0:T(8,128)(2,1)S(1)}, bf16[256,512]{1,0:T(8,128)(2,1)S(1)}, u32[]{:S(2)}, u32[]{:S(2)}) collective-permute-start(bf16[256,512]{1,0:T(8,128)(2,1)S(1)} %get-tuple-element.18), channel_id=1, source_target_pairs={{0,16},{8,24},{16,0},{24,8},{1,17},{9,25},{17,1},{25,9},{2,18},{10... | collective-permute-start | bytes 786440 | tf_op jit(solution)/shard_map/ppermute | solution.py:236
  51.9 12.6 %collective-permute-start.6 = (bf16[256,512]{1,0:T(8,128)(2,1)S(1)}, bf16[256,512]{1,0:T(8,128)(2,1)S(1)}, u32[]{:S(2)}, u32[]{:S(2)}) collective-permute-start(bf16[256,512]{1,0:T(8,128)(2,1)S(1)} %get-tuple-element.19), channel_id=1, source_target_pairs={{0,8},{8,0},{16,24},{24,16},{1,9},{9,1},{17,25},{25,17},{2,10},{10... | collective-permute-start | bytes 786440 | tf_op jit(solution)/shard_map/ppermute | solution.py:236
  68.3 28.9 %copy-start.8 = (bf16[64,16,2,256]{3,1,2,0:T(8,128)(2,1)}, bf16[64,16,2,256]{3,1,2,0:T(8,128)(2,1)S(1)}, u32[]{:S(2)}) copy-start(bf16[64,16,2,256]{3,1,2,0:T(8,128)(2,1)S(1)} %copy.47) | copy-start | bytes 3145732
  97.3 21.2 %all-to-all-start.1 = ((bf16[8,1,40,2048]{3,2,1,0:T(8,128)(2,1)}), bf16[8,1,40,2048]{3,2,1,0:T(8,128)(2,1)S(1)}, u32[]{:S(2)}, u32[]{:S(2)}) async-start(bf16[8,1,40,2048]{3,2,1,0:T(8,128)(2,1)} %copy-done.12), calls=%async_computation.1 | async-start | bytes 2621440 | tf_op jit(solution)/shard_map/all_to_all | solution.py:591
  100.8 14.5 %collective-permute-start.9 = (bf16[128,2048]{1,0:T(8,128)(2,1)}, bf16[128,2048]{1,0:T(8,128)(2,1)S(1)}, u32[]{:S(2)}, u32[]{:S(2)}) collective-permute-start(bf16[128,2048]{1,0:T(8,128)(2,1)} %copy-done.21), channel_id=1, source_target_pairs={{0,2},{2,0},{4,6},{6,4},{1,3},{3,1},{5,7},{7,5},{8,10},{10,8},{12,... | collective-permute-start | bytes 1572872 | tf_op jit(solution)/shard_map/ppermute | solution.py:608
  120.1 21.2 %all-to-all-start.2 = ((bf16[8,1,40,2048]{3,2,1,0:T(8,128)(2,1)}), bf16[8,1,40,2048]{3,2,1,0:T(8,128)(2,1)S(1)}, u32[]{:S(2)}, u32[]{:S(2)}) async-start(bf16[8,1,40,2048]{3,2,1,0:T(8,128)(2,1)} %shard_map.246.refs_0_), calls=%async_computation.2 | async-start | bytes 2621440 | tf_op jit(solution)/shard_map/all_to_all | solution.py:591
  123.9 16.2 %collective-permute-start.10 = (bf16[128,2048]{1,0:T(8,128)(2,1)}, bf16[128,2048]{1,0:T(8,128)(2,1)S(1)}, u32[]{:S(2)}, u32[]{:S(2)}) collective-permute-start(bf16[128,2048]{1,0:T(8,128)(2,1)} %copy-done.21), channel_id=1, source_target_pairs={{0,6},{2,4},{4,2},{6,0},{1,7},{3,5},{5,3},{7,1},{8,14},{10,12},{12... | collective-permute-start | bytes 1572872 | tf_op jit(solution)/shard_map/ppermute | solution.py:608
  144.3 39.2 %all-to-all-start.4 = ((bf16[8,1,40,2048]{3,2,1,0:T(8,128)(2,1)}), bf16[8,1,40,2048]{3,2,1,0:T(8,128)(2,1)S(1)}, u32[]{:S(2)}, u32[]{:S(2)}) async-start(bf16[8,1,40,2048]{3,2,1,0:T(8,128)(2,1)} %shard_map.248.refs_0_), calls=%async_computation.4 | async-start | bytes 2621440 | tf_op jit(solution)/shard_map/all_to_all | solution.py:591
  148.0 31.8 %collective-permute-start.11 = (bf16[128,2048]{1,0:T(8,128)(2,1)S(1)}, bf16[128,2048]{1,0:T(8,128)(2,1)S(1)}, u32[]{:S(2)}, u32[]{:S(2)}) collective-permute-start(bf16[128,2048]{1,0:T(8,128)(2,1)S(1)} %copy-done.22), channel_id=1, source_target_pairs={{0,4},{2,6},{4,0},{6,2},{1,5},{3,7},{5,1},{7,3},{8,12},{10,14},{12... | collective-permute-start | bytes 1572872 | tf_op jit(solution)/shard_map/ppermute | solution.py:608
  184.6 35.6 %all-to-all-start.3 = ((bf16[8,2,40,2048]{3,2,1,0:T(8,128)(2,1)}), bf16[8,2,40,2048]{3,2,1,0:T(8,128)(2,1)S(1)}, u32[]{:S(2)}, u32[]{:S(2)}) async-start(bf16[8,2,40,2048]{3,2,1,0:T(8,128)(2,1)} %copy-done.1), calls=%async_computation.3 | async-start | bytes 5242880 | tf_op jit(solution)/shard_map/all_to_all | solution.py:591
  221.7 21.3 %all-to-all-start.5 = ((bf16[8,1,40,2048]{3,2,1,0:T(8,128)(2,1)}), bf16[8,1,40,2048]{3,2,1,0:T(8,128)(2,1)S(1)}, u32[]{:S(2)}, u32[]{:S(2)}) async-start(bf16[8,1,40,2048]{3,2,1,0:T(8,128)(2,1)} %shard_map.251.refs_0_), calls=%async_computation.5 | async-start | bytes 2621440 | tf_op jit(solution)/shard_map/all_to_all | solution.py:591
  227.7 14.5 %collective-permute-start.12 = (bf16[128,2048]{1,0:T(8,128)(2,1)S(1)}, bf16[128,2048]{1,0:T(8,128)(2,1)S(1)}, u32[]{:S(2)}, u32[]{:S(2)}) collective-permute-start(bf16[128,2048]{1,0:T(8,128)(2,1)S(1)} %fusion.2.refs_1_), channel_id=1, source_target_pairs={{0,2},{2,0},{4,6},{6,4},{1,3},{3,1},{5,7},{7,5},{8,10},{10,8},{12,... | collective-permute-start | bytes 1572872 | tf_op jit(solution)/shard_map/ppermute | solution.py:608
  243.0 21.8 %all-to-all-start.6 = ((bf16[8,1,40,2048]{3,2,1,0:T(8,128)(2,1)}), bf16[8,1,40,2048]{3,2,1,0:T(8,128)(2,1)S(1)}, u32[]{:S(2)}, u32[]{:S(2)}) async-start(bf16[8,1,40,2048]{3,2,1,0:T(8,128)(2,1)} %shard_map.253.refs_1_), calls=%async_computation.6 | async-start | bytes 2621440 | tf_op jit(solution)/shard_map/all_to_all | solution.py:591
  266.0 35.6 %all-to-all-start.7 = ((bf16[8,1,40,2048]{3,2,1,0:T(8,128)(2,1)}), bf16[8,1,40,2048]{3,2,1,0:T(8,128)(2,1)S(1)}, u32[]{:S(2)}, u32[]{:S(2)}) async-start(bf16[8,1,40,2048]{3,2,1,0:T(8,128)(2,1)} %shard_map.255), calls=%async_computation.7 | async-start | bytes 2621440 | tf_op jit(solution)/shard_map/all_to_all | solution.py:591
  271.4 16.2 %collective-permute-start.13 = (bf16[128,2048]{1,0:T(8,128)(2,1)S(1)}, bf16[128,2048]{1,0:T(8,128)(2,1)S(1)}, u32[]{:S(2)}, u32[]{:S(2)}) collective-permute-start(bf16[128,2048]{1,0:T(8,128)(2,1)S(1)} %fusion.3), channel_id=1, source_target_pairs={{0,6},{2,4},{4,2},{6,0},{1,7},{3,5},{5,3},{7,1},{8,14},{10,12},{12... | collective-permute-start | bytes 1572872 | tf_op jit(solution)/shard_map/ppermute | solution.py:608
  290.9 33.7 %collective-permute-start.14 = (bf16[128,2048]{1,0:T(8,128)(2,1)S(1)}, bf16[128,2048]{1,0:T(8,128)(2,1)S(1)}, u32[]{:S(2)}, u32[]{:S(2)}) collective-permute-start(bf16[128,2048]{1,0:T(8,128)(2,1)S(1)} %fusion.4), channel_id=1, source_target_pairs={{0,4},{2,6},{4,0},{6,2},{1,5},{3,7},{5,1},{7,3},{8,12},{10,14},{12... | collective-permute-start | bytes 1572872 | tf_op jit(solution)/shard_map/ppermute | solution.py:608
  (45 other events, 286.3 us)

commit v8 on v7

--- a/solution.py
+++ b/solution.py
@@ -611,8 +611,7 @@
     own = exchange(packed)
     packed_first = pack_after([own], pickings[1], blocks[1], sources)
     first = exchange(packed_first)
-    outs_own = experts([packed_first], own)
-    packed_third = pack_after([first, outs_own], pickings[3], blocks[3], sources)
+    packed_third = pack_after([first], pickings[3], blocks[3], sources)
     third = exchange(packed_third)
     outs_first = experts([packed_third], first, 2)
     outs_first = pack_after([outs_first], pickings[2], blocks[2], sources, into=True)
@@ -625,9 +624,11 @@
     outs_second = tie(outs_second, got_first)
     back_second = exchange(outs_second)
     share_third = mixed(3, tie(back_third, outs_second)).astype(jnp.bfloat16)
+    outs_own = experts([share_third], own)
     got_third = to_plane(3, share_third)
-    back_own = exchange(tie(outs_own, back_second))
-    share_second = mixed(2, tie(back_second, got_third)).astype(jnp.bfloat16)
+    outs_own = tie(outs_own, got_third)
+    back_own = exchange(outs_own)
+    share_second = mixed(2, tie(back_second, outs_own)).astype(jnp.bfloat16)
     got_second = to_plane(2, share_second)
     total = residual + got_first.astype(jnp.float32) + got_third.astype(jnp.float32)
     total = total + mixed(0, back_own) + got_second.astype(jnp.float32)

time: 327 us -> 310 us (0.948)
  waiting for transfers between devices: 139 us -> 126 us
    all_to_all x7, waiting for transfers between devices: 35.9 us -> 25.7 us  [exchange(): lax.all_to_all(block, ('req', 'x'), split_axis=0, concat_axis=0, tiled=True)]
    unnamed x92 -> x94, local copies, waits for them, and re-layouts: 20.9 us -> 20.5 us
  transfers between devices with their start and end apart: 23 -> 23, of which waited for: 13 -> 13; matrix products, arithmetic and copies ran while one was open for 9% -> 8% of each run, Pallas kernels for 20% -> 21%
where the time goes in v8:
time: 310 us; the launch traced here: 309 us
  waiting for transfers between devices  126 us (41%)
  Pallas kernels  69.1 us (22%)
  starting transfers between devices  62.9 us (20%)
  local copies, waits for them, and re-layouts  29.5 us (10%)
  matrix products  11.1 us (4%)
  other arithmetic  8.94 us (3%)
    ppermute x6, waiting for transfers between devices, to_plane(): return lax.ppermute(block, 'z', pairs[turn])  58 us
    pallas_call x4, Pallas kernels, run_experts(): pl.pallas_call(expert_kernel, grid=(4,), in_specs=[pl.BlockSpec(memory_sp...  56.9 us
    all_to_all x7, starting transfers between devices, exchange(): lax.all_to_all(block, ('req', 'x'), split_axis=0, concat_axis=0, tiled=True)  26.4 us
    all_to_all x7, waiting for transfers between devices, exchange(): lax.all_to_all(block, ('req', 'x'), split_axis=0, concat_axis=0, tiled=True)  25.7 us
    all_to_all x1, waiting for transfers between devices, on_device_whole(): lax.all_to_all(partial, 'z', split_axis=0, concat_axis=0, tiled=True)  23.9 us
    ppermute x6, starting transfers between devices, to_plane(): return lax.ppermute(block, 'z', pairs[turn])  21.7 us
    unnamed x94, local copies, waits for them, and re-layouts  20.5 us
    ppermute x3, waiting for transfers between devices, move_pages(): incoming.append(lax.ppermute(sent[apart], 'req', pairs))  10.1 us
  transfers between devices with their start and end apart: 23, of which 13 were waited for; matrix products, arithmetic and copies ran while one was open for 8% of the time, Pallas kernels for 21%

profile of v8, /device:TPU:0, one launch (start us, length us, event | category | flops | bytes accessed | tf_op | source)
XLA Modules:
  0.0 308.9 jit_solution(10884780032469860970)
XLA Ops:
  15.0 5.0 %shard_map.239.refs_1_.mine_ref = bf16[2,512,256]{2,1,0:T(8,128)(2,1)S(1)} custom-call(bf16[1024,256]{1,0:T(8,128)(2,1)S(1)} %copy-done.18, bf16[1024,256]{1,0:T(8,128)(2,1)S(1)} %copy-done.19, bf16[1024,256]{1,0:T(8,128)(2,1)S(1)} %copy-done.20, s32[1024,1]{1,0:T(8,128)S(1)} %copy.43.line_ref, s32[1,1024]{1,0:T(1,128)S(1)} %copy-done.17), custom_call_target="tpu_custom_call" | custom-call | flops 1073741824 | bytes 2097152 | tf_op jit(solution)/shard_map/pallas_call | solution.py:283
  22.5 8.5 %collective-permute-done.1.other_ref = bf16[512,256]{1,0:T(8,128)(2,1)S(1)} collective-permute-done((bf16[512,256]{1,0:T(8,128)(2,1)}, bf16[512,256]{1,0:T(8,128)(2,1)S(1)}, u32[]{:S(2)}, u32[]{:S(2)}) %collective-permute-start.1) | collective-permute-done | bytes 262176 | tf_op jit(solution)/shard_map/ppermute | solution.py:548
  33.1 3.6 %shard_map.242.refs_0_ = bf16[4,128,2048]{2,1,0:T(8,128)(2,1)S(1)} custom-call(s32[2]{0:T(128)S(1)} %pad_add_fusion.place_ref, bf16[2,512,256]{2,1,0:T(8,128)(2,1)S(1)} %copy-done.10, bf16[512,256]{1,0:T(8,128)(2,1)S(1)} %collective-permute-done.1.other_ref, bf16[256,2048]{1,0:T(8,128)(2,1)S(1)} %copy-done.11, bf16[256,1024]{1,0:T(8,128)(2,1)S(1)} %copy-done.7, ...), custom_call_target="tpu_custom_call" | custom-call | flops 1073741824 | bytes 4194304 | tf_op jit(solution)/shard_map/pallas_call | solution.py:323
  39.3 5.0 %all-to-all-start = ((bf16[4,128,2048]{2,1,0:T(8,128)(2,1)}), bf16[4,128,2048]{2,1,0:T(8,128)(2,1)S(1)}, u32[]{:S(2)}, u32[]{:S(2)}) async-start(bf16[4,128,2048]{2,1,0:T(8,128)(2,1)} %shard_map.243.refs_1_), calls=%async_computation | async-start | bytes 4194304 | tf_op jit(solution)/shard_map/all_to_all | solution.py:584
  54.5 4.4 %collective-permute-done.8 = bf16[256,512]{1,0:T(8,128)(2,1)S(1)} collective-permute-done((bf16[256,512]{1,0:T(8,128)(2,1)S(1)}, bf16[256,512]{1,0:T(8,128)(2,1)S(1)}, u32[]{:S(2)}, u32[]{:S(2)}) %collective-permute-start.8) | collective-permute-done | bytes 262176 | tf_op jit(solution)/shard_map/ppermute | solution.py:236
  58.9 5.7 %collective-permute-done.7 = bf16[256,512]{1,0:T(8,128)(2,1)S(1)} collective-permute-done((bf16[256,512]{1,0:T(8,128)(2,1)S(1)}, bf16[256,512]{1,0:T(8,128)(2,1)S(1)}, u32[]{:S(2)}, u32[]{:S(2)}) %collective-permute-start.7) | collective-permute-done | bytes 262176 | tf_op jit(solution)/shard_map/ppermute | solution.py:236
  68.4 23.9 %all-to-all-done.refs_5_ = bf16[4,128,2048]{2,1,0:T(8,128)(2,1)S(1)} async-done(((bf16[4,128,2048]{2,1,0:T(8,128)(2,1)}), bf16[4,128,2048]{2,1,0:T(8,128)(2,1)S(1)}, u32[]{:S(2)}, u32[]{:S(2)}) %all-to-all-start) | async-done | bytes 2097184 | tf_op jit(solution)/shard_map/all_to_all | solution.py:584
  97.3 3.6 %all-to-all-start.1 = ((bf16[8,1,40,2048]{3,2,1,0:T(8,128)(2,1)}), bf16[8,1,40,2048]{3,2,1,0:T(8,128)(2,1)S(1)}, u32[]{:S(2)}, u32[]{:S(2)}) async-start(bf16[8,1,40,2048]{3,2,1,0:T(8,128)(2,1)} %copy-done.12), calls=%async_computation.1 | async-start | bytes 2621440 | tf_op jit(solution)/shard_map/all_to_all | solution.py:591
  100.9 14.4 %collective-permute-done.9.refs_2_ = bf16[128,2048]{1,0:T(8,128)(2,1)S(1)} collective-permute-done((bf16[128,2048]{1,0:T(8,128)(2,1)}, bf16[128,2048]{1,0:T(8,128)(2,1)S(1)}, u32[]{:S(2)}, u32[]{:S(2)}) %collective-permute-start.9) | collective-permute-done | bytes 524320 | tf_op jit(solution)/shard_map/ppermute | solution.py:608
  125.3 14.8 %collective-permute-done.10.refs_2_ = bf16[128,2048]{1,0:T(8,128)(2,1)S(1)} collective-permute-done((bf16[128,2048]{1,0:T(8,128)(2,1)}, bf16[128,2048]{1,0:T(8,128)(2,1)S(1)}, u32[]{:S(2)}, u32[]{:S(2)}) %collective-permute-start.10) | collective-permute-done | bytes 524320 | tf_op jit(solution)/shard_map/ppermute | solution.py:608
  143.0 3.9 %all-to-all-start.4 = ((bf16[8,1,40,2048]{3,2,1,0:T(8,128)(2,1)}), bf16[8,1,40,2048]{3,2,1,0:T(8,128)(2,1)S(1)}, u32[]{:S(2)}, u32[]{:S(2)}) async-start(bf16[8,1,40,2048]{3,2,1,0:T(8,128)(2,1)} %shard_map.247.refs_0_), calls=%async_computation.4 | async-start | bytes 2621440 | tf_op jit(solution)/shard_map/all_to_all | solution.py:591
  146.9 7.8 %collective-permute-start.11 = (bf16[128,2048]{1,0:T(8,128)(2,1)S(1)}, bf16[128,2048]{1,0:T(8,128)(2,1)S(1)}, u32[]{:S(2)}, u32[]{:S(2)}) collective-permute-start(bf16[128,2048]{1,0:T(8,128)(2,1)S(1)} %copy-done.22), channel_id=1, source_target_pairs={{0,4},{2,6},{4,0},{6,2},{1,5},{3,7},{5,1},{7,3},{8,12},{10,14},{12... | collective-permute-start | bytes 1572872 | tf_op jit(solution)/shard_map/ppermute | solution.py:608
  154.7 14.4 %shard_map.248.refs_0_ = bf16[8,2,40,2048]{3,2,1,0:T(8,128)(2,1)} custom-call(bf16[8,1,40,2048]{3,2,1,0:T(8,128)(2,1)} %shard_map.247.refs_0_, bf16[8,1,40,2048]{3,2,1,0:T(8,128)(2,1)} %copy-done.4, bf16[320,320]{1,0:T(8,128)(2,1)} %constant.134.clone.refs_2_.refs_3_, bf16[320,320]{1,0:T(8,128)(2,1)} %constant.135.clone.refs_3_.refs_4_, ...), custom_call_target="tpu_custom_call" | custom-call | flops 4865392640 | bytes 27787264 | tf_op jit(solution)/shard_map/pallas_call | solution.py:480
  169.1 9.4 %collective-permute-done.11.refs_2_ = bf16[128,2048]{1,0:T(8,128)(2,1)S(1)} collective-permute-done((bf16[128,2048]{1,0:T(8,128)(2,1)S(1)}, bf16[128,2048]{1,0:T(8,128)(2,1)S(1)}, u32[]{:S(2)}, u32[]{:S(2)}) %collective-permute-start.11) | collective-permute-done | bytes 524320 | tf_op jit(solution)/shard_map/ppermute | solution.py:608
  183.3 3.8 %all-to-all-start.3 = ((bf16[8,2,40,2048]{3,2,1,0:T(8,128)(2,1)}), bf16[8,2,40,2048]{3,2,1,0:T(8,128)(2,1)S(1)}, u32[]{:S(2)}, u32[]{:S(2)}) async-start(bf16[8,2,40,2048]{3,2,1,0:T(8,128)(2,1)} %copy-done.1), calls=%async_computation.3 | async-start | bytes 5242880 | tf_op jit(solution)/shard_map/all_to_all | solution.py:591
  187.2 14.4 %shard_map.250.refs_0_ = bf16[8,1,40,2048]{3,2,1,0:T(8,128)(2,1)} custom-call(bf16[8,2,40,2048]{3,2,1,0:T(8,128)(2,1)} %copy-done.1, bf16[8,1,40,2048]{3,2,1,0:T(8,128)(2,1)} %copy-done.28, bf16[320,320]{1,0:T(8,128)(2,1)} %constant.134.clone.refs_2_.refs_3_, bf16[320,320]{1,0:T(8,128)(2,1)} %constant.135.clone.refs_3_.refs_4_, ...), custom_call_target="tpu_custom_call" | custom-call | flops 4865392640 | bytes 27787264 | tf_op jit(solution)/shard_map/pallas_call | solution.py:480
  201.6 17.4 %all-to-all-done.3.refs_2_ = bf16[8,2,40,2048]{3,2,1,0:T(8,128)(2,1)S(1)} async-done(((bf16[8,2,40,2048]{3,2,1,0:T(8,128)(2,1)}), bf16[8,2,40,2048]{3,2,1,0:T(8,128)(2,1)S(1)}, u32[]{:S(2)}, u32[]{:S(2)}) %all-to-all-start.3) | async-done | bytes 2621472 | tf_op jit(solution)/shard_map/all_to_all | solution.py:591
  227.2 13.7 %shard_map.251.refs_0_ = bf16[8,1,40,2048]{3,2,1,0:T(8,128)(2,1)} custom-call(bf16[8,1,40,2048]{3,2,1,0:T(8,128)(2,1)} %shard_map.250.refs_0_, bf16[128,2048]{1,0:T(8,128)(2,1)} %copy-done.30, bf16[8,2,40,2048]{3,2,1,0:T(8,128)(2,1)} %copy-done.27, bf16[320,320]{1,0:T(8,128)(2,1)} %constant.134.clone.refs_2_.refs_3_, ...), custom_call_target="tpu_custom_call" | custom-call | flops 4865392640 | bytes 27787264 | tf_op jit(solution)/shard_map/pallas_call | solution.py:480
  241.8 4.1 %all-to-all-start.7 = ((bf16[8,1,40,2048]{3,2,1,0:T(8,128)(2,1)}), bf16[8,1,40,2048]{3,2,1,0:T(8,128)(2,1)S(1)}, u32[]{:S(2)}, u32[]{:S(2)}) async-start(bf16[8,1,40,2048]{3,2,1,0:T(8,128)(2,1)} %shard_map.252.refs_1_), calls=%async_computation.7 | async-start | bytes 2621440 | tf_op jit(solution)/shard_map/all_to_all | solution.py:591
  250.6 14.4 %shard_map.254.refs_0_ = bf16[8,1,40,2048]{3,2,1,0:T(8,128)(2,1)} custom-call(bf16[128,2048]{1,0:T(8,128)(2,1)} %copy-done.29, bf16[8,1,40,2048]{3,2,1,0:T(8,128)(2,1)} %copy-done.3, bf16[320,320]{1,0:T(8,128)(2,1)} %constant.134.clone.refs_2_.refs_3_, bf16[320,320]{1,0:T(8,128)(2,1)} %constant.135.clone.refs_3_.refs_4_, bf16[4,2048,512]{2,1,0:T(8,128)(2,1)} %refs_4_.8, ...), custom_call_target="tpu_custom_call" | custom-call | flops 4865392640 | bytes 27787264 | tf_op jit(solution)/shard_map/pallas_call | solution.py:480
  266.2 3.8 %all-to-all-start.6 = ((bf16[8,1,40,2048]{3,2,1,0:T(8,128)(2,1)}), bf16[8,1,40,2048]{3,2,1,0:T(8,128)(2,1)S(1)}, u32[]{:S(2)}, u32[]{:S(2)}) async-start(bf16[8,1,40,2048]{3,2,1,0:T(8,128)(2,1)} %shard_map.255.refs_1_), calls=%async_computation.6 | async-start | bytes 2621440 | tf_op jit(solution)/shard_map/all_to_all | solution.py:591
  273.2 10.7 %collective-permute-start.14 = (bf16[128,2048]{1,0:T(8,128)(2,1)S(1)}, bf16[128,2048]{1,0:T(8,128)(2,1)S(1)}, u32[]{:S(2)}, u32[]{:S(2)}) collective-permute-start(bf16[128,2048]{1,0:T(8,128)(2,1)S(1)} %fusion.4), channel_id=1, source_target_pairs={{0,4},{2,6},{4,0},{6,2},{1,5},{3,7},{5,1},{7,3},{8,12},{10,14},{12... | collective-permute-start | bytes 1572872 | tf_op jit(solution)/shard_map/ppermute | solution.py:608
  284.0 3.8 %all-to-all-done.6 = bf16[8,1,40,2048]{3,2,1,0:T(8,128)(2,1)S(1)} async-done(((bf16[8,1,40,2048]{3,2,1,0:T(8,128)(2,1)}), bf16[8,1,40,2048]{3,2,1,0:T(8,128)(2,1)S(1)}, u32[]{:S(2)}, u32[]{:S(2)}) %all-to-all-start.6) | async-done | bytes 1310752 | tf_op jit(solution)/shard_map/all_to_all | solution.py:591
  288.8 19.0 %collective-permute-done.14 = bf16[128,2048]{1,0:T(8,128)(2,1)S(1)} collective-permute-done((bf16[128,2048]{1,0:T(8,128)(2,1)S(1)}, bf16[128,2048]{1,0:T(8,128)(2,1)S(1)}, u32[]{:S(2)}, u32[]{:S(2)}) %collective-permute-start.14) | collective-permute-done | bytes 524320 | tf_op jit(solution)/shard_map/ppermute | solution.py:608
  (185 shorter events, 78.0 us)
Async XLA Ops:
  2.7 18.2 %collective-permute-start = (bf16[256,1024]{1,0:T(8,128)(2,1)}, bf16[256,1024]{1,0:T(8,128)(2,1)S(1)}, u32[]{:S(2)}, u32[]{:S(2)}) collective-permute-start(bf16[256,1024]{1,0:T(8,128)(2,1)} %constant_dynamic-slice_fusion), channel_id=1, source_target_pairs={{0,1},{1,0},{2,3},{3,2},{4,5},{5,4},{6,7},{7,6},{8,9},{9,8},{10,11... | collective-permute-start | bytes 1572872 | tf_op jit(solution)/shard_map/ppermute | solution.py:545
  8.8 29.2 %collective-permute-start.3 = (f32[2,16,128]{2,1,0:T(8,128)S(1)}, f32[2,16,128]{2,1,0:T(8,128)S(1)}, u32[]{:S(2)}, u32[]{:S(2)}) collective-permute-start(f32[2,16,128]{2,1,0:T(8,128)S(1)} %get-tuple-element.24), channel_id=1, source_target_pairs={{0,2},{2,0},{4,6},{6,4},{1,3},{3,1},{5,7},{7,5},{8,10},{10,8},{12,... | collective-permute-start | bytes 49160 | tf_op jit(solution)/shard_map/ppermute | solution.py:574
  10.5 27.6 %collective-permute-start.4 = (f32[2,16,128]{2,1,0:T(8,128)S(1)}, f32[2,16,128]{2,1,0:T(8,128)S(1)}, u32[]{:S(2)}, u32[]{:S(2)}) collective-permute-start(f32[2,16,128]{2,1,0:T(8,128)S(1)} %get-tuple-element.23), channel_id=1, source_target_pairs={{0,4},{2,6},{4,0},{6,2},{1,5},{3,7},{5,1},{7,3},{8,12},{10,14},{12... | collective-permute-start | bytes 49160 | tf_op jit(solution)/shard_map/ppermute | solution.py:574
  13.1 25.0 %collective-permute-start.5 = (f32[2,16,128]{2,1,0:T(8,128)S(1)}, f32[2,16,128]{2,1,0:T(8,128)S(1)}, u32[]{:S(2)}, u32[]{:S(2)}) collective-permute-start(f32[2,16,128]{2,1,0:T(8,128)S(1)} %get-tuple-element.22), channel_id=1, source_target_pairs={{0,6},{2,4},{4,2},{6,0},{1,7},{3,5},{5,3},{7,1},{8,14},{10,12},{12... | collective-permute-start | bytes 49160 | tf_op jit(solution)/shard_map/ppermute | solution.py:574
  21.8 9.2 %collective-permute-start.2 = (bf16[256,1024]{1,0:T(8,128)(2,1)}, bf16[256,1024]{1,0:T(8,128)(2,1)S(1)}, u32[]{:S(2)}, u32[]{:S(2)}) collective-permute-start(bf16[256,1024]{1,0:T(8,128)(2,1)} %shard_map.241.first_ref), channel_id=1, source_target_pairs={{0,8},{8,0},{16,24},{24,16},{1,9},{9,1},{17,25},{25,17},{2,10},{10... | collective-permute-start | bytes 1572872 | tf_op jit(solution)/shard_map/ppermute | solution.py:550
  22.0 9.0 %collective-permute-start.1 = (bf16[512,256]{1,0:T(8,128)(2,1)}, bf16[512,256]{1,0:T(8,128)(2,1)S(1)}, u32[]{:S(2)}, u32[]{:S(2)}) collective-permute-start(bf16[512,256]{1,0:T(8,128)(2,1)} %shard_map.240), channel_id=1, source_target_pairs={{0,1},{1,0},{2,3},{3,2},{4,5},{5,4},{6,7},{7,6},{8,9},{9,8},{10,11... | collective-permute-start | bytes 786440 | tf_op jit(solution)/shard_map/ppermute | solution.py:548
  39.3 53.1 %all-to-all-start = ((bf16[4,128,2048]{2,1,0:T(8,128)(2,1)}), bf16[4,128,2048]{2,1,0:T(8,128)(2,1)S(1)}, u32[]{:S(2)}, u32[]{:S(2)}) async-start(bf16[4,128,2048]{2,1,0:T(8,128)(2,1)} %shard_map.243.refs_1_), calls=%async_computation | async-start | bytes 4194304 | tf_op jit(solution)/shard_map/all_to_all | solution.py:584
  50.3 8.6 %collective-permute-start.8 = (bf16[256,512]{1,0:T(8,128)(2,1)S(1)}, bf16[256,512]{1,0:T(8,128)(2,1)S(1)}, u32[]{:S(2)}, u32[]{:S(2)}) collective-permute-start(bf16[256,512]{1,0:T(8,128)(2,1)S(1)} %get-tuple-element.17), channel_id=1, source_target_pairs={{0,24},{8,16},{16,8},{24,0},{1,25},{9,17},{17,9},{25,1},{2,26},{10... | collective-permute-start | bytes 786440 | tf_op jit(solution)/shard_map/ppermute | solution.py:236
  50.9 13.7 %collective-permute-start.7 = (bf16[256,512]{1,0:T(8,128)(2,1)S(1)}, bf16[256,512]{1,0:T(8,128)(2,1)S(1)}, u32[]{:S(2)}, u32[]{:S(2)}) collective-permute-start(bf16[256,512]{1,0:T(8,128)(2,1)S(1)} %get-tuple-element.18), channel_id=1, source_target_pairs={{0,16},{8,24},{16,0},{24,8},{1,17},{9,25},{17,1},{25,9},{2,18},{10... | collective-permute-start | bytes 786440 | tf_op jit(solution)/shard_map/ppermute | solution.py:236
  51.9 12.6 %collective-permute-start.6 = (bf16[256,512]{1,0:T(8,128)(2,1)S(1)}, bf16[256,512]{1,0:T(8,128)(2,1)S(1)}, u32[]{:S(2)}, u32[]{:S(2)}) collective-permute-start(bf16[256,512]{1,0:T(8,128)(2,1)S(1)} %get-tuple-element.19), channel_id=1, source_target_pairs={{0,8},{8,0},{16,24},{24,16},{1,9},{9,1},{17,25},{25,17},{2,10},{10... | collective-permute-start | bytes 786440 | tf_op jit(solution)/shard_map/ppermute | solution.py:236
  68.4 28.9 %copy-start.8 = (bf16[64,16,2,256]{3,1,2,0:T(8,128)(2,1)}, bf16[64,16,2,256]{3,1,2,0:T(8,128)(2,1)S(1)}, u32[]{:S(2)}) copy-start(bf16[64,16,2,256]{3,1,2,0:T(8,128)(2,1)S(1)} %copy.47) | copy-start | bytes 3145732
  97.3 21.2 %all-to-all-start.1 = ((bf16[8,1,40,2048]{3,2,1,0:T(8,128)(2,1)}), bf16[8,1,40,2048]{3,2,1,0:T(8,128)(2,1)S(1)}, u32[]{:S(2)}, u32[]{:S(2)}) async-start(bf16[8,1,40,2048]{3,2,1,0:T(8,128)(2,1)} %copy-done.12), calls=%async_computation.1 | async-start | bytes 2621440 | tf_op jit(solution)/shard_map/all_to_all | solution.py:591
  100.9 14.5 %collective-permute-start.9 = (bf16[128,2048]{1,0:T(8,128)(2,1)}, bf16[128,2048]{1,0:T(8,128)(2,1)S(1)}, u32[]{:S(2)}, u32[]{:S(2)}) collective-permute-start(bf16[128,2048]{1,0:T(8,128)(2,1)} %copy-done.21), channel_id=1, source_target_pairs={{0,2},{2,0},{4,6},{6,4},{1,3},{3,1},{5,7},{7,5},{8,10},{10,8},{12,... | collective-permute-start | bytes 1572872 | tf_op jit(solution)/shard_map/ppermute | solution.py:608
  120.1 21.2 %all-to-all-start.2 = ((bf16[8,1,40,2048]{3,2,1,0:T(8,128)(2,1)}), bf16[8,1,40,2048]{3,2,1,0:T(8,128)(2,1)S(1)}, u32[]{:S(2)}, u32[]{:S(2)}) async-start(bf16[8,1,40,2048]{3,2,1,0:T(8,128)(2,1)} %copy-done.5), calls=%async_computation.2 | async-start | bytes 2621440 | tf_op jit(solution)/shard_map/all_to_all | solution.py:591
  123.7 16.4 %collective-permute-start.10 = (bf16[128,2048]{1,0:T(8,128)(2,1)}, bf16[128,2048]{1,0:T(8,128)(2,1)S(1)}, u32[]{:S(2)}, u32[]{:S(2)}) collective-permute-start(bf16[128,2048]{1,0:T(8,128)(2,1)} %copy-done.21), channel_id=1, source_target_pairs={{0,6},{2,4},{4,2},{6,0},{1,7},{3,5},{5,3},{7,1},{8,14},{10,12},{12... | collective-permute-start | bytes 1572872 | tf_op jit(solution)/shard_map/ppermute | solution.py:608
  143.0 39.2 %all-to-all-start.4 = ((bf16[8,1,40,2048]{3,2,1,0:T(8,128)(2,1)}), bf16[8,1,40,2048]{3,2,1,0:T(8,128)(2,1)S(1)}, u32[]{:S(2)}, u32[]{:S(2)}) async-start(bf16[8,1,40,2048]{3,2,1,0:T(8,128)(2,1)} %shard_map.247.refs_0_), calls=%async_computation.4 | async-start | bytes 2621440 | tf_op jit(solution)/shard_map/all_to_all | solution.py:591
  146.9 31.6 %collective-permute-start.11 = (bf16[128,2048]{1,0:T(8,128)(2,1)S(1)}, bf16[128,2048]{1,0:T(8,128)(2,1)S(1)}, u32[]{:S(2)}, u32[]{:S(2)}) collective-permute-start(bf16[128,2048]{1,0:T(8,128)(2,1)S(1)} %copy-done.22), channel_id=1, source_target_pairs={{0,4},{2,6},{4,0},{6,2},{1,5},{3,7},{5,1},{7,3},{8,12},{10,14},{12... | collective-permute-start | bytes 1572872 | tf_op jit(solution)/shard_map/ppermute | solution.py:608
  183.3 35.6 %all-to-all-start.3 = ((bf16[8,2,40,2048]{3,2,1,0:T(8,128)(2,1)}), bf16[8,2,40,2048]{3,2,1,0:T(8,128)(2,1)S(1)}, u32[]{:S(2)}, u32[]{:S(2)}) async-start(bf16[8,2,40,2048]{3,2,1,0:T(8,128)(2,1)} %copy-done.1), calls=%async_computation.3 | async-start | bytes 5242880 | tf_op jit(solution)/shard_map/all_to_all | solution.py:591
  220.4 21.3 %all-to-all-start.5 = ((bf16[8,1,40,2048]{3,2,1,0:T(8,128)(2,1)}), bf16[8,1,40,2048]{3,2,1,0:T(8,128)(2,1)S(1)}, u32[]{:S(2)}, u32[]{:S(2)}) async-start(bf16[8,1,40,2048]{3,2,1,0:T(8,128)(2,1)} %shard_map.250.refs_0_), calls=%async_computation.5 | async-start | bytes 2621440 | tf_op jit(solution)/shard_map/all_to_all | solution.py:591
  226.4 14.5 %collective-permute-start.12 = (bf16[128,2048]{1,0:T(8,128)(2,1)S(1)}, bf16[128,2048]{1,0:T(8,128)(2,1)S(1)}, u32[]{:S(2)}, u32[]{:S(2)}) collective-permute-start(bf16[128,2048]{1,0:T(8,128)(2,1)S(1)} %fusion.2.refs_1_), channel_id=1, source_target_pairs={{0,2},{2,0},{4,6},{6,4},{1,3},{3,1},{5,7},{7,5},{8,10},{10,8},{12,... | collective-permute-start | bytes 1572872 | tf_op jit(solution)/shard_map/ppermute | solution.py:608
  241.8 24.4 %all-to-all-start.7 = ((bf16[8,1,40,2048]{3,2,1,0:T(8,128)(2,1)}), bf16[8,1,40,2048]{3,2,1,0:T(8,128)(2,1)S(1)}, u32[]{:S(2)}, u32[]{:S(2)}) async-start(bf16[8,1,40,2048]{3,2,1,0:T(8,128)(2,1)} %shard_map.252.refs_1_), calls=%async_computation.7 | async-start | bytes 2621440 | tf_op jit(solution)/shard_map/all_to_all | solution.py:591
  249.1 16.3 %collective-permute-start.13 = (bf16[128,2048]{1,0:T(8,128)(2,1)S(1)}, bf16[128,2048]{1,0:T(8,128)(2,1)S(1)}, u32[]{:S(2)}, u32[]{:S(2)}) collective-permute-start(bf16[128,2048]{1,0:T(8,128)(2,1)S(1)} %fusion.3.refs_0_), channel_id=1, source_target_pairs={{0,6},{2,4},{4,2},{6,0},{1,7},{3,5},{5,3},{7,1},{8,14},{10,12},{12... | collective-permute-start | bytes 1572872 | tf_op jit(solution)/shard_map/ppermute | solution.py:608
  266.2 21.6 %all-to-all-start.6 = ((bf16[8,1,40,2048]{3,2,1,0:T(8,128)(2,1)}), bf16[8,1,40,2048]{3,2,1,0:T(8,128)(2,1)S(1)}, u32[]{:S(2)}, u32[]{:S(2)}) async-start(bf16[8,1,40,2048]{3,2,1,0:T(8,128)(2,1)} %shard_map.255.refs_1_), calls=%async_computation.6 | async-start | bytes 2621440 | tf_op jit(solution)/shard_map/all_to_all | solution.py:591
  273.2 34.5 %collective-permute-start.14 = (bf16[128,2048]{1,0:T(8,128)(2,1)S(1)}, bf16[128,2048]{1,0:T(8,128)(2,1)S(1)}, u32[]{:S(2)}, u32[]{:S(2)}) collective-permute-start(bf16[128,2048]{1,0:T(8,128)(2,1)S(1)} %fusion.4), channel_id=1, source_target_pairs={{0,4},{2,6},{4,0},{6,2},{1,5},{3,7},{5,1},{7,3},{8,12},{10,14},{12... | collective-permute-start | bytes 1572872 | tf_op jit(solution)/shard_map/ppermute | solution.py:608
  (46 other events, 269.3 us)

commit v9 on v8

--- a/solution.py
+++ b/solution.py
@@ -380,7 +380,7 @@
         in_specs=[pl.BlockSpec(memory_space=pl.ANY)] * len(after) + [whole(a) for a in operands],
         out_specs=[whole(a) for a in shapes],
         out_shape=shapes,
-        compiler_params=pltpu.CompilerParams(vmem_limit_bytes=40 * 1024 * 1024),
+        compiler_params=pltpu.CompilerParams(vmem_limit_bytes=56 * 1024 * 1024),
         cost_estimate=pl.CostEstimate(
             flops=2 * height * tok_rows * D + 10 * tok_rows * D,
             bytes_accessed=(16 * tok_rows + 2 * height) * D,
@@ -410,7 +410,7 @@
         out_specs=pl.BlockSpec((sources, 1, height // sources, D), lambda i: (0, parts - 1, 0, 0)),
         out_shape=jax.ShapeDtypeStruct((sources, parts, height // sources, D), jnp.bfloat16),
         input_output_aliases={0: 0} if into else {},
-        compiler_params=pltpu.CompilerParams(vmem_limit_bytes=40 * 1024 * 1024),
+        compiler_params=pltpu.CompilerParams(vmem_limit_bytes=56 * 1024 * 1024),
         cost_estimate=pl.CostEstimate(
             flops=2 * height * tok_rows * D, bytes_accessed=4 * height * D, transcendentals=0
         ),

time: 310 us -> 314 us (1.013)
  Pallas kernels: 69.1 us -> 77.3 us
  local copies, waits for them, and re-layouts: 29.5 us -> 24.6 us
    pallas_call x3, Pallas kernels: 2.56 us -> 8.05 us  [pack_after(): pl.pallas_call(pack_kernel, grid=(1,), in_specs=[pl.BlockSpec(memory_spac...]
    unnamed x94 -> x80, local copies, waits for them, and re-layouts: 20.5 us -> 15.7 us
  transfers between devices with their start and end apart: 23 -> 23, of which waited for: 13 -> 13; matrix products, arithmetic and copies ran while one was open for 8% -> 8% of each run, Pallas kernels for 21% -> 22%
where the time goes in v9:
time: 314 us; the launch traced here: 313 us
  waiting for transfers between devices  126 us (40%)
  Pallas kernels  77.3 us (25%)
  starting transfers between devices  63.4 us (20%)
  local copies, waits for them, and re-layouts  24.6 us (8%)
  matrix products  11.8 us (4%)
  other arithmetic  8.93 us (3%)
    pallas_call x4, Pallas kernels, run_experts(): pl.pallas_call(expert_kernel, grid=(4,), in_specs=[pl.BlockSpec(memory_sp...  56.9 us
    ppermute x6, waiting for transfers between devices, to_plane(): return lax.ppermute(block, 'z', pairs[turn])  56.8 us
    all_to_all x7, waiting for transfers between devices, exchange(): lax.all_to_all(block, ('req', 'x'), split_axis=0, concat_axis=0, tiled=True)  26.9 us
    all_to_all x7, starting transfers between devices, exchange(): lax.all_to_all(block, ('req', 'x'), split_axis=0, concat_axis=0, tiled=True)  26.4 us
    all_to_all x1, waiting for transfers between devices, on_device_whole(): lax.all_to_all(partial, 'z', split_axis=0, concat_axis=0, tiled=True)  23.4 us
    ppermute x6, starting transfers between devices, to_plane(): return lax.ppermute(block, 'z', pairs[turn])  22.3 us
    unnamed x80, local copies, waits for them, and re-layouts  15.7 us
    ppermute x3, waiting for transfers between devices, move_pages(): incoming.append(lax.ppermute(sent[apart], 'req', pairs))  10.1 us
  transfers between devices with their start and end apart: 23, of which 13 were waited for; matrix products, arithmetic and copies ran while one was open for 8% of the time, Pallas kernels for 22%

profile of v9, /device:TPU:0, one launch (start us, length us, event | category | flops | bytes accessed | tf_op | source)
XLA Modules:
  0.0 313.0 jit_solution(5041275549151660969)
XLA Ops:
  15.0 5.0 %shard_map.239.refs_1_.mine_ref = bf16[2,512,256]{2,1,0:T(8,128)(2,1)S(1)} custom-call(bf16[1024,256]{1,0:T(8,128)(2,1)S(1)} %copy-done.7, bf16[1024,256]{1,0:T(8,128)(2,1)S(1)} %copy-done.8, bf16[1024,256]{1,0:T(8,128)(2,1)S(1)} %copy-done.9, s32[1024,1]{1,0:T(8,128)S(1)} %copy.43.line_ref, s32[1,1024]{1,0:T(1,128)S(1)} %copy-done.6), custom_call_target="tpu_custom_call" | custom-call | flops 1073741824 | bytes 2097152 | tf_op jit(solution)/shard_map/pallas_call | solution.py:283
  22.5 8.5 %collective-permute-done.1.other_ref = bf16[512,256]{1,0:T(8,128)(2,1)S(1)} collective-permute-done((bf16[512,256]{1,0:T(8,128)(2,1)}, bf16[512,256]{1,0:T(8,128)(2,1)S(1)}, u32[]{:S(2)}, u32[]{:S(2)}) %collective-permute-start.1) | collective-permute-done | bytes 262176 | tf_op jit(solution)/shard_map/ppermute | solution.py:548
  39.3 5.0 %all-to-all-start = ((bf16[4,128,2048]{2,1,0:T(8,128)(2,1)}), bf16[4,128,2048]{2,1,0:T(8,128)(2,1)S(1)}, u32[]{:S(2)}, u32[]{:S(2)}) async-start(bf16[4,128,2048]{2,1,0:T(8,128)(2,1)} %shard_map.243.refs_1_), calls=%async_computation | async-start | bytes 4194304 | tf_op jit(solution)/shard_map/all_to_all | solution.py:584
  54.1 4.4 %collective-permute-done.8 = bf16[256,512]{1,0:T(8,128)(2,1)S(1)} collective-permute-done((bf16[256,512]{1,0:T(8,128)(2,1)S(1)}, bf16[256,512]{1,0:T(8,128)(2,1)S(1)}, u32[]{:S(2)}, u32[]{:S(2)}) %collective-permute-start.8) | collective-permute-done | bytes 262176 | tf_op jit(solution)/shard_map/ppermute | solution.py:236
  58.5 5.7 %collective-permute-done.7 = bf16[256,512]{1,0:T(8,128)(2,1)S(1)} collective-permute-done((bf16[256,512]{1,0:T(8,128)(2,1)S(1)}, bf16[256,512]{1,0:T(8,128)(2,1)S(1)}, u32[]{:S(2)}, u32[]{:S(2)}) %collective-permute-start.7) | collective-permute-done | bytes 262176 | tf_op jit(solution)/shard_map/ppermute | solution.py:236
  69.0 23.4 %all-to-all-done.refs_5_ = bf16[4,128,2048]{2,1,0:T(8,128)(2,1)S(1)} async-done(((bf16[4,128,2048]{2,1,0:T(8,128)(2,1)}), bf16[4,128,2048]{2,1,0:T(8,128)(2,1)S(1)}, u32[]{:S(2)}, u32[]{:S(2)}) %all-to-all-start) | async-done | bytes 2097184 | tf_op jit(solution)/shard_map/all_to_all | solution.py:584
  93.7 3.7 %shard_map.245 = (bf16[128,2048]{1,0:T(8,128)(2,1)}, f32[128,2048]{1,0:T(8,128)}, bf16[8,1,40,2048]{3,2,1,0:T(8,128)(2,1)}) custom-call(bf16[64,2,16,256]{3,2,1,0:T(8,128)(2,1)} %bitcast.66, bf16[320,128]{1,0:T(8,128)(2,1)} %get-tuple-element.15.refs_1_, bf16[320,128]{1,0:T(8,128)(2,1)} %get-tuple-element.11.refs_2_.refs_1_, ...), custom_call_target="tpu_custom_call" | custom-call | flops 170393600 | bytes 5505024 | tf_op jit(solution)/shard_map/pallas_call | solution.py:377
  97.4 3.7 %all-to-all-start.1 = ((bf16[8,1,40,2048]{3,2,1,0:T(8,128)(2,1)}), bf16[8,1,40,2048]{3,2,1,0:T(8,128)(2,1)S(1)}, u32[]{:S(2)}, u32[]{:S(2)}) async-start(bf16[8,1,40,2048]{3,2,1,0:T(8,128)(2,1)} %get-tuple-element.6), calls=%async_computation.1 | async-start | bytes 2621440 | tf_op jit(solution)/shard_map/all_to_all | solution.py:591
  101.2 14.2 %collective-permute-done.9.refs_2_ = bf16[128,2048]{1,0:T(8,128)(2,1)S(1)} collective-permute-done((bf16[128,2048]{1,0:T(8,128)(2,1)S(1)}, bf16[128,2048]{1,0:T(8,128)(2,1)S(1)}, u32[]{:S(2)}, u32[]{:S(2)}) %collective-permute-start.9) | collective-permute-done | bytes 524320 | tf_op jit(solution)/shard_map/ppermute | solution.py:608
  127.7 14.6 %collective-permute-done.10.refs_2_ = bf16[128,2048]{1,0:T(8,128)(2,1)S(1)} collective-permute-done((bf16[128,2048]{1,0:T(8,128)(2,1)S(1)}, bf16[128,2048]{1,0:T(8,128)(2,1)S(1)}, u32[]{:S(2)}, u32[]{:S(2)}) %collective-permute-start.10) | collective-permute-done | bytes 524320 | tf_op jit(solution)/shard_map/ppermute | solution.py:608
  147.6 3.7 %all-to-all-start.4 = ((bf16[8,1,40,2048]{3,2,1,0:T(8,128)(2,1)}), bf16[8,1,40,2048]{3,2,1,0:T(8,128)(2,1)S(1)}, u32[]{:S(2)}, u32[]{:S(2)}) async-start(bf16[8,1,40,2048]{3,2,1,0:T(8,128)(2,1)} %shard_map.247.refs_0_), calls=%async_computation.4 | async-start | bytes 2621440 | tf_op jit(solution)/shard_map/all_to_all | solution.py:591
  151.3 8.4 %collective-permute-start.11 = (bf16[128,2048]{1,0:T(8,128)(2,1)S(1)}, bf16[128,2048]{1,0:T(8,128)(2,1)S(1)}, u32[]{:S(2)}, u32[]{:S(2)}) collective-permute-start(bf16[128,2048]{1,0:T(8,128)(2,1)S(1)} %copy-done.38), channel_id=1, source_target_pairs={{0,4},{2,6},{4,0},{6,2},{1,5},{3,7},{5,1},{7,3},{8,12},{10,14},{12... | collective-permute-start | bytes 1572872 | tf_op jit(solution)/shard_map/ppermute | solution.py:608
  159.7 14.4 %shard_map.248.refs_0_ = bf16[8,2,40,2048]{3,2,1,0:T(8,128)(2,1)} custom-call(bf16[8,1,40,2048]{3,2,1,0:T(8,128)(2,1)} %shard_map.247.refs_0_, bf16[8,1,40,2048]{3,2,1,0:T(8,128)(2,1)} %copy-done.16, bf16[320,320]{1,0:T(8,128)(2,1)} %constant.134.clone.refs_2_.refs_3_, bf16[320,320]{1,0:T(8,128)(2,1)} %constant.135.clone.refs_3_.refs_4_, ...), custom_call_target="tpu_custom_call" | custom-call | flops 4865392640 | bytes 27787264 | tf_op jit(solution)/shard_map/pallas_call | solution.py:480
  174.1 9.4 %collective-permute-done.11.refs_2_ = bf16[128,2048]{1,0:T(8,128)(2,1)S(1)} collective-permute-done((bf16[128,2048]{1,0:T(8,128)(2,1)S(1)}, bf16[128,2048]{1,0:T(8,128)(2,1)S(1)}, u32[]{:S(2)}, u32[]{:S(2)}) %collective-permute-start.11) | collective-permute-done | bytes 524320 | tf_op jit(solution)/shard_map/ppermute | solution.py:608
  188.1 3.8 %all-to-all-start.3 = ((bf16[8,2,40,2048]{3,2,1,0:T(8,128)(2,1)}), bf16[8,2,40,2048]{3,2,1,0:T(8,128)(2,1)S(1)}, u32[]{:S(2)}, u32[]{:S(2)}) async-start(bf16[8,2,40,2048]{3,2,1,0:T(8,128)(2,1)} %shard_map.249.refs_0_), calls=%async_computation.3 | async-start | bytes 5242880 | tf_op jit(solution)/shard_map/all_to_all | solution.py:591
  192.0 14.4 %shard_map.250.refs_0_ = bf16[8,1,40,2048]{3,2,1,0:T(8,128)(2,1)} custom-call(bf16[8,2,40,2048]{3,2,1,0:T(8,128)(2,1)} %shard_map.249.refs_0_, bf16[8,1,40,2048]{3,2,1,0:T(8,128)(2,1)} %copy-done.18, bf16[320,320]{1,0:T(8,128)(2,1)} %constant.134.clone.refs_2_.refs_3_, bf16[320,320]{1,0:T(8,128)(2,1)} %constant.135.clone.refs_3_.refs_4_, ...), custom_call_target="tpu_custom_call" | custom-call | flops 4865392640 | bytes 27787264 | tf_op jit(solution)/shard_map/pallas_call | solution.py:480
  206.4 17.4 %all-to-all-done.3.refs_2_ = bf16[8,2,40,2048]{3,2,1,0:T(8,128)(2,1)S(1)} async-done(((bf16[8,2,40,2048]{3,2,1,0:T(8,128)(2,1)}), bf16[8,2,40,2048]{3,2,1,0:T(8,128)(2,1)S(1)}, u32[]{:S(2)}, u32[]{:S(2)}) %all-to-all-start.3) | async-done | bytes 2621472 | tf_op jit(solution)/shard_map/all_to_all | solution.py:591
  232.0 13.7 %shard_map.251.refs_0_ = bf16[8,1,40,2048]{3,2,1,0:T(8,128)(2,1)} custom-call(bf16[8,1,40,2048]{3,2,1,0:T(8,128)(2,1)} %shard_map.250.refs_0_, bf16[128,2048]{1,0:T(8,128)(2,1)} %copy-done.20, bf16[8,2,40,2048]{3,2,1,0:T(8,128)(2,1)} %copy-done.14, bf16[320,320]{1,0:T(8,128)(2,1)} %constant.134.clone.refs_2_.refs_3_, ...), custom_call_target="tpu_custom_call" | custom-call | flops 4865392640 | bytes 27787264 | tf_op jit(solution)/shard_map/pallas_call | solution.py:480
  246.6 4.1 %all-to-all-start.7 = ((bf16[8,1,40,2048]{3,2,1,0:T(8,128)(2,1)}), bf16[8,1,40,2048]{3,2,1,0:T(8,128)(2,1)S(1)}, u32[]{:S(2)}, u32[]{:S(2)}) async-start(bf16[8,1,40,2048]{3,2,1,0:T(8,128)(2,1)} %shard_map.252.refs_1_), calls=%async_computation.7 | async-start | bytes 2621440 | tf_op jit(solution)/shard_map/all_to_all | solution.py:591
  255.4 14.4 %shard_map.254.refs_0_ = bf16[8,1,40,2048]{3,2,1,0:T(8,128)(2,1)} custom-call(bf16[128,2048]{1,0:T(8,128)(2,1)} %copy-done.19, bf16[8,1,40,2048]{3,2,1,0:T(8,128)(2,1)} %copy-done.15, bf16[320,320]{1,0:T(8,128)(2,1)} %constant.134.clone.refs_2_.refs_3_, bf16[320,320]{1,0:T(8,128)(2,1)} %constant.135.clone.refs_3_.refs_4_, bf16[4,2048,512]{2,1,0:T(8,128)(2,1)} %refs_4_.8, ...), custom_call_target="tpu_custom_call" | custom-call | flops 4865392640 | bytes 27787264 | tf_op jit(solution)/shard_map/pallas_call | solution.py:480
  271.0 3.8 %all-to-all-start.6 = ((bf16[8,1,40,2048]{3,2,1,0:T(8,128)(2,1)}), bf16[8,1,40,2048]{3,2,1,0:T(8,128)(2,1)S(1)}, u32[]{:S(2)}, u32[]{:S(2)}) async-start(bf16[8,1,40,2048]{3,2,1,0:T(8,128)(2,1)} %shard_map.255.refs_1_), calls=%async_computation.6 | async-start | bytes 2621440 | tf_op jit(solution)/shard_map/all_to_all | solution.py:591
  277.3 10.7 %collective-permute-start.14 = (bf16[128,2048]{1,0:T(8,128)(2,1)S(1)}, bf16[128,2048]{1,0:T(8,128)(2,1)S(1)}, u32[]{:S(2)}, u32[]{:S(2)}) collective-permute-start(bf16[128,2048]{1,0:T(8,128)(2,1)S(1)} %fusion.4), channel_id=1, source_target_pairs={{0,4},{2,6},{4,0},{6,2},{1,5},{3,7},{5,1},{7,3},{8,12},{10,14},{12... | collective-permute-start | bytes 1572872 | tf_op jit(solution)/shard_map/ppermute | solution.py:608
  288.0 4.6 %all-to-all-done.6 = bf16[8,1,40,2048]{3,2,1,0:T(8,128)(2,1)S(1)} async-done(((bf16[8,1,40,2048]{3,2,1,0:T(8,128)(2,1)}), bf16[8,1,40,2048]{3,2,1,0:T(8,128)(2,1)S(1)}, u32[]{:S(2)}, u32[]{:S(2)}) %all-to-all-start.6) | async-done | bytes 1310752 | tf_op jit(solution)/shard_map/all_to_all | solution.py:591
  293.6 18.2 %collective-permute-done.14 = bf16[128,2048]{1,0:T(8,128)(2,1)S(1)} collective-permute-done((bf16[128,2048]{1,0:T(8,128)(2,1)S(1)}, bf16[128,2048]{1,0:T(8,128)(2,1)S(1)}, u32[]{:S(2)}, u32[]{:S(2)}) %collective-permute-start.14) | collective-permute-done | bytes 524320 | tf_op jit(solution)/shard_map/ppermute | solution.py:608
  (171 shorter events, 82.4 us)
Async XLA Ops:
  2.7 18.3 %collective-permute-start = (bf16[256,1024]{1,0:T(8,128)(2,1)}, bf16[256,1024]{1,0:T(8,128)(2,1)S(1)}, u32[]{:S(2)}, u32[]{:S(2)}) collective-permute-start(bf16[256,1024]{1,0:T(8,128)(2,1)} %constant_dynamic-slice_fusion), channel_id=1, source_target_pairs={{0,1},{1,0},{2,3},{3,2},{4,5},{5,4},{6,7},{7,6},{8,9},{9,8},{10,11... | collective-permute-start | bytes 1572872 | tf_op jit(solution)/shard_map/ppermute | solution.py:545
  8.8 29.2 %collective-permute-start.3 = (f32[2,16,128]{2,1,0:T(8,128)S(1)}, f32[2,16,128]{2,1,0:T(8,128)S(1)}, u32[]{:S(2)}, u32[]{:S(2)}) collective-permute-start(f32[2,16,128]{2,1,0:T(8,128)S(1)} %get-tuple-element.24), channel_id=1, source_target_pairs={{0,2},{2,0},{4,6},{6,4},{1,3},{3,1},{5,7},{7,5},{8,10},{10,8},{12,... | collective-permute-start | bytes 49160 | tf_op jit(solution)/shard_map/ppermute | solution.py:574
  10.5 27.6 %collective-permute-start.4 = (f32[2,16,128]{2,1,0:T(8,128)S(1)}, f32[2,16,128]{2,1,0:T(8,128)S(1)}, u32[]{:S(2)}, u32[]{:S(2)}) collective-permute-start(f32[2,16,128]{2,1,0:T(8,128)S(1)} %get-tuple-element.23), channel_id=1, source_target_pairs={{0,4},{2,6},{4,0},{6,2},{1,5},{3,7},{5,1},{7,3},{8,12},{10,14},{12... | collective-permute-start | bytes 49160 | tf_op jit(solution)/shard_map/ppermute | solution.py:574
  13.1 25.0 %collective-permute-start.5 = (f32[2,16,128]{2,1,0:T(8,128)S(1)}, f32[2,16,128]{2,1,0:T(8,128)S(1)}, u32[]{:S(2)}, u32[]{:S(2)}) collective-permute-start(f32[2,16,128]{2,1,0:T(8,128)S(1)} %get-tuple-element.22), channel_id=1, source_target_pairs={{0,6},{2,4},{4,2},{6,0},{1,7},{3,5},{5,3},{7,1},{8,14},{10,12},{12... | collective-permute-start | bytes 49160 | tf_op jit(solution)/shard_map/ppermute | solution.py:574
  21.8 9.2 %collective-permute-start.2 = (bf16[256,1024]{1,0:T(8,128)(2,1)}, bf16[256,1024]{1,0:T(8,128)(2,1)S(1)}, u32[]{:S(2)}, u32[]{:S(2)}) collective-permute-start(bf16[256,1024]{1,0:T(8,128)(2,1)} %shard_map.241.first_ref), channel_id=1, source_target_pairs={{0,8},{8,0},{16,24},{24,16},{1,9},{9,1},{17,25},{25,17},{2,10},{10... | collective-permute-start | bytes 1572872 | tf_op jit(solution)/shard_map/ppermute | solution.py:550
  22.0 9.0 %collective-permute-start.1 = (bf16[512,256]{1,0:T(8,128)(2,1)}, bf16[512,256]{1,0:T(8,128)(2,1)S(1)}, u32[]{:S(2)}, u32[]{:S(2)}) collective-permute-start(bf16[512,256]{1,0:T(8,128)(2,1)} %shard_map.240), channel_id=1, source_target_pairs={{0,1},{1,0},{2,3},{3,2},{4,5},{5,4},{6,7},{7,6},{8,9},{9,8},{10,11... | collective-permute-start | bytes 786440 | tf_op jit(solution)/shard_map/ppermute | solution.py:548
  39.3 53.1 %all-to-all-start = ((bf16[4,128,2048]{2,1,0:T(8,128)(2,1)}), bf16[4,128,2048]{2,1,0:T(8,128)(2,1)S(1)}, u32[]{:S(2)}, u32[]{:S(2)}) async-start(bf16[4,128,2048]{2,1,0:T(8,128)(2,1)} %shard_map.243.refs_1_), calls=%async_computation | async-start | bytes 4194304 | tf_op jit(solution)/shard_map/all_to_all | solution.py:584
  49.9 8.6 %collective-permute-start.8 = (bf16[256,512]{1,0:T(8,128)(2,1)S(1)}, bf16[256,512]{1,0:T(8,128)(2,1)S(1)}, u32[]{:S(2)}, u32[]{:S(2)}) collective-permute-start(bf16[256,512]{1,0:T(8,128)(2,1)S(1)} %get-tuple-element.17), channel_id=1, source_target_pairs={{0,24},{8,16},{16,8},{24,0},{1,25},{9,17},{17,9},{25,1},{2,26},{10... | collective-permute-start | bytes 786440 | tf_op jit(solution)/shard_map/ppermute | solution.py:236
  50.5 13.7 %collective-permute-start.7 = (bf16[256,512]{1,0:T(8,128)(2,1)S(1)}, bf16[256,512]{1,0:T(8,128)(2,1)S(1)}, u32[]{:S(2)}, u32[]{:S(2)}) collective-permute-start(bf16[256,512]{1,0:T(8,128)(2,1)S(1)} %get-tuple-element.18), channel_id=1, source_target_pairs={{0,16},{8,24},{16,0},{24,8},{1,17},{9,25},{17,1},{25,9},{2,18},{10... | collective-permute-start | bytes 786440 | tf_op jit(solution)/shard_map/ppermute | solution.py:236
  51.5 12.6 %collective-permute-start.6 = (bf16[256,512]{1,0:T(8,128)(2,1)S(1)}, bf16[256,512]{1,0:T(8,128)(2,1)S(1)}, u32[]{:S(2)}, u32[]{:S(2)}) collective-permute-start(bf16[256,512]{1,0:T(8,128)(2,1)S(1)} %get-tuple-element.19), channel_id=1, source_target_pairs={{0,8},{8,0},{16,24},{24,16},{1,9},{9,1},{17,25},{25,17},{2,10},{10... | collective-permute-start | bytes 786440 | tf_op jit(solution)/shard_map/ppermute | solution.py:236
  97.4 21.4 %all-to-all-start.1 = ((bf16[8,1,40,2048]{3,2,1,0:T(8,128)(2,1)}), bf16[8,1,40,2048]{3,2,1,0:T(8,128)(2,1)S(1)}, u32[]{:S(2)}, u32[]{:S(2)}) async-start(bf16[8,1,40,2048]{3,2,1,0:T(8,128)(2,1)} %get-tuple-element.6), calls=%async_computation.1 | async-start | bytes 2621440 | tf_op jit(solution)/shard_map/all_to_all | solution.py:591
  101.1 14.2 %collective-permute-start.9 = (bf16[128,2048]{1,0:T(8,128)(2,1)S(1)}, bf16[128,2048]{1,0:T(8,128)(2,1)S(1)}, u32[]{:S(2)}, u32[]{:S(2)}) collective-permute-start(bf16[128,2048]{1,0:T(8,128)(2,1)S(1)} %copy-done.38), channel_id=1, source_target_pairs={{0,2},{2,0},{4,6},{6,4},{1,3},{3,1},{5,7},{7,5},{8,10},{10,8},{12,... | collective-permute-start | bytes 1572872 | tf_op jit(solution)/shard_map/ppermute | solution.py:608
  122.5 21.2 %all-to-all-start.2 = ((bf16[8,1,40,2048]{3,2,1,0:T(8,128)(2,1)}), bf16[8,1,40,2048]{3,2,1,0:T(8,128)(2,1)S(1)}, u32[]{:S(2)}, u32[]{:S(2)}) async-start(bf16[8,1,40,2048]{3,2,1,0:T(8,128)(2,1)} %shard_map.246), calls=%async_computation.2 | async-start | bytes 2621440 | tf_op jit(solution)/shard_map/all_to_all | solution.py:591
  126.1 16.1 %collective-permute-start.10 = (bf16[128,2048]{1,0:T(8,128)(2,1)S(1)}, bf16[128,2048]{1,0:T(8,128)(2,1)S(1)}, u32[]{:S(2)}, u32[]{:S(2)}) collective-permute-start(bf16[128,2048]{1,0:T(8,128)(2,1)S(1)} %copy-done.38), channel_id=1, source_target_pairs={{0,6},{2,4},{4,2},{6,0},{1,7},{3,5},{5,3},{7,1},{8,14},{10,12},{12... | collective-permute-start | bytes 1572872 | tf_op jit(solution)/shard_map/ppermute | solution.py:608
  147.6 39.4 %all-to-all-start.4 = ((bf16[8,1,40,2048]{3,2,1,0:T(8,128)(2,1)}), bf16[8,1,40,2048]{3,2,1,0:T(8,128)(2,1)S(1)}, u32[]{:S(2)}, u32[]{:S(2)}) async-start(bf16[8,1,40,2048]{3,2,1,0:T(8,128)(2,1)} %shard_map.247.refs_0_), calls=%async_computation.4 | async-start | bytes 2621440 | tf_op jit(solution)/shard_map/all_to_all | solution.py:591
  151.3 32.2 %collective-permute-start.11 = (bf16[128,2048]{1,0:T(8,128)(2,1)S(1)}, bf16[128,2048]{1,0:T(8,128)(2,1)S(1)}, u32[]{:S(2)}, u32[]{:S(2)}) collective-permute-start(bf16[128,2048]{1,0:T(8,128)(2,1)S(1)} %copy-done.38), channel_id=1, source_target_pairs={{0,4},{2,6},{4,0},{6,2},{1,5},{3,7},{5,1},{7,3},{8,12},{10,14},{12... | collective-permute-start | bytes 1572872 | tf_op jit(solution)/shard_map/ppermute | solution.py:608
  188.1 35.6 %all-to-all-start.3 = ((bf16[8,2,40,2048]{3,2,1,0:T(8,128)(2,1)}), bf16[8,2,40,2048]{3,2,1,0:T(8,128)(2,1)S(1)}, u32[]{:S(2)}, u32[]{:S(2)}) async-start(bf16[8,2,40,2048]{3,2,1,0:T(8,128)(2,1)} %shard_map.249.refs_0_), calls=%async_computation.3 | async-start | bytes 5242880 | tf_op jit(solution)/shard_map/all_to_all | solution.py:591
  206.4 23.9 %copy-start.25 = (f32[320,128]{1,0:T(8,128)S(1)}, f32[320,128]{1,0:T(8,128)}, u32[]{:S(2)}) copy-start(f32[320,128]{1,0:T(8,128)} %get-tuple-element.14) | copy-start | bytes 491524
  225.2 21.3 %all-to-all-start.5 = ((bf16[8,1,40,2048]{3,2,1,0:T(8,128)(2,1)}), bf16[8,1,40,2048]{3,2,1,0:T(8,128)(2,1)S(1)}, u32[]{:S(2)}, u32[]{:S(2)}) async-start(bf16[8,1,40,2048]{3,2,1,0:T(8,128)(2,1)} %shard_map.250.refs_0_), calls=%async_computation.5 | async-start | bytes 2621440 | tf_op jit(solution)/shard_map/all_to_all | solution.py:591
  231.3 14.5 %collective-permute-start.12 = (bf16[128,2048]{1,0:T(8,128)(2,1)S(1)}, bf16[128,2048]{1,0:T(8,128)(2,1)S(1)}, u32[]{:S(2)}, u32[]{:S(2)}) collective-permute-start(bf16[128,2048]{1,0:T(8,128)(2,1)S(1)} %fusion.2.refs_1_), channel_id=1, source_target_pairs={{0,2},{2,0},{4,6},{6,4},{1,3},{3,1},{5,7},{7,5},{8,10},{10,8},{12,... | collective-permute-start | bytes 1572872 | tf_op jit(solution)/shard_map/ppermute | solution.py:608
  246.6 24.5 %all-to-all-start.7 = ((bf16[8,1,40,2048]{3,2,1,0:T(8,128)(2,1)}), bf16[8,1,40,2048]{3,2,1,0:T(8,128)(2,1)S(1)}, u32[]{:S(2)}, u32[]{:S(2)}) async-start(bf16[8,1,40,2048]{3,2,1,0:T(8,128)(2,1)} %shard_map.252.refs_1_), calls=%async_computation.7 | async-start | bytes 2621440 | tf_op jit(solution)/shard_map/all_to_all | solution.py:591
  253.9 16.3 %collective-permute-start.13 = (bf16[128,2048]{1,0:T(8,128)(2,1)S(1)}, bf16[128,2048]{1,0:T(8,128)(2,1)S(1)}, u32[]{:S(2)}, u32[]{:S(2)}) collective-permute-start(bf16[128,2048]{1,0:T(8,128)(2,1)S(1)} %fusion.3.refs_0_), channel_id=1, source_target_pairs={{0,6},{2,4},{4,2},{6,0},{1,7},{3,5},{5,3},{7,1},{8,14},{10,12},{12... | collective-permute-start | bytes 1572872 | tf_op jit(solution)/shard_map/ppermute | solution.py:608
  271.0 21.6 %all-to-all-start.6 = ((bf16[8,1,40,2048]{3,2,1,0:T(8,128)(2,1)}), bf16[8,1,40,2048]{3,2,1,0:T(8,128)(2,1)S(1)}, u32[]{:S(2)}, u32[]{:S(2)}) async-start(bf16[8,1,40,2048]{3,2,1,0:T(8,128)(2,1)} %shard_map.255.refs_1_), calls=%async_computation.6 | async-start | bytes 2621440 | tf_op jit(solution)/shard_map/all_to_all | solution.py:591
  277.3 34.5 %collective-permute-start.14 = (bf16[128,2048]{1,0:T(8,128)(2,1)S(1)}, bf16[128,2048]{1,0:T(8,128)(2,1)S(1)}, u32[]{:S(2)}, u32[]{:S(2)}) collective-permute-start(bf16[128,2048]{1,0:T(8,128)(2,1)S(1)} %fusion.4), channel_id=1, source_target_pairs={{0,4},{2,6},{4,0},{6,2},{1,5},{3,7},{5,1},{7,3},{8,12},{10,14},{12... | collective-permute-start | bytes 1572872 | tf_op jit(solution)/shard_map/ppermute | solution.py:608
  (39 other events, 197.2 us)
